TPU v7x, 256 devices: a whole 4x4x8 slice. The times are simulated.
256 devices in a mesh: genome: 16 (over x_hi, y, core), people: 16 (over z, x_lo).
Axes of the slice: x: 4 (x_hi: 2, x_lo: 2; x = x_hi * 2 + x_lo), y: 4, z: 8, core: 2. Of those that a mesh axis runs over, the one named last changes fastest.
Arguments:
- genotypes: bfloat16 [49152, 16384], P('people', 'genome'), may hold values from -6 to 6
- expression: bfloat16 [49152, 4096], P('people', 'genome'), may hold values from -6 to 6
- coef_start: float32 [4096, 2048], P('genome'), may hold values from -4 to 4
- penalty: float32 [4096], P('genome'), may hold values from 0.02 to 0.3
- step_size: float32 [4096], P('genome'), may hold values from 0.3 to 0.8
- window_start: int32 [4096], P('genome'), may hold values from 0 to 15872, as said below
- window_end: int32 [4096], P('genome'), may hold values from 512 to 16384, as said below
- active_blocks: int32 [4096, 16], P('genome'), may hold values 0 or 1
Outputs:
- coef: float32 [4096, 2048], P('genome')
- peaks: float32 [4096, 16], P('genome')
Inputs may be any that keep to these rules, and one draw needn't show every extreme that they name: `window_start`: gene g's window lies within variants g // 256 * 1024 - 512 to (g // 256 + 1) * 1024 + 512 clipped to the region, and is not empty. window_end exceeds window_start by 512 or more.
All inputs are finite; a program needn't handle non-finite values. No bound on the sum of `active_blocks` on one device may be relied on, other than what follows from the above.
Results may differ from a plain program's by a relative error of at most 0.0035.
Values may be sent and summed in bfloat16 or wider, within the bound.
No kernel may reach another device: no remote copies, remote signals or barrier semaphores. Data moves between devices by JAX's collectives and lax.ppermute only.
A program may use at most 128 MiB of HBM per device.

v0:
```python
import jax
import jax.numpy as jnp
from jax import lax
from jax.sharding import PartitionSpec as P

l1_share = 0.5


def with_halo(block, sides, width):
    for axis, dim in sides:
        count = lax.axis_size(axis)
        forward = [(i, i + 1) for i in range(count - 1)]
        backward = [(target, source) for source, target in forward]
        low = lax.ppermute(
            lax.slice_in_dim(block, block.shape[dim] - width, None, axis=dim), axis, forward
        )
        high = lax.ppermute(lax.slice_in_dim(block, 0, width, axis=dim), axis, backward)
        block = jnp.concatenate([low, block, high], axis=dim)
    return block


def shrink(coef, grad, penalty, step, mask):
    moved = coef + step[:, None] * grad
    cut = step[:, None] * penalty[:, None]
    kept = jnp.sign(moved) * jnp.maximum(jnp.abs(moved) - cut * l1_share, 0.0)
    return mask * kept / (1.0 + cut * (1.0 - l1_share))


def block_peaks(grad, mask, penalty):
    scaled = mask * jnp.abs(grad) / penalty[:, None]
    return jnp.max(scaled.reshape(grad.shape[0], -1, 128), axis=2)


def on_device(
    genotypes, expression, coef_start, penalty, step_size, window_start, window_end, active_blocks
):
    v_local = genotypes.shape[1]
    total = genotypes.shape[0] * lax.axis_size("people")
    width = coef_start.shape[1]
    reach = (width - v_local) // 2
    wide = with_halo(genotypes, (("genome", 1),), reach)
    column = jnp.arange(width, dtype=jnp.int32)
    place = lax.axis_index("genome") * v_local - reach + column
    inside = (place[None, :] >= window_start[:, None]) & (place[None, :] < window_end[:, None])
    blocks = jnp.repeat(active_blocks, 128, axis=1) > 0
    mask = jnp.where(inside & blocks, 1.0, 0.0).astype(jnp.float32)
    target = expression.astype(jnp.float32)
    coef = mask * coef_start
    peaks = None
    for turn in range(2):
        fitted = jnp.dot(wide, coef.astype(jnp.bfloat16).T, preferred_element_type=jnp.float32)
        resid = (target - fitted).astype(jnp.bfloat16)
        local = jnp.dot(resid.T, wide, preferred_element_type=jnp.float32)
        grad = lax.psum(local, "people") / total
        if turn == 0:
            peaks = block_peaks(grad, mask, penalty)
        coef = shrink(coef, grad, penalty, step_size, mask)
    return (coef, peaks)


def solution(mesh):
    return jax.shard_map(
        on_device,
        mesh=mesh,
        in_specs=(
            P("people", "genome"),
            P("people", "genome"),
            P("genome", None),
            P("genome"),
            P("genome"),
            P("genome"),
            P("genome"),
            P("genome", None),
        ),
        out_specs=(P("genome", None), P("genome", None)),
        check_vma=False,
    )
```

profile of v0, /device:TPU:56, one launch (start us, length us, event | category | flops | bytes accessed | tf_op | source)
XLA Modules:
  0.0 417.8 jit_solution(16232319154396713135)
XLA Ops:
  7.2 0.0 copy-start.2
  7.2 0.0 all-reduce.3.cloned.1.call-start
  7.2 5.9 %fusion.23 = (bf16[3072,512]{1,0:T(8,128)(2,1)}, bf16[3072,512]{1,0:T(8,128)(2,1)}) fusion(bf16[3072,1024]{1,0:T(8,128)(2,1)} %param.8), kind=kLoop, calls=%fused_computation.29 | loop fusion | bytes 12582912 | tf_op jit(solution)/shard_map/slice | solution.py:17
  13.1 1.9 collective-permute-start
  15.0 3.6 collective-permute-start.1
  18.6 0.0 copy-done.2
  18.7 0.1 copy.11
  18.8 0.0 copy-start
  18.8 33.1 %collective-permute-done = bf16[3072,512]{1,0:T(8,128)(2,1)} collective-permute-done((bf16[3072,512]{1,0:T(8,128)(2,1)}, bf16[3072,512]{1,0:T(8,128)(2,1)}, u32[]{:S(2)}, u32[]{:S(2)}) %collective-permute-start) | collective-permute-done | bytes 3145760 | tf_op jit(solution)/shard_map/ppermute | solution.py:14
  52.0 3.8 constant_dynamic-update-slice_fusion.2
  55.8 0.0 copy-done
  55.8 3.3 constant_dynamic-update-slice_fusion.1
  59.2 0.0 copy-start.4
  59.2 0.0 copy-start.5
  59.2 0.0 collective-permute-done.1
  59.2 1.9 constant_dynamic-update-slice_fusion
  61.1 1.3 broadcast_in_dim.10
  62.4 0.0 copy-done.4
  62.4 0.0 copy-done.5
  62.4 23.4 %fusion.2 = f32[256,2048]{1,0:T(8,128)} fusion(bf16[3072,2048]{1,0:T(8,128)(2,1)} %constant_dynamic-update-slice_fusion, bf16[3072,256]{1,0:T(8,128)(2,1)} %param.9, f32[256,2048]{1,0:T(8,128)} %param.10, pred[32,8,16,128]{3,2,1,0:T(8,128)(4,1)S(1)} %bitcast.23, s32[2048]{0:T(1024)S(1)} %iota_add_fusion, s32[256]{0:T(256)S(1)} %copy-done.4, s32[256]{0:T(256)S(1)} %copy-done.5), kind=kOutput, calls=%fused_computation.8 | convolution fusion | flops 6448480256 | bytes 18884608 | tf_op jit(solution)/shard_map/dot_general | solution.py:53
  85.7 0.0 copy-start.3
  85.7 0.0 copy-start.6
  85.7 0.0 copy-start.1
  85.8 0.0 all-reduce.3.cloned.1.call-update
  85.8 0.3 all-reduce.5.cloned.1.call-start
  86.0 0.4 copy-done.3
  86.4 0.0 copy-done.6
  86.4 148.1 %all-reduce.3.cloned.1.call-done = f32[256,2048]{1,0:T(8,128)} async-done(((f32[256,2048]{1,0:T(8,128)}), f32[256,2048]{1,0:T(8,128)}) %all-reduce.3.cloned.1.call-update) | async-done | bytes 2097168 | tf_op jit(solution)/shard_map/psum | solution.py:54
  234.6 0.0 copy-done.1
  234.6 23.7 %fusion.3 = f32[256,2048]{1,0:T(8,128)} fusion(bf16[3072,2048]{1,0:T(8,128)(2,1)} %constant_dynamic-update-slice_fusion, bf16[3072,256]{1,0:T(8,128)(2,1)} %param.9, f32[256,2048]{1,0:T(8,128)} %all-reduce.3.cloned.1.call-done, f32[256,2048]{1,0:T(8,128)S(1)} %copy-done.1, f32[256]{0:T(256)S(1)} %get-tuple-element.4, f32[256]{0:T(256)S(1)} %get-tuple-element.5, ...), kind=kOutput, calls=%fused_computation.9 | convolution fusion | flops 6453198848 | bytes 20984832 | tf_op jit(solution)/shard_map/dot_general | solution.py:53
  258.2 0.0 all-reduce.5.cloned.1.call-update
  258.2 145.2 %all-reduce.5.cloned.1.call-done = f32[256,2048]{1,0:T(8,128)} async-done(((f32[256,2048]{1,0:T(8,128)}), f32[256,2048]{1,0:T(8,128)}) %all-reduce.5.cloned.1.call-update) | async-done | bytes 2097168 | tf_op jit(solution)/shard_map/psum | solution.py:54
  403.5 5.8 %fusion.7 = (f32[32,8,16,128]{3,1,2,0:T(8,128)S(1)}, f32[256,2048]{1,0:T(8,128)}) fusion(f32[256,2048]{1,0:T(8,128)} %all-reduce.3.cloned.1.call-done, f32[256]{0:T(256)S(1)} %copy-done.3, pred[32,8,16,128]{3,2,1,0:T(8,128)(4,1)S(1)} %bitcast.25, s32[256]{0:T(256)S(1)} %copy-done.4, s32[256]{0:T(256)S(1)} %copy-done.5, s32[2048]{0:T(1024)S(1)} %iota_add_fusion, ...), kind=kLoop, calls=%fused_computation.13 | loop fusion | flops 14680064 | bytes 11024384
  409.3 0.4 copy.14
  409.7 0.6 reduce_max.9
  410.3 0.7 copy.12
  (3 shorter events, 0.0 us)
Async XLA Ops:
  7.2 11.5 %copy-start.2 = (s32[256,16]{0,1:T(8,128)S(1)}, s32[256,16]{0,1:T(8,128)}, u32[]{:S(2)}) copy-start(s32[256,16]{0,1:T(8,128)} %param.15) | copy-start | bytes 49156
  7.2 227.4 %all-reduce.3.cloned.1.call-start = ((), (), s32[]{:S(2)}) async-start(), calls=%async_computation | async-start | bytes 4194304 | tf_op jit(solution)/shard_map/psum | solution.py:54
  13.1 38.9 %collective-permute-start = (bf16[3072,512]{1,0:T(8,128)(2,1)}, bf16[3072,512]{1,0:T(8,128)(2,1)}, u32[]{:S(2)}, u32[]{:S(2)}) collective-permute-start(bf16[3072,512]{1,0:T(8,128)(2,1)} %get-tuple-element.7), channel_id=1, source_target_pairs={{0,16},{16,32},{32,48},{48,64},{64,80},{80,96},{96,112},{112,128},... | collective-permute-start | bytes 9437192 | tf_op jit(solution)/shard_map/ppermute | solution.py:14
  15.0 44.2 %collective-permute-start.1 = (bf16[3072,512]{1,0:T(8,128)(2,1)}, bf16[3072,512]{1,0:T(8,128)(2,1)S(1)}, u32[]{:S(2)}, u32[]{:S(2)}) collective-permute-start(bf16[3072,512]{1,0:T(8,128)(2,1)} %get-tuple-element.6), channel_id=1, source_target_pairs={{16,0},{32,16},{48,32},{64,48},{80,64},{96,80},{112,96},{128,112},... | collective-permute-start | bytes 9437192 | tf_op jit(solution)/shard_map/ppermute | solution.py:17
  18.8 37.0 %copy-start = (bf16[3072,1024]{1,0:T(8,128)(2,1)S(1)}, bf16[3072,1024]{1,0:T(8,128)(2,1)}, u32[]{:S(2)}) copy-start(bf16[3072,1024]{1,0:T(8,128)(2,1)} %param.8) | copy-start | bytes 18874372
  59.2 3.2 copy-start.4
  59.2 3.2 copy-start.5
  85.7 0.7 copy-start.3
  85.7 0.7 copy-start.6
  85.7 148.8 %copy-start.1 = (f32[256,2048]{1,0:T(8,128)S(1)}, f32[256,2048]{1,0:T(8,128)}, u32[]{:S(2)}) copy-start(f32[256,2048]{1,0:T(8,128)} %param.10) | copy-start | bytes 6291460
  85.8 317.7 %all-reduce.5.cloned.1.call-start = ((), (), s32[]{:S(2)}) async-start(), calls=%async_computation.1 | async-start | bytes 4194304 | tf_op jit(solution)/shard_map/psum | solution.py:54
Sparse Core Ops, SparseCore 0:
  85.9 148.6 all-reduce.2
  258.4 145.0 all-reduce.4
where the time goes:
time: 420 us; the launch traced here: 418 us
  waiting for transfers between devices  327 us (78%)
  matrix products  47 us (11%)
  local copies, waits for them, and re-layouts  17.8 us (4%)
  between operations  14.1 us (3%)
  other arithmetic  6.47 us (2%)
  starting transfers between devices  5.85 us (1%)
    psum x2, waiting for transfers between devices, on_device(): grad = lax.psum(local, 'people') / total  293 us
    dot_general x2, matrix products, on_device(): local = jnp.dot(resid.T, wide, preferred_element_type=jnp.float32)  47 us
    ppermute x1, waiting for transfers between devices, with_halo(): lax.ppermute(lax.slice_in_dim(block, block.shape[dim] - width, None, axis...  33.1 us
    unnamed x18, local copies, waits for them, and re-layouts  8.67 us
  transfers between devices with their start and end apart: 4, of which 3 were waited for; matrix products, arithmetic and copies ran while one was open for 2% of the time, Pallas kernels for 0%

commit v1 on v0

v1 whole, which is shorter than its diff:
```python
import functools

import jax
import jax.numpy as jnp
from jax import lax
from jax.experimental import pallas as pl
from jax.experimental.pallas import tpu as pltpu
from jax.sharding import PartitionSpec as P

l1_share = 0.5
SIDE, MIRROR = 1, 14
NEAR = (0, 2, 4, 6)
GIVE = ((6,), (4, 2), (0,))
OWN = 16

TILE = 512
CUT = 256


def dot(a, b):
    return jnp.dot(a, b, preferred_element_type=jnp.float32)


def rows_of(me, hop):
    return pl.ds(pl.multiple_of((me ^ hop) * OWN, OWN), OWN)


def place(me, pieces, put):
    for k, piece in enumerate(pieces):
        hop = NEAR[k % len(NEAR)] ^ (k // len(NEAR) * SIDE)
        put(rows_of(me, hop), piece[:OWN, :])
        put(rows_of(me, hop ^ MIRROR), piece[OWN:, :])


def turn_kernel(n_blocks, n_pieces, *refs):
    where, *refs = refs
    blocks, target, refs = refs[:n_blocks], refs[n_blocks], refs[n_blocks + 1 :]
    pieces, refs = refs[:n_pieces], refs[n_pieces:]
    keep, *refs = refs
    gives, refs = refs[: len(GIVE)], refs[len(GIVE) :]
    people, reach = blocks[0].shape
    width = n_blocks * reach
    me = where[0]
    if n_pieces == 1:
        coef = pieces[0]
        grad, coef_t, resid_t = refs
    else:
        tail, grad, coef_t, resid_t, coef = refs

        def put(rows, piece):
            coef[rows, :] = piece[:, :width]
            tail[rows, :] = piece[:, width:]

        place(me, pieces, put)
    coef_t[...] = coef[...].T

    @pl.loop(0, people // TILE)
    def _(step):
        rows = pl.ds(pl.multiple_of(step * TILE, TILE), TILE)
        fitted = dot(blocks[0][rows, :], coef_t[:reach, :])
        for i in range(1, n_blocks):
            fitted += dot(blocks[i][rows, :], coef_t[i * reach : (i + 1) * reach, :])
        resid = (target[rows, :].astype(jnp.float32) - fitted).astype(jnp.bfloat16)
        resid_t[:, rows] = resid.T

    for i, block in enumerate(blocks):
        for j in range(0, reach, CUT):
            at = i * reach + j
            grad[:, at : at + CUT] = dot(resid_t[...], block[:, j : j + CUT])

    def read(hop):
        rows = rows_of(me, hop)
        return grad[rows, :] + coef[rows, :].astype(jnp.float32) * people

    for give, hops in zip(gives, GIVE):
        for n, hop in enumerate(hops):
            for k, far in enumerate((0, MIRROR)):
                at = (2 * n + k) * OWN
                give[at : at + OWN, :] = read(hop ^ SIDE ^ far).astype(jnp.bfloat16)
    for n, hop in enumerate(NEAR):
        for k, far in enumerate((0, MIRROR)):
            at = (2 * n + k) * OWN
            keep[at : at + OWN, :] = read(hop ^ far)


def output_kernel(where, *refs):
    *pieces, out = refs

    def put(rows, piece):
        out[rows, :] = piece.astype(jnp.float32)

    place(where[0], pieces, put)


def in_vmem(array):
    return pltpu.with_memory_space_constraint(array, pltpu.VMEM)


def specs(count):
    vmem = pl.BlockSpec(memory_space=pltpu.VMEM)
    return [pl.BlockSpec(memory_space=pltpu.SMEM)] + [vmem] * count


def local_grad(where, blocks, target, pieces):
    people, genes = target.shape
    reach = blocks[0].shape[1]
    width = len(blocks) * reach
    operands = [in_vmem(v) for v in (*blocks, target, *pieces)]
    outs = [pltpu.VMEM((2 * OWN * len(NEAR), width), jnp.float32)]
    outs += [pltpu.VMEM((2 * OWN * len(hops), width), jnp.bfloat16) for hops in GIVE]
    scratch = [
        pltpu.VMEM((genes, width), jnp.float32),
        pltpu.VMEM((width, genes), jnp.bfloat16),
        pltpu.VMEM((genes, people), jnp.bfloat16),
    ]
    if len(pieces) > 1:
        outs.append(pltpu.VMEM((genes, pieces[0].shape[1] - width), jnp.bfloat16))
        scratch.append(pltpu.VMEM((genes, width), jnp.bfloat16))
    return pl.pallas_call(
        functools.partial(turn_kernel, len(blocks), len(pieces)),
        out_shape=outs,
        in_specs=specs(len(operands)),
        out_specs=[pl.BlockSpec(memory_space=pltpu.VMEM)] * len(outs),
        scratch_shapes=scratch,
        compiler_params=pltpu.CompilerParams(vmem_limit_bytes=20 << 20),
        cost_estimate=pl.CostEstimate(
            flops=4 * people * width * genes, bytes_accessed=0, transcendentals=0
        ),
    )(where, *operands)


def swap(block, hop):
    count = lax.axis_size("people")
    return lax.ppermute(block, "people", [(i, i ^ hop) for i in range(count)])


def sum_to_owner(keep, gives):
    part = {}
    for hops, give in zip(GIVE, gives):
        got = swap(give, SIDE)
        for n, hop in enumerate(hops):
            at = NEAR.index(hop) * 2 * OWN
            part[hop] = keep[at : at + 2 * OWN] + got[2 * n * OWN : 2 * (n + 1) * OWN]
    total = part[0]
    for hop in (6, 4, 2):
        total = total + swap(part[hop].astype(jnp.bfloat16), hop)
    return total[:OWN] + swap(total[OWN:].astype(jnp.bfloat16), MIRROR)


def gather_rows(own):
    pair = jnp.concatenate([own, swap(own, MIRROR)], axis=0)
    got = {0: pair}
    for hop in (2, 6, 4):
        got[hop] = swap(pair, hop)
    return [got[hop] for hop in NEAR] + [swap(got[hop], SIDE) for hop in NEAR]


def shrink(coef, grad, penalty, step, mask):
    moved = coef + step[:, None] * grad
    cut = step[:, None] * penalty[:, None]
    kept = jnp.sign(moved) * jnp.maximum(jnp.abs(moved) - cut * l1_share, 0.0)
    return mask * kept / (1.0 + cut * (1.0 - l1_share))


def block_peaks(grad, mask, penalty):
    scaled = mask * jnp.abs(grad) / penalty[:, None]
    return jnp.max(scaled.reshape(grad.shape[0], -1, 128), axis=2)


def mask_of(start, end, active, first, width):
    place = first + jnp.arange(width, dtype=jnp.int32)
    inside = (place[None, :] >= start[:, None]) & (place[None, :] < end[:, None])
    blocks = jnp.repeat(active, 128, axis=1) > 0
    return jnp.where(inside & blocks, 1.0, 0.0).astype(jnp.float32)


def on_device(
    genotypes, expression, coef_start, penalty, step_size, window_start, window_end, active_blocks
):
    v_local = genotypes.shape[1]
    count = lax.axis_size("people")
    total = genotypes.shape[0] * count
    genes, width = coef_start.shape
    reach = (width - v_local) // 2
    chain = [(i, i + 1) for i in range(lax.axis_size("genome") - 1)]
    back = [(target, source) for source, target in chain]
    right = in_vmem(genotypes[:, v_local - reach :])
    right, rest = lax.optimization_barrier((right, genotypes))
    low = lax.ppermute(right, "genome", chain)
    left = in_vmem(rest[:, :reach])
    high = lax.ppermute(left, "genome", back)
    blocks = [low, left, right, high]

    me = lax.axis_index("people")
    where = me[None].astype(jnp.int32)
    first = lax.axis_index("genome") * v_local - reach

    def mine(array):
        return lax.dynamic_slice_in_dim(array, me * OWN, OWN, 0)

    penalty_own, step_own = mine(penalty), mine(step_size)
    mask_own = mask_of(mine(window_start), mine(window_end), mine(active_blocks), first, width)
    coef_own = mask_own * mine(coef_start)
    mask = mask_of(window_start, window_end, active_blocks, first, width)
    coef = (mask * coef_start).astype(jnp.bfloat16)

    keep, *gives = local_grad(where, blocks, expression, [coef])
    base = mine(coef).astype(jnp.float32)
    grad = sum_to_owner(keep, gives) / total - base
    peaks = block_peaks(grad, mask_own, penalty_own)
    coef_own = shrink(coef_own, grad, penalty_own, step_own, mask_own)
    sent = coef_own.astype(jnp.bfloat16)
    major = lax.reduce_precision(peaks, 8, 7)
    tail = jnp.concatenate([major, peaks - major], axis=1).astype(jnp.bfloat16)
    tail = jnp.pad(tail, ((0, 0), (0, 128 - tail.shape[1])))
    pieces = gather_rows(jnp.concatenate([sent, tail], axis=1))

    keep, *gives, tail = local_grad(where, blocks, expression, pieces)
    tail = tail.astype(jnp.float32)
    n_peaks = peaks.shape[1]
    peaks = tail[:, :n_peaks] + tail[:, n_peaks : 2 * n_peaks]
    grad = sum_to_owner(keep, gives) / total - sent.astype(jnp.float32)
    coef_own = shrink(coef_own, grad, penalty_own, step_own, mask_own)
    pieces = gather_rows(coef_own.astype(jnp.bfloat16))
    coef = pl.pallas_call(
        output_kernel,
        out_shape=jax.ShapeDtypeStruct((genes, width), jnp.float32),
        in_specs=specs(len(pieces)),
        out_specs=pl.BlockSpec(memory_space=pltpu.VMEM),
        compiler_params=pltpu.CompilerParams(vmem_limit_bytes=8 << 20),
    )(where, *[in_vmem(piece) for piece in pieces])
    return (coef, peaks)


def solution(mesh):
    return jax.shard_map(
        on_device,
        mesh=mesh,
        in_specs=(
            P("people", "genome"),
            P("people", "genome"),
            P("genome", None),
            P("genome"),
            P("genome"),
            P("genome"),
            P("genome"),
            P("genome", None),
        ),
        out_specs=(P("genome", None), P("genome", None)),
        check_vma=False,
    )
```

time: 420 us -> 191 us (0.45)
  waiting for transfers between devices: 327 us -> 87.5 us
  starting transfers between devices: 5.85 us -> 58.5 us
  matrix products: 47 us -> 0 us
  Pallas kernels: 0 us -> 26.2 us
  between operations: 14.1 us -> 0.93 us
  local copies, waits for them, and re-layouts: 17.8 us -> 9.69 us
    psum x2 -> x0, waiting for transfers between devices: 293 us -> none  [on_device(): grad = lax.psum(local, 'people') / total]
    ppermute x2 -> x32, waiting for transfers between devices: 33.1 us -> 87.5 us  [the longest x30 54.9 us: swap(): return lax.ppermute(block, 'people', [(i, i ^ hop) for i in range(count)])]
    ppermute x2 -> x32, starting transfers between devices: 5.55 us -> 58.5 us  [the longest x30 54.1 us: swap(): return lax.ppermute(block, 'people', [(i, i ^ hop) for i in range(count)])]
    dot_general x2 -> x0, matrix products: 47 us -> none  [on_device(): local = jnp.dot(resid.T, wide, preferred_element_type=jnp.float32)]
    pallas_call x0 -> x3, Pallas kernels: none -> 26.2 us  [the longest x2 24.7 us: local_grad(): pl.pallas_call(functools.partial(turn_kernel, len(blocks), len(pieces)),...]
    unnamed x1 -> x0, other arithmetic: 5.84 us -> none
    unnamed x18 -> x22, local copies, waits for them, and re-layouts: 8.67 us -> 3.62 us
    convert_element_type x0 -> x6, other arithmetic: none -> 4.54 us  [the longest x1 2.36 us: on_device(): coef = (mask * coef_start).astype(jnp.bfloat16)]
  transfers between devices with their start and end apart: 4 -> 32, of which waited for: 3 -> 20; matrix products, arithmetic and copies ran while one was open for 2% -> 3% of each run, Pallas kernels for 0% -> 0%
where the time goes in v1:
time: 191 us; the launch traced here: 189 us
  waiting for transfers between devices  87.5 us (46%)
  starting transfers between devices  58.5 us (31%)
  Pallas kernels  26.2 us (14%)
  local copies, waits for them, and re-layouts  9.69 us (5%)
  other arithmetic  6.37 us (3%)
    ppermute x30, waiting for transfers between devices, swap(): return lax.ppermute(block, 'people', [(i, i ^ hop) for i in range(count)])  54.9 us
    ppermute x30, starting transfers between devices, swap(): return lax.ppermute(block, 'people', [(i, i ^ hop) for i in range(count)])  54.1 us
    ppermute x1, waiting for transfers between devices, on_device(): high = lax.ppermute(left, 'genome', back)  29 us
    pallas_call x2, Pallas kernels, local_grad(): pl.pallas_call(functools.partial(turn_kernel, len(blocks), len(pieces)),...  24.7 us
  transfers between devices with their start and end apart: 32, of which 20 were waited for; matrix products, arithmetic and copies ran while one was open for 3% of the time, Pallas kernels for 0%

profile of v1, /device:TPU:56, one launch (start us, length us, event | category | flops | bytes accessed | tf_op | source)
XLA Modules:
  0.0 189.1 jit_solution(7883703936641958254)
XLA Ops:
  0.6 2.2 %slice.62.refs_3_ = bf16[3072,512]{1,0:T(8,128)(2,1)S(1)} slice(bf16[3072,1024]{1,0:T(8,128)(2,1)} %param.8), slice={[0:3072], [512:1024]} | slice | bytes 6291456 | tf_op jit(solution)/shard_map/slice | solution.py:187
  2.9 1.5 copy-done.4
  4.4 2.1 %slice.63.refs_2_ = bf16[3072,512]{1,0:T(8,128)(2,1)} slice(bf16[3072,1024]{1,0:T(8,128)(2,1)S(1)} %copy-done.4), slice={[0:3072], [0:512]} | slice | bytes 6291456 | tf_op jit(solution)/shard_map/slice | solution.py:190
  6.4 2.1 %collective-permute-start.1 = (bf16[3072,512]{1,0:T(8,128)(2,1)}, bf16[3072,512]{1,0:T(8,128)(2,1)}, u32[]{:S(2)}, u32[]{:S(2)}) collective-permute-start(bf16[3072,512]{1,0:T(8,128)(2,1)} %slice.63.refs_2_), channel_id=1, source_target_pairs={{16,0},{32,16},{48,32},{64,48},{80,64},{96,80},{112,96},{128,112},... | collective-permute-start | bytes 9437192 | tf_op jit(solution)/shard_map/ppermute | solution.py:191
  8.5 2.2 %collective-permute-start = (bf16[3072,512]{1,0:T(8,128)(2,1)S(1)}, bf16[3072,512]{1,0:T(8,128)(2,1)}, u32[]{:S(2)}, u32[]{:S(2)}) collective-permute-start(bf16[3072,512]{1,0:T(8,128)(2,1)S(1)} %slice.62.refs_3_), channel_id=1, source_target_pairs={{0,16},{16,32},{32,48},{48,64},{64,80},{80,96},{96,112},{112,128},... | collective-permute-start | bytes 9437192 | tf_op jit(solution)/shard_map/ppermute | solution.py:189
  10.9 1.3 broadcast_in_dim.44
  12.3 2.4 %multiply_convert_fusion.refs_6_ = bf16[256,2048]{1,0:T(8,128)(2,1)S(1)} fusion(f32[256,2048]{1,0:T(8,128)} %param.10, pred[32,8,16,128]{3,2,1,0:T(8,128)(4,1)S(1)} %bitcast.19, s32[2048]{0:T(1024)S(1)} %iota_add_fusion, s32[256]{0:T(256)S(1)} %copy-done.7, s32[256]{0:T(256)S(1)} %copy-done.6), kind=kLoop, calls=%fused_computation | loop fusion | flops 3670016 | bytes 3680256 | tf_op jit(solution)/shard_map/convert_element_type | solution.py:205
  14.6 29.0 %collective-permute-done.1.refs_4_ = bf16[3072,512]{1,0:T(8,128)(2,1)} collective-permute-done((bf16[3072,512]{1,0:T(8,128)(2,1)}, bf16[3072,512]{1,0:T(8,128)(2,1)}, u32[]{:S(2)}, u32[]{:S(2)}) %collective-permute-start.1) | collective-permute-done | bytes 3145760 | tf_op jit(solution)/shard_map/ppermute | solution.py:191
  43.6 3.6 %collective-permute-done.refs_1_ = bf16[3072,512]{1,0:T(8,128)(2,1)} collective-permute-done((bf16[3072,512]{1,0:T(8,128)(2,1)S(1)}, bf16[3072,512]{1,0:T(8,128)(2,1)}, u32[]{:S(2)}, u32[]{:S(2)}) %collective-permute-start) | collective-permute-done | bytes 3145760 | tf_op jit(solution)/shard_map/ppermute | solution.py:189
  47.2 12.3 %shard_map.95 = (f32[128,2048]{1,0:T(8,128)S(1)}, bf16[32,2048]{1,0:T(8,128)(2,1)S(1)}, bf16[64,2048]{1,0:T(8,128)(2,1)S(1)}, bf16[32,2048]{1,0:T(8,128)(2,1)S(1)}) custom-call(s32[1]{0:T(128)} %bitcast.refs_0_.where, bf16[3072,512]{1,0:T(8,128)(2,1)} %collective-permute-done.refs_1_, bf16[3072,512]{1,0:T(8,128)(2,1)} %slice.63.refs_2_, ...), custom_call_target="tpu_custom_call" | custom-call | flops 6442450944 | tf_op jit(solution)/shard_map/pallas_call | solution.py:119
  59.6 1.6 collective-permute-start.5
  61.2 0.5 collective-permute-start.3
  61.7 1.5 collective-permute-start.2
  63.2 6.9 %collective-permute-done.3 = bf16[32,2048]{1,0:T(8,128)(2,1)S(1)} collective-permute-done((bf16[32,2048]{1,0:T(8,128)(2,1)S(1)}, bf16[32,2048]{1,0:T(8,128)(2,1)S(1)}, u32[]{:S(2)}, u32[]{:S(2)}) %collective-permute-start.3) | collective-permute-done | bytes 131104 | tf_op jit(solution)/shard_map/ppermute | solution.py:134
  70.1 0.8 add_convert_fusion.4
  70.9 1.9 %collective-permute-start.4 = (bf16[32,2048]{1,0:T(8,128)(2,1)}, bf16[32,2048]{1,0:T(8,128)(2,1)}, u32[]{:S(2)}, u32[]{:S(2)}) collective-permute-start(bf16[32,2048]{1,0:T(8,128)(2,1)} %get-tuple-element.38), channel_id=1, source_target_pairs={{0,6},{1,7},{2,4},{3,5},{4,2},{5,3},{6,0},{7,1},{8,14},{9,15},{10,... | collective-permute-start | bytes 393224 | tf_op jit(solution)/shard_map/ppermute | solution.py:134
  72.8 1.4 collective-permute-start.6
  74.2 1.5 collective-permute-start.7
  76.0 1.6 collective-permute-done.4
  77.6 4.3 %collective-permute-done.6 = bf16[32,2048]{1,0:T(8,128)(2,1)} collective-permute-done((bf16[32,2048]{1,0:T(8,128)(2,1)}, bf16[32,2048]{1,0:T(8,128)(2,1)}, u32[]{:S(2)}, u32[]{:S(2)}) %collective-permute-start.6) | collective-permute-done | bytes 131104 | tf_op jit(solution)/shard_map/ppermute | solution.py:134
  81.9 1.9 %collective-permute-done.7 = bf16[32,2048]{1,0:T(8,128)(2,1)} collective-permute-done((bf16[32,2048]{1,0:T(8,128)(2,1)S(1)}, bf16[32,2048]{1,0:T(8,128)(2,1)}, u32[]{:S(2)}, u32[]{:S(2)}) %collective-permute-start.7) | collective-permute-done | bytes 131104 | tf_op jit(solution)/shard_map/ppermute | solution.py:134
  83.9 1.3 convert_add_fusion.1
  85.2 5.2 %collective-permute-start.8 = (bf16[16,2048]{1,0:T(8,128)(2,1)S(1)}, bf16[16,2048]{1,0:T(8,128)(2,1)S(1)}, u32[]{:S(2)}, u32[]{:S(2)}) collective-permute-start(bf16[16,2048]{1,0:T(8,128)(2,1)S(1)} %slice.129), channel_id=1, source_target_pairs={{0,14},{1,15},{2,12},{3,13},{4,10},{5,11},{6,8},{7,9},{8,6},{9,7},... | collective-permute-start | bytes 196616 | tf_op jit(solution)/shard_map/ppermute | solution.py:134
  90.5 2.2 %collective-permute-done.8 = bf16[16,2048]{1,0:T(8,128)(2,1)S(1)} collective-permute-done((bf16[16,2048]{1,0:T(8,128)(2,1)S(1)}, bf16[16,2048]{1,0:T(8,128)(2,1)S(1)}, u32[]{:S(2)}, u32[]{:S(2)}) %collective-permute-start.8) | collective-permute-done | bytes 65568 | tf_op jit(solution)/shard_map/ppermute | solution.py:134
  92.7 1.1 fusion.16
  94.1 5.4 %collective-permute-start.9 = (bf16[16,2176]{1,0:T(8,128)(2,1)S(1)}, bf16[16,2176]{1,0:T(8,128)(2,1)S(1)}, u32[]{:S(2)}, u32[]{:S(2)}) collective-permute-start(bf16[16,2176]{1,0:T(8,128)(2,1)S(1)} %pad_maximum_fusion.2), channel_id=1, source_target_pairs={{0,14},{1,15},{2,12},{3,13},{4,10},{5,11},{6,8},{7,9},{8,6},{9,7},... | collective-permute-start | bytes 208904 | tf_op jit(solution)/shard_map/ppermute | solution.py:134
  99.5 2.8 %collective-permute-done.9 = bf16[16,2176]{1,0:T(8,128)(2,1)S(1)} collective-permute-done((bf16[16,2176]{1,0:T(8,128)(2,1)S(1)}, bf16[16,2176]{1,0:T(8,128)(2,1)S(1)}, u32[]{:S(2)}, u32[]{:S(2)}) %collective-permute-start.9) | collective-permute-done | bytes 69664 | tf_op jit(solution)/shard_map/ppermute | solution.py:134
  102.3 2.1 %collective-permute-start.10 = (bf16[32,2176]{1,0:T(8,128)(2,1)S(1)}, bf16[32,2176]{1,0:T(8,128)(2,1)S(1)}, u32[]{:S(2)}, u32[]{:S(2)}) collective-permute-start(bf16[32,2176]{1,0:T(8,128)(2,1)S(1)} %pad_maximum_fusion.refs_6_), channel_id=1, source_target_pairs={{0,2},{1,3},{2,0},{3,1},{4,6},{5,7},{6,4},{7,5},{8,10},{9,11},{10,... | collective-permute-start | bytes 417800 | tf_op jit(solution)/shard_map/ppermute | solution.py:134
  104.4 0.6 collective-permute-start.11
  104.9 1.0 collective-permute-start.12
  105.9 1.5 collective-permute-start.13
  107.4 2.3 %collective-permute-done.10.refs_7_ = bf16[32,2176]{1,0:T(8,128)(2,1)S(1)} collective-permute-done((bf16[32,2176]{1,0:T(8,128)(2,1)S(1)}, bf16[32,2176]{1,0:T(8,128)(2,1)S(1)}, u32[]{:S(2)}, u32[]{:S(2)}) %collective-permute-start.10) | collective-permute-done | bytes 139296 | tf_op jit(solution)/shard_map/ppermute | solution.py:134
  109.7 1.5 collective-permute-start.14
  111.2 3.8 %collective-permute-done.11.refs_8_ = bf16[32,2176]{1,0:T(8,128)(2,1)S(1)} collective-permute-done((bf16[32,2176]{1,0:T(8,128)(2,1)S(1)}, bf16[32,2176]{1,0:T(8,128)(2,1)S(1)}, u32[]{:S(2)}, u32[]{:S(2)}) %collective-permute-start.11) | collective-permute-done | bytes 139296 | tf_op jit(solution)/shard_map/ppermute | solution.py:134
  115.0 1.5 collective-permute-start.15
  116.5 2.1 %collective-permute-done.12.refs_9_ = bf16[32,2176]{1,0:T(8,128)(2,1)S(1)} collective-permute-done((bf16[32,2176]{1,0:T(8,128)(2,1)S(1)}, bf16[32,2176]{1,0:T(8,128)(2,1)S(1)}, u32[]{:S(2)}, u32[]{:S(2)}) %collective-permute-start.12) | collective-permute-done | bytes 139296 | tf_op jit(solution)/shard_map/ppermute | solution.py:134
  118.5 1.5 collective-permute-start.16
  120.0 3.6 %collective-permute-done.16.refs_13_ = bf16[32,2176]{1,0:T(8,128)(2,1)S(1)} collective-permute-done((bf16[32,2176]{1,0:T(8,128)(2,1)S(1)}, bf16[32,2176]{1,0:T(8,128)(2,1)S(1)}, u32[]{:S(2)}, u32[]{:S(2)}) %collective-permute-start.16) | collective-permute-done | bytes 139296 | tf_op jit(solution)/shard_map/ppermute | solution.py:134
  123.6 1.4 copy-done.3
  125.0 12.4 %shard_map.96 = (f32[128,2048]{1,0:T(8,128)S(1)}, bf16[32,2048]{1,0:T(8,128)(2,1)S(1)}, bf16[64,2048]{1,0:T(8,128)(2,1)S(1)}, bf16[32,2048]{1,0:T(8,128)(2,1)S(1)}, bf16[256,128]{1,0:T(8,128)(2,1)S(1)}) custom-call(s32[1]{0:T(128)} %bitcast.refs_0_.where, bf16[3072,512]{1,0:T(8,128)(2,1)} %collective-permute-done.refs_1_, bf16[3072,512]{1,0:T(8,128)(2,1)} %slice.63.refs_2_, ...), custom_call_target="tpu_custom_call" | custom-call | flops 6442450944 | tf_op jit(solution)/shard_map/pallas_call | solution.py:119
  137.4 1.6 collective-permute-start.20
  139.0 0.5 collective-permute-start.18
  139.5 1.5 collective-permute-start.17
  141.0 7.0 %collective-permute-done.18 = bf16[32,2048]{1,0:T(8,128)(2,1)S(1)} collective-permute-done((bf16[32,2048]{1,0:T(8,128)(2,1)S(1)}, bf16[32,2048]{1,0:T(8,128)(2,1)S(1)}, u32[]{:S(2)}, u32[]{:S(2)}) %collective-permute-start.18) | collective-permute-done | bytes 131104 | tf_op jit(solution)/shard_map/ppermute | solution.py:134
  148.1 1.1 collective-permute-start.19
  149.2 2.5 %collective-permute-start.22 = (bf16[32,2048]{1,0:T(8,128)(2,1)S(1)}, bf16[32,2048]{1,0:T(8,128)(2,1)S(1)}, u32[]{:S(2)}, u32[]{:S(2)}) collective-permute-start(bf16[32,2048]{1,0:T(8,128)(2,1)S(1)} %get-tuple-element.34), channel_id=1, source_target_pairs={{0,2},{1,3},{2,0},{3,1},{4,6},{5,7},{6,4},{7,5},{8,10},{9,11},{10,... | collective-permute-start | bytes 393224 | tf_op jit(solution)/shard_map/ppermute | solution.py:134
  151.7 3.5 %collective-permute-done.19 = bf16[32,2048]{1,0:T(8,128)(2,1)S(1)} collective-permute-done((bf16[32,2048]{1,0:T(8,128)(2,1)S(1)}, bf16[32,2048]{1,0:T(8,128)(2,1)S(1)}, u32[]{:S(2)}, u32[]{:S(2)}) %collective-permute-start.19) | collective-permute-done | bytes 131104 | tf_op jit(solution)/shard_map/ppermute | solution.py:134
  155.2 0.8 collective-permute-done.22
  156.2 4.4 %collective-permute-start.23 = (bf16[16,2048]{1,0:T(8,128)(2,1)S(1)}, bf16[16,2048]{1,0:T(8,128)(2,1)S(1)}, u32[]{:S(2)}, u32[]{:S(2)}) collective-permute-start(bf16[16,2048]{1,0:T(8,128)(2,1)S(1)} %slice.128), channel_id=1, source_target_pairs={{0,14},{1,15},{2,12},{3,13},{4,10},{5,11},{6,8},{7,9},{8,6},{9,7},... | collective-permute-start | bytes 196616 | tf_op jit(solution)/shard_map/ppermute | solution.py:134
  160.5 3.3 %collective-permute-done.23 = bf16[16,2048]{1,0:T(8,128)(2,1)S(1)} collective-permute-done((bf16[16,2048]{1,0:T(8,128)(2,1)S(1)}, bf16[16,2048]{1,0:T(8,128)(2,1)S(1)}, u32[]{:S(2)}, u32[]{:S(2)}) %collective-permute-start.23) | collective-permute-done | bytes 65568 | tf_op jit(solution)/shard_map/ppermute | solution.py:134
  163.8 0.2 fusion.5
  164.0 4.6 %collective-permute-start.24 = (bf16[16,2048]{1,0:T(8,128)(2,1)S(1)}, bf16[16,2048]{1,0:T(8,128)(2,1)S(1)}, u32[]{:S(2)}, u32[]{:S(2)}) collective-permute-start(bf16[16,2048]{1,0:T(8,128)(2,1)S(1)} %fusion.5), channel_id=1, source_target_pairs={{0,14},{1,15},{2,12},{3,13},{4,10},{5,11},{6,8},{7,9},{8,6},{9,7},... | collective-permute-start | bytes 196616 | tf_op jit(solution)/shard_map/ppermute | solution.py:134
  168.5 3.4 %collective-permute-done.24 = bf16[16,2048]{1,0:T(8,128)(2,1)S(1)} collective-permute-done((bf16[16,2048]{1,0:T(8,128)(2,1)S(1)}, bf16[16,2048]{1,0:T(8,128)(2,1)S(1)}, u32[]{:S(2)}, u32[]{:S(2)}) %collective-permute-start.24) | collective-permute-done | bytes 65568 | tf_op jit(solution)/shard_map/ppermute | solution.py:134
  172.1 2.5 %collective-permute-start.26 = (bf16[32,2048]{1,0:T(8,128)(2,1)S(1)}, bf16[32,2048]{1,0:T(8,128)(2,1)S(1)}, u32[]{:S(2)}, u32[]{:S(2)}) collective-permute-start(bf16[32,2048]{1,0:T(8,128)(2,1)S(1)} %pad_maximum_fusion.1.refs_0_), channel_id=1, source_target_pairs={{0,4},{1,5},{2,6},{3,7},{4,0},{5,1},{6,2},{7,3},{8,12},{9,13},{10,... | collective-permute-start | bytes 393224 | tf_op jit(solution)/shard_map/ppermute | solution.py:134
  174.5 1.0 collective-permute-start.27
  175.6 1.6 collective-permute-start.28
  177.1 1.4 collective-permute-start.29
  178.5 1.3 collective-permute-done.26.refs_2_
  179.8 1.5 collective-permute-start.30
  181.3 1.4 collective-permute-done.27.refs_3_
  182.7 1.5 collective-permute-start.31
  184.3 0.7 copy.12
  185.0 2.7 %collective-permute-done.31.refs_7_ = bf16[32,2048]{1,0:T(8,128)(2,1)S(1)} collective-permute-done((bf16[32,2048]{1,0:T(8,128)(2,1)S(1)}, bf16[32,2048]{1,0:T(8,128)(2,1)S(1)}, u32[]{:S(2)}, u32[]{:S(2)}) %collective-permute-start.31) | collective-permute-done | bytes 131104 | tf_op jit(solution)/shard_map/ppermute | solution.py:134
  187.7 1.5 shard_map.97
  (54 shorter events, 1.3 us)
Async XLA Ops:
  0.6 3.7 %copy-start.4 = (bf16[3072,1024]{1,0:T(8,128)(2,1)S(1)}, bf16[3072,1024]{1,0:T(8,128)(2,1)}, u32[]{:S(2)}) copy-start(bf16[3072,1024]{1,0:T(8,128)(2,1)} %param.8) | copy-start | bytes 18874372
  4.4 6.4 %copy-start.5 = (s32[256,16]{0,1:T(8,128)S(1)}, s32[256,16]{0,1:T(8,128)}, u32[]{:S(2)}) copy-start(s32[256,16]{0,1:T(8,128)} %param.15) | copy-start | bytes 49156
  4.4 7.9 %copy-start.6 = (s32[256]{0:T(256)S(1)}, s32[256]{0:T(256)}, u32[]{:S(2)}) copy-start(s32[256]{0:T(256)} %param.13) | copy-start | bytes 3076
  4.4 7.9 %copy-start.7 = (s32[256]{0:T(256)S(1)}, s32[256]{0:T(256)}, u32[]{:S(2)}) copy-start(s32[256]{0:T(256)} %param.14) | copy-start | bytes 3076
  6.4 37.2 %collective-permute-start.1 = (bf16[3072,512]{1,0:T(8,128)(2,1)}, bf16[3072,512]{1,0:T(8,128)(2,1)}, u32[]{:S(2)}, u32[]{:S(2)}) collective-permute-start(bf16[3072,512]{1,0:T(8,128)(2,1)} %slice.63.refs_2_), channel_id=1, source_target_pairs={{16,0},{32,16},{48,32},{64,48},{80,64},{96,80},{112,96},{128,112},... | collective-permute-start | bytes 9437192 | tf_op jit(solution)/shard_map/ppermute | solution.py:191
  8.5 38.7 %collective-permute-start = (bf16[3072,512]{1,0:T(8,128)(2,1)S(1)}, bf16[3072,512]{1,0:T(8,128)(2,1)}, u32[]{:S(2)}, u32[]{:S(2)}) collective-permute-start(bf16[3072,512]{1,0:T(8,128)(2,1)S(1)} %slice.62.refs_3_), channel_id=1, source_target_pairs={{0,16},{16,32},{32,48},{48,64},{64,80},{80,96},{96,112},{112,128},... | collective-permute-start | bytes 9437192 | tf_op jit(solution)/shard_map/ppermute | solution.py:189
  10.9 36.3 %copy-start.2 = (bf16[3072,256]{1,0:T(8,128)(2,1)S(1)}, bf16[3072,256]{1,0:T(8,128)(2,1)}, u32[]{:S(2)}) copy-start(bf16[3072,256]{1,0:T(8,128)(2,1)} %refs_5_.3) | copy-start | bytes 4718596
  14.6 44.9 %copy-start = (bf16[256,2048]{1,0:T(8,128)(2,1)}, bf16[256,2048]{1,0:T(8,128)(2,1)S(1)}, u32[]{:S(2)}) copy-start(bf16[256,2048]{1,0:T(8,128)(2,1)S(1)} %multiply_convert_fusion.refs_6_) | copy-start | bytes 3145732
  59.6 10.6 %copy-start.1 = (f32[128,2048]{1,0:T(8,128)}, f32[128,2048]{1,0:T(8,128)S(1)}, u32[]{:S(2)}) copy-start(f32[128,2048]{1,0:T(8,128)S(1)} %get-tuple-element.15) | copy-start | bytes 3145732
  59.6 30.8 %copy-start.8 = (f32[256]{0:T(256)S(1)}, f32[256]{0:T(256)}, u32[]{:S(2)}) copy-start(f32[256]{0:T(256)} %param.11) | copy-start | bytes 3076
  59.6 30.8 %copy-start.9 = (f32[256]{0:T(256)S(1)}, f32[256]{0:T(256)}, u32[]{:S(2)}) copy-start(f32[256]{0:T(256)} %param.12) | copy-start | bytes 3076
  59.6 10.5 %collective-permute-start.5 = (bf16[64,2048]{1,0:T(8,128)(2,1)S(1)}, bf16[64,2048]{1,0:T(8,128)(2,1)S(1)}, u32[]{:S(2)}, u32[]{:S(2)}) collective-permute-start(bf16[64,2048]{1,0:T(8,128)(2,1)S(1)} %get-tuple-element.18), channel_id=1, source_target_pairs={{0,1},{1,0},{2,3},{3,2},{4,5},{5,4},{6,7},{7,6},{8,9},{9,8},{10,11... | collective-permute-start | bytes 786440 | tf_op jit(solution)/shard_map/ppermute | solution.py:134
  61.2 8.9 %collective-permute-start.3 = (bf16[32,2048]{1,0:T(8,128)(2,1)S(1)}, bf16[32,2048]{1,0:T(8,128)(2,1)S(1)}, u32[]{:S(2)}, u32[]{:S(2)}) collective-permute-start(bf16[32,2048]{1,0:T(8,128)(2,1)S(1)} %get-tuple-element.17), channel_id=1, source_target_pairs={{0,1},{1,0},{2,3},{3,2},{4,5},{5,4},{6,7},{7,6},{8,9},{9,8},{10,11... | collective-permute-start | bytes 393224 | tf_op jit(solution)/shard_map/ppermute | solution.py:134
  61.7 14.2 %collective-permute-start.2 = (bf16[32,2048]{1,0:T(8,128)(2,1)S(1)}, bf16[32,2048]{1,0:T(8,128)(2,1)}, u32[]{:S(2)}, u32[]{:S(2)}) collective-permute-start(bf16[32,2048]{1,0:T(8,128)(2,1)S(1)} %get-tuple-element.16), channel_id=1, source_target_pairs={{0,1},{1,0},{2,3},{3,2},{4,5},{5,4},{6,7},{7,6},{8,9},{9,8},{10,11... | collective-permute-start | bytes 393224 | tf_op jit(solution)/shard_map/ppermute | solution.py:134
  70.9 6.7 %collective-permute-start.4 = (bf16[32,2048]{1,0:T(8,128)(2,1)}, bf16[32,2048]{1,0:T(8,128)(2,1)}, u32[]{:S(2)}, u32[]{:S(2)}) collective-permute-start(bf16[32,2048]{1,0:T(8,128)(2,1)} %get-tuple-element.38), channel_id=1, source_target_pairs={{0,6},{1,7},{2,4},{3,5},{4,2},{5,3},{6,0},{7,1},{8,14},{9,15},{10,... | collective-permute-start | bytes 393224 | tf_op jit(solution)/shard_map/ppermute | solution.py:134
  72.8 9.1 %collective-permute-start.6 = (bf16[32,2048]{1,0:T(8,128)(2,1)}, bf16[32,2048]{1,0:T(8,128)(2,1)}, u32[]{:S(2)}, u32[]{:S(2)}) collective-permute-start(bf16[32,2048]{1,0:T(8,128)(2,1)} %get-tuple-element.35), channel_id=1, source_target_pairs={{0,4},{1,5},{2,6},{3,7},{4,0},{5,1},{6,2},{7,3},{8,12},{9,13},{10,... | collective-permute-start | bytes 393224 | tf_op jit(solution)/shard_map/ppermute | solution.py:134
  74.2 9.7 %collective-permute-start.7 = (bf16[32,2048]{1,0:T(8,128)(2,1)S(1)}, bf16[32,2048]{1,0:T(8,128)(2,1)}, u32[]{:S(2)}, u32[]{:S(2)}) collective-permute-start(bf16[32,2048]{1,0:T(8,128)(2,1)S(1)} %get-tuple-element.36), channel_id=1, source_target_pairs={{0,2},{1,3},{2,0},{3,1},{4,6},{5,7},{6,4},{7,5},{8,10},{9,11},{10,... | collective-permute-start | bytes 393224 | tf_op jit(solution)/shard_map/ppermute | solution.py:134
  85.2 7.5 %collective-permute-start.8 = (bf16[16,2048]{1,0:T(8,128)(2,1)S(1)}, bf16[16,2048]{1,0:T(8,128)(2,1)S(1)}, u32[]{:S(2)}, u32[]{:S(2)}) collective-permute-start(bf16[16,2048]{1,0:T(8,128)(2,1)S(1)} %slice.129), channel_id=1, source_target_pairs={{0,14},{1,15},{2,12},{3,13},{4,10},{5,11},{6,8},{7,9},{8,6},{9,7},... | collective-permute-start | bytes 196616 | tf_op jit(solution)/shard_map/ppermute | solution.py:134
  94.1 8.1 %collective-permute-start.9 = (bf16[16,2176]{1,0:T(8,128)(2,1)S(1)}, bf16[16,2176]{1,0:T(8,128)(2,1)S(1)}, u32[]{:S(2)}, u32[]{:S(2)}) collective-permute-start(bf16[16,2176]{1,0:T(8,128)(2,1)S(1)} %pad_maximum_fusion.2), channel_id=1, source_target_pairs={{0,14},{1,15},{2,12},{3,13},{4,10},{5,11},{6,8},{7,9},{8,6},{9,7},... | collective-permute-start | bytes 208904 | tf_op jit(solution)/shard_map/ppermute | solution.py:134
  102.3 7.4 %collective-permute-start.10 = (bf16[32,2176]{1,0:T(8,128)(2,1)S(1)}, bf16[32,2176]{1,0:T(8,128)(2,1)S(1)}, u32[]{:S(2)}, u32[]{:S(2)}) collective-permute-start(bf16[32,2176]{1,0:T(8,128)(2,1)S(1)} %pad_maximum_fusion.refs_6_), channel_id=1, source_target_pairs={{0,2},{1,3},{2,0},{3,1},{4,6},{5,7},{6,4},{7,5},{8,10},{9,11},{10,... | collective-permute-start | bytes 417800 | tf_op jit(solution)/shard_map/ppermute | solution.py:134
  104.4 10.6 %collective-permute-start.11 = (bf16[32,2176]{1,0:T(8,128)(2,1)S(1)}, bf16[32,2176]{1,0:T(8,128)(2,1)S(1)}, u32[]{:S(2)}, u32[]{:S(2)}) collective-permute-start(bf16[32,2176]{1,0:T(8,128)(2,1)S(1)} %pad_maximum_fusion.refs_6_), channel_id=1, source_target_pairs={{0,4},{1,5},{2,6},{3,7},{4,0},{5,1},{6,2},{7,3},{8,12},{9,13},{10,... | collective-permute-start | bytes 417800 | tf_op jit(solution)/shard_map/ppermute | solution.py:134
  104.9 13.6 %collective-permute-start.12 = (bf16[32,2176]{1,0:T(8,128)(2,1)S(1)}, bf16[32,2176]{1,0:T(8,128)(2,1)S(1)}, u32[]{:S(2)}, u32[]{:S(2)}) collective-permute-start(bf16[32,2176]{1,0:T(8,128)(2,1)S(1)} %pad_maximum_fusion.refs_6_), channel_id=1, source_target_pairs={{0,6},{1,7},{2,4},{3,5},{4,2},{5,3},{6,0},{7,1},{8,14},{9,15},{10,... | collective-permute-start | bytes 417800 | tf_op jit(solution)/shard_map/ppermute | solution.py:134
  105.9 14.1 %collective-permute-start.13 = (bf16[32,2176]{1,0:T(8,128)(2,1)S(1)}, bf16[32,2176]{1,0:T(8,128)(2,1)S(1)}, u32[]{:S(2)}, u32[]{:S(2)}) collective-permute-start(bf16[32,2176]{1,0:T(8,128)(2,1)S(1)} %pad_maximum_fusion.refs_6_), channel_id=1, source_target_pairs={{0,1},{1,0},{2,3},{3,2},{4,5},{5,4},{6,7},{7,6},{8,9},{9,8},{10,11... | collective-permute-start | bytes 417800 | tf_op jit(solution)/shard_map/ppermute | solution.py:134
  109.7 10.4 %collective-permute-start.14 = (bf16[32,2176]{1,0:T(8,128)(2,1)S(1)}, bf16[32,2176]{1,0:T(8,128)(2,1)S(1)}, u32[]{:S(2)}, u32[]{:S(2)}) collective-permute-start(bf16[32,2176]{1,0:T(8,128)(2,1)S(1)} %collective-permute-done.10.refs_7_), channel_id=1, source_target_pairs={{0,1},{1,0},{2,3},{3,2},{4,5},{5,4},{6,7},{7,6},{8,9},{9,8},{10,11... | collective-permute-start | bytes 417800 | tf_op jit(solution)/shard_map/ppermute | solution.py:134
  115.0 5.1 %collective-permute-start.15 = (bf16[32,2176]{1,0:T(8,128)(2,1)S(1)}, bf16[32,2176]{1,0:T(8,128)(2,1)S(1)}, u32[]{:S(2)}, u32[]{:S(2)}) collective-permute-start(bf16[32,2176]{1,0:T(8,128)(2,1)S(1)} %collective-permute-done.11.refs_8_), channel_id=1, source_target_pairs={{0,1},{1,0},{2,3},{3,2},{4,5},{5,4},{6,7},{7,6},{8,9},{9,8},{10,11... | collective-permute-start | bytes 417800 | tf_op jit(solution)/shard_map/ppermute | solution.py:134
  118.5 5.1 %collective-permute-start.16 = (bf16[32,2176]{1,0:T(8,128)(2,1)S(1)}, bf16[32,2176]{1,0:T(8,128)(2,1)S(1)}, u32[]{:S(2)}, u32[]{:S(2)}) collective-permute-start(bf16[32,2176]{1,0:T(8,128)(2,1)S(1)} %collective-permute-done.12.refs_9_), channel_id=1, source_target_pairs={{0,1},{1,0},{2,3},{3,2},{4,5},{5,4},{6,7},{7,6},{8,9},{9,8},{10,11... | collective-permute-start | bytes 417800 | tf_op jit(solution)/shard_map/ppermute | solution.py:134
  123.6 1.4 copy-start.3
  137.4 10.6 %collective-permute-start.20 = (bf16[64,2048]{1,0:T(8,128)(2,1)S(1)}, bf16[64,2048]{1,0:T(8,128)(2,1)S(1)}, u32[]{:S(2)}, u32[]{:S(2)}) collective-permute-start(bf16[64,2048]{1,0:T(8,128)(2,1)S(1)} %get-tuple-element.22), channel_id=1, source_target_pairs={{0,1},{1,0},{2,3},{3,2},{4,5},{5,4},{6,7},{7,6},{8,9},{9,8},{10,11... | collective-permute-start | bytes 786440 | tf_op jit(solution)/shard_map/ppermute | solution.py:134
  139.0 9.0 %collective-permute-start.18 = (bf16[32,2048]{1,0:T(8,128)(2,1)S(1)}, bf16[32,2048]{1,0:T(8,128)(2,1)S(1)}, u32[]{:S(2)}, u32[]{:S(2)}) collective-permute-start(bf16[32,2048]{1,0:T(8,128)(2,1)S(1)} %get-tuple-element.21), channel_id=1, source_target_pairs={{0,1},{1,0},{2,3},{3,2},{4,5},{5,4},{6,7},{7,6},{8,9},{9,8},{10,11... | collective-permute-start | bytes 393224 | tf_op jit(solution)/shard_map/ppermute | solution.py:134
  139.5 12.1 %collective-permute-start.17 = (bf16[32,2048]{1,0:T(8,128)(2,1)S(1)}, bf16[32,2048]{1,0:T(8,128)(2,1)S(1)}, u32[]{:S(2)}, u32[]{:S(2)}) collective-permute-start(bf16[32,2048]{1,0:T(8,128)(2,1)S(1)} %get-tuple-element.20), channel_id=1, source_target_pairs={{0,1},{1,0},{2,3},{3,2},{4,5},{5,4},{6,7},{7,6},{8,9},{9,8},{10,11... | collective-permute-start | bytes 393224 | tf_op jit(solution)/shard_map/ppermute | solution.py:134
  148.1 7.1 %collective-permute-start.19 = (bf16[32,2048]{1,0:T(8,128)(2,1)S(1)}, bf16[32,2048]{1,0:T(8,128)(2,1)S(1)}, u32[]{:S(2)}, u32[]{:S(2)}) collective-permute-start(bf16[32,2048]{1,0:T(8,128)(2,1)S(1)} %get-tuple-element.37), channel_id=1, source_target_pairs={{0,6},{1,7},{2,4},{3,5},{4,2},{5,3},{6,0},{7,1},{8,14},{9,15},{10,... | collective-permute-start | bytes 393224 | tf_op jit(solution)/shard_map/ppermute | solution.py:134
  149.2 6.0 %collective-permute-start.21 = (bf16[32,2048]{1,0:T(8,128)(2,1)S(1)}, bf16[32,2048]{1,0:T(8,128)(2,1)S(1)}, u32[]{:S(2)}, u32[]{:S(2)}) collective-permute-start(bf16[32,2048]{1,0:T(8,128)(2,1)S(1)} %get-tuple-element.33), channel_id=1, source_target_pairs={{0,4},{1,5},{2,6},{3,7},{4,0},{5,1},{6,2},{7,3},{8,12},{9,13},{10,... | collective-permute-start | bytes 393224 | tf_op jit(solution)/shard_map/ppermute | solution.py:134
  149.2 6.9 %collective-permute-start.22 = (bf16[32,2048]{1,0:T(8,128)(2,1)S(1)}, bf16[32,2048]{1,0:T(8,128)(2,1)S(1)}, u32[]{:S(2)}, u32[]{:S(2)}) collective-permute-start(bf16[32,2048]{1,0:T(8,128)(2,1)S(1)} %get-tuple-element.34), channel_id=1, source_target_pairs={{0,2},{1,3},{2,0},{3,1},{4,6},{5,7},{6,4},{7,5},{8,10},{9,11},{10,... | collective-permute-start | bytes 393224 | tf_op jit(solution)/shard_map/ppermute | solution.py:134
  156.2 7.6 %collective-permute-start.23 = (bf16[16,2048]{1,0:T(8,128)(2,1)S(1)}, bf16[16,2048]{1,0:T(8,128)(2,1)S(1)}, u32[]{:S(2)}, u32[]{:S(2)}) collective-permute-start(bf16[16,2048]{1,0:T(8,128)(2,1)S(1)} %slice.128), channel_id=1, source_target_pairs={{0,14},{1,15},{2,12},{3,13},{4,10},{5,11},{6,8},{7,9},{8,6},{9,7},... | collective-permute-start | bytes 196616 | tf_op jit(solution)/shard_map/ppermute | solution.py:134
  164.0 8.0 %collective-permute-start.24 = (bf16[16,2048]{1,0:T(8,128)(2,1)S(1)}, bf16[16,2048]{1,0:T(8,128)(2,1)S(1)}, u32[]{:S(2)}, u32[]{:S(2)}) collective-permute-start(bf16[16,2048]{1,0:T(8,128)(2,1)S(1)} %fusion.5), channel_id=1, source_target_pairs={{0,14},{1,15},{2,12},{3,13},{4,10},{5,11},{6,8},{7,9},{8,6},{9,7},... | collective-permute-start | bytes 196616 | tf_op jit(solution)/shard_map/ppermute | solution.py:134
  172.0 5.2 %collective-permute-start.25 = (bf16[32,2048]{1,0:T(8,128)(2,1)S(1)}, bf16[32,2048]{1,0:T(8,128)(2,1)S(1)}, u32[]{:S(2)}, u32[]{:S(2)}) collective-permute-start(bf16[32,2048]{1,0:T(8,128)(2,1)S(1)} %pad_maximum_fusion.1.refs_0_), channel_id=1, source_target_pairs={{0,2},{1,3},{2,0},{3,1},{4,6},{5,7},{6,4},{7,5},{8,10},{9,11},{10,... | collective-permute-start | bytes 393224 | tf_op jit(solution)/shard_map/ppermute | solution.py:134
  172.1 7.8 %collective-permute-start.26 = (bf16[32,2048]{1,0:T(8,128)(2,1)S(1)}, bf16[32,2048]{1,0:T(8,128)(2,1)S(1)}, u32[]{:S(2)}, u32[]{:S(2)}) collective-permute-start(bf16[32,2048]{1,0:T(8,128)(2,1)S(1)} %pad_maximum_fusion.1.refs_0_), channel_id=1, source_target_pairs={{0,4},{1,5},{2,6},{3,7},{4,0},{5,1},{6,2},{7,3},{8,12},{9,13},{10,... | collective-permute-start | bytes 393224 | tf_op jit(solution)/shard_map/ppermute | solution.py:134
  174.5 8.2 %collective-permute-start.27 = (bf16[32,2048]{1,0:T(8,128)(2,1)S(1)}, bf16[32,2048]{1,0:T(8,128)(2,1)S(1)}, u32[]{:S(2)}, u32[]{:S(2)}) collective-permute-start(bf16[32,2048]{1,0:T(8,128)(2,1)S(1)} %pad_maximum_fusion.1.refs_0_), channel_id=1, source_target_pairs={{0,6},{1,7},{2,4},{3,5},{4,2},{5,3},{6,0},{7,1},{8,14},{9,15},{10,... | collective-permute-start | bytes 393224 | tf_op jit(solution)/shard_map/ppermute | solution.py:134
  175.6 9.4 %collective-permute-start.28 = (bf16[32,2048]{1,0:T(8,128)(2,1)S(1)}, bf16[32,2048]{1,0:T(8,128)(2,1)S(1)}, u32[]{:S(2)}, u32[]{:S(2)}) collective-permute-start(bf16[32,2048]{1,0:T(8,128)(2,1)S(1)} %pad_maximum_fusion.1.refs_0_), channel_id=1, source_target_pairs={{0,1},{1,0},{2,3},{3,2},{4,5},{5,4},{6,7},{7,6},{8,9},{9,8},{10,11... | collective-permute-start | bytes 393224 | tf_op jit(solution)/shard_map/ppermute | solution.py:134
  177.1 7.8 %collective-permute-start.29 = (bf16[32,2048]{1,0:T(8,128)(2,1)S(1)}, bf16[32,2048]{1,0:T(8,128)(2,1)S(1)}, u32[]{:S(2)}, u32[]{:S(2)}) collective-permute-start(bf16[32,2048]{1,0:T(8,128)(2,1)S(1)} %collective-permute-done.25.refs_1_), channel_id=1, source_target_pairs={{0,1},{1,0},{2,3},{3,2},{4,5},{5,4},{6,7},{7,6},{8,9},{9,8},{10,11... | collective-permute-start | bytes 393224 | tf_op jit(solution)/shard_map/ppermute | solution.py:134
  179.8 5.1 %collective-permute-start.30 = (bf16[32,2048]{1,0:T(8,128)(2,1)S(1)}, bf16[32,2048]{1,0:T(8,128)(2,1)S(1)}, u32[]{:S(2)}, u32[]{:S(2)}) collective-permute-start(bf16[32,2048]{1,0:T(8,128)(2,1)S(1)} %collective-permute-done.26.refs_2_), channel_id=1, source_target_pairs={{0,1},{1,0},{2,3},{3,2},{4,5},{5,4},{6,7},{7,6},{8,9},{9,8},{10,11... | collective-permute-start | bytes 393224 | tf_op jit(solution)/shard_map/ppermute | solution.py:134
  182.7 5.0 %collective-permute-start.31 = (bf16[32,2048]{1,0:T(8,128)(2,1)S(1)}, bf16[32,2048]{1,0:T(8,128)(2,1)S(1)}, u32[]{:S(2)}, u32[]{:S(2)}) collective-permute-start(bf16[32,2048]{1,0:T(8,128)(2,1)S(1)} %collective-permute-done.27.refs_3_), channel_id=1, source_target_pairs={{0,1},{1,0},{2,3},{3,2},{4,5},{5,4},{6,7},{7,6},{8,9},{9,8},{10,11... | collective-permute-start | bytes 393224 | tf_op jit(solution)/shard_map/ppermute | solution.py:134

commit v2 on v1

v2 whole, which is shorter than its diff:
```python
import functools

import jax
import jax.numpy as jnp
from jax import lax
from jax.experimental import pallas as pl
from jax.experimental.pallas import tpu as pltpu
from jax.sharding import PartitionSpec as P

l1_share = 0.5
SIDE, MIRROR = 1, 14
NEAR = (0, 2, 4, 6)
GIVE = ((6,), (4, 2), (0,))
OWN = 16
PEOPLE = 16
LANES = 128
START, END, PENALTY, STEP = 16, 17, 18, 19

TILE = 768
PARTS = (2304, 768)
CUT = 256


def dot(a, b):
    return jnp.dot(a, b, preferred_element_type=jnp.float32)


def rows_of(me, hop):
    return pl.ds(pl.multiple_of((me ^ hop) * OWN, OWN), OWN)


def dot_t(a, b):
    return lax.dot_general(a, b, (((1,), (1,)), ((), ())), preferred_element_type=jnp.float32)


def person(where):
    return where[0] % PEOPLE


def place(me, pieces, put):
    for k, piece in enumerate(pieces):
        hop = NEAR[k % len(NEAR)] ^ (k // len(NEAR) * SIDE)
        put(rows_of(me, hop), piece[:OWN, :])
        put(rows_of(me, hop ^ MIRROR), piece[OWN:, :])


def turn_kernel(parts, n_pieces, add, pack, *refs):
    where, *refs = refs
    blocks, refs = refs[: 4 * len(parts)], refs[4 * len(parts) :]
    target, *refs = refs
    pieces, refs = refs[:n_pieces], refs[n_pieces:]
    if add:
        prior, *refs = refs
    reach = blocks[0].shape[1]
    width = 4 * reach
    me = person(where)
    if pack:
        keep, *refs = refs
        gives, refs = refs[: len(GIVE)], refs[len(GIVE) :]
    if n_pieces > 1:
        peaks, *refs = refs
    grad, resid_t, *refs = refs
    if n_pieces > 1:
        coef, tail = refs

        def put(rows, piece):
            coef[rows, :] = piece[:, :width]
            tail[rows, :] = piece[:, width:]

        place(me, pieces, put)
        count = peaks.shape[0]
        flat = tail[...].astype(jnp.float32).T
        peaks[...] = flat[:count, :] + flat[count : 2 * count, :]
    else:
        (coef,) = pieces

    done = 0
    for k, (first, count) in enumerate(parts):
        for step in range(0, count, TILE):
            rows = pl.ds(step, TILE)
            fitted = 0.0
            for i in range(4):
                weights = coef[:, i * reach : (i + 1) * reach]
                fitted += dot_t(blocks[4 * k + i][rows, :], weights)
            goal = target[pl.ds(first + step, TILE), :].astype(jnp.float32)
            resid_t[:, pl.ds(done, TILE)] = (goal - fitted).astype(jnp.bfloat16).T
            done += TILE

    for i in range(4):
        for j in range(0, reach, CUT):
            at = i * reach + j
            total = prior[:, at : at + CUT] if add else 0.0
            done = 0
            for k, (first, count) in enumerate(parts):
                block = blocks[4 * k + i]
                total += dot(resid_t[:, pl.ds(done, count)], block[:, j : j + CUT])
                done += count
            grad[:, at : at + CUT] = total
    if not pack:
        return

    def read(hop):
        rows = rows_of(me, hop)
        return grad[rows, :] + coef[rows, :].astype(jnp.float32) * target.shape[0]

    for give, hops in zip(gives, GIVE):
        for n, hop in enumerate(hops):
            for k, far in enumerate((0, MIRROR)):
                at = (2 * n + k) * OWN
                give[at : at + OWN, :] = read(hop ^ SIDE ^ far).astype(jnp.bfloat16)
    for n, hop in enumerate(NEAR):
        for k, far in enumerate((0, MIRROR)):
            at = (2 * n + k) * OWN
            keep[at : at + OWN, :] = read(hop ^ far)


def block_mask(where, table, block, reach):
    rows = table.shape[0]
    first = where[0] // PEOPLE * (2 * reach) - reach + block * LANES
    column = lax.broadcasted_iota(jnp.int32, (rows, LANES), 1) + first
    column = column.astype(jnp.float32)
    inside = (column >= table[:, START : START + 1]) & (column < table[:, END : END + 1])
    return jnp.where(inside & (table[:, block : block + 1] > 0), 1.0, 0.0)


def start_kernel(where, active, *refs):
    *vectors, coef_start, by_gene, coef, coef_own, table = refs
    table[...] = jnp.zeros(table.shape, jnp.float32)
    table[: active.shape[0], :] = active[...].astype(jnp.float32)
    for row, vector in zip((START, END, PENALTY, STEP), vectors):
        table[row : row + 1, :] = vector[...].astype(jnp.float32)
    by_gene[...] = table[...].T
    own = rows_of(person(where), 0)
    width = coef.shape[1]
    for block in range(width // LANES):
        cols = slice(block * LANES, (block + 1) * LANES)
        mask = block_mask(where, by_gene[...], block, width // 4)
        coef[:, cols] = (mask * coef_start[:, cols]).astype(jnp.bfloat16)
        mask = block_mask(where, by_gene[own, :], block, width // 4)
        coef_own[:, cols] = mask * coef_start[own, cols]


def update_kernel(total, first, where, by_gene, near, far, coef_own, base, *refs):
    own = rows_of(person(where), 0)
    table = by_gene[own, :]
    width = coef_own.shape[1]
    penalty, step = table[:, PENALTY : PENALTY + 1], table[:, STEP : STEP + 1]
    cut = step * penalty
    lane = lax.broadcasted_iota(jnp.int32, (OWN, LANES), 1)
    high = low = jnp.zeros((OWN, LANES), jnp.float32)
    for block in range(width // LANES):
        cols = slice(block * LANES, (block + 1) * LANES)
        mask = block_mask(where, table, block, width // 4)
        used = base[own, cols] if first else base[:, cols]
        grad = (near[:OWN, cols] + far[:, cols].astype(jnp.float32)) / total - used.astype(jnp.float32)
        moved = coef_own[:, cols] + step * grad
        size = jnp.maximum(jnp.abs(moved) - cut * l1_share, 0.0)
        kept = mask * jnp.where(moved < 0, -size, size) / (1.0 + cut * (1.0 - l1_share))
        if first:
            refs[0][:, cols] = kept
            peak = jnp.max(mask * jnp.abs(grad) / penalty, axis=1, keepdims=True)
            rounded = peak.astype(jnp.bfloat16).astype(jnp.float32)
            high = jnp.where(lane == block, rounded, high)
            low = jnp.where(lane == block + width // LANES, peak - rounded, low)
        refs[-1][:, cols] = kept.astype(jnp.bfloat16)
    if first:
        refs[-1][:, width:] = (high + low).astype(jnp.bfloat16)


def output_kernel(where, *refs):
    *pieces, out = refs

    def put(rows, piece):
        out[rows, :] = piece.astype(jnp.float32)

    place(person(where), pieces, put)


def in_vmem(array):
    return pltpu.with_memory_space_constraint(array, pltpu.VMEM)


def specs(count):
    vmem = pl.BlockSpec(memory_space=pltpu.VMEM)
    return [pl.BlockSpec(memory_space=pltpu.SMEM)] + [vmem] * count


def split(genotypes, reach):
    out, first = [], 0
    for count in PARTS:
        for column in (reach, 0):
            piece = genotypes[first : first + count, column : column + reach]
            piece, genotypes = lax.optimization_barrier((piece, genotypes))
            out.append(in_vmem(piece))
        first += count
    return out


def local_grad(where, chosen, blocks, target, pieces, prior=None, pack=True):
    genes = target.shape[1]
    reach = blocks[0][0].shape[1]
    width = 4 * reach
    parts = [(sum(PARTS[:k]), PARTS[k]) for k in chosen]
    people = sum(count for _, count in parts)
    given = [block for k in chosen for block in blocks[k]]
    operands = [*given, target, *pieces] + ([] if prior is None else [prior])
    operands = [in_vmem(v) for v in operands]
    local = pltpu.VMEM((genes, width), jnp.float32)
    outs, scratch = [], [pltpu.VMEM((genes, people), jnp.bfloat16)]
    if pack:
        outs.append(pltpu.VMEM((2 * OWN * len(NEAR), width), jnp.float32))
        outs += [pltpu.VMEM((2 * OWN * len(hops), width), jnp.bfloat16) for hops in GIVE]
        scratch = [local, *scratch]
    else:
        outs.append(local)
    if len(pieces) > 1:
        outs.append(pltpu.VMEM((width // LANES, genes), jnp.float32))
        scratch.append(pltpu.VMEM((genes, width), jnp.bfloat16))
        scratch.append(pltpu.VMEM((genes, LANES), jnp.bfloat16))
    return pl.pallas_call(
        functools.partial(turn_kernel, parts, len(pieces), prior is not None, pack),
        out_shape=outs,
        in_specs=specs(len(operands)),
        out_specs=[pl.BlockSpec(memory_space=pltpu.VMEM)] * len(outs),
        scratch_shapes=scratch,
        compiler_params=pltpu.CompilerParams(vmem_limit_bytes=20 << 20),
        cost_estimate=pl.CostEstimate(
            flops=4 * people * width * genes, bytes_accessed=0, transcendentals=0
        ),
    )(where, *operands)


def small_call(kernel, where, operands, outs, scratch=()):
    return pl.pallas_call(
        kernel,
        out_shape=[pltpu.VMEM(shape, dtype) for shape, dtype in outs],
        in_specs=specs(len(operands)),
        out_specs=[pl.BlockSpec(memory_space=pltpu.VMEM)] * len(outs),
        scratch_shapes=list(scratch),
        compiler_params=pltpu.CompilerParams(vmem_limit_bytes=8 << 20),
    )(where, *[in_vmem(v) for v in operands])


def swap(block, hop):
    count = lax.axis_size("people")
    return lax.ppermute(block, "people", [(i, i ^ hop) for i in range(count)])


def sum_to_owner(keep, gives):
    part = {}
    for hops, give in zip(GIVE, gives):
        got = swap(give, SIDE)
        for n, hop in enumerate(hops):
            at = NEAR.index(hop) * 2 * OWN
            part[hop] = keep[at : at + 2 * OWN] + got[2 * n * OWN : 2 * (n + 1) * OWN]
    total = part[0]
    for hop in (6, 4, 2):
        total = total + swap(part[hop].astype(jnp.bfloat16), hop)
    return total, swap(total[OWN:].astype(jnp.bfloat16), MIRROR)


def gather_rows(own):
    pair = jnp.concatenate([own, swap(own, MIRROR)], axis=0)
    got = {0: pair}
    for hop in (2, 6, 4):
        got[hop] = swap(pair, hop)
    return [got[hop] for hop in NEAR] + [swap(got[hop], SIDE) for hop in NEAR]


def on_device(
    genotypes, expression, coef_start, penalty, step_size, window_start, window_end, active_blocks
):
    v_local = genotypes.shape[1]
    total = genotypes.shape[0] * lax.axis_size("people")
    genes, width = coef_start.shape
    reach = (width - v_local) // 2
    chain = [(i, i + 1) for i in range(lax.axis_size("genome") - 1)]
    back = [(target, source) for source, target in chain]
    where = lax.axis_index(("genome", "people")).astype(jnp.int32)[None]
    vectors = [v[None] for v in (window_start, window_end, penalty, step_size)]
    by_gene, coef, coef_own = small_call(
        start_kernel,
        where,
        [active_blocks.T, *vectors, coef_start],
        [((genes, LANES), jnp.float32), ((genes, width), jnp.bfloat16), ((OWN, width), jnp.float32)],
        [pltpu.VMEM((LANES, genes), jnp.float32)],
    )

    halves = split(genotypes, reach)
    blocks = []
    for k in range(len(PARTS)):
        right, left = halves[2 * k], halves[2 * k + 1]
        before = (blocks[0][0], blocks[0][3], coef) if k else (where,)
        right, left, *_ = lax.optimization_barrier((right, left, *before))
        low = lax.ppermute(right, "genome", chain)
        high = lax.ppermute(left, "genome", back)
        blocks.append((low, left, right, high))

    (prior,) = local_grad(where, (0,), blocks, expression, [coef], pack=False)
    keep, *gives = local_grad(where, (1,), blocks, expression, [coef], prior)
    near, far = sum_to_owner(keep, gives)
    coef_own, sent = small_call(
        functools.partial(update_kernel, total, True),
        where,
        [by_gene, near, far, coef_own, coef],
        [((OWN, width), jnp.float32), ((OWN, width + LANES), jnp.bfloat16)],
    )
    pieces = gather_rows(sent)

    keep, *gives, peaks = local_grad(where, (0, 1), blocks, expression, pieces)
    near, far = sum_to_owner(keep, gives)
    (last,) = small_call(
        functools.partial(update_kernel, total, False),
        where,
        [by_gene, near, far, coef_own, sent],
        [((OWN, width), jnp.bfloat16)],
    )
    pieces = gather_rows(last)
    coef = pl.pallas_call(
        output_kernel,
        out_shape=jax.ShapeDtypeStruct((genes, width), jnp.float32),
        in_specs=specs(len(pieces)),
        out_specs=pl.BlockSpec(memory_space=pltpu.VMEM),
        compiler_params=pltpu.CompilerParams(vmem_limit_bytes=8 << 20),
    )(where, *[in_vmem(piece) for piece in pieces])
    return (coef, peaks.T)


def solution(mesh):
    return jax.shard_map(
        on_device,
        mesh=mesh,
        in_specs=(
            P("people", "genome"),
            P("people", "genome"),
            P("genome", None),
            P("genome"),
            P("genome"),
            P("genome"),
            P("genome"),
            P("genome", None),
        ),
        out_specs=(P("genome", None), P("genome", None)),
        check_vma=False,
    )
```

time: 191 us -> 186 us (0.974); the launches traced: 189 us -> 182 us
  other arithmetic: 6.37 us -> 0.35 us
  Pallas kernels: 26.2 us -> 21.3 us
  starting transfers between devices: 58.5 us -> 62.7 us
    ppermute x1 -> x2, waiting for transfers between devices: 29 us -> 4.19 us  [on_device(): high = lax.ppermute(left, 'genome', back)]
    ppermute x1 -> x2, waiting for transfers between devices: 3.61 us -> 20.1 us  [on_device(): low = lax.ppermute(right, 'genome', chain)]
    ppermute x1 -> x2, starting transfers between devices: 2.24 us -> 10.5 us  [on_device(): low = lax.ppermute(right, 'genome', chain)]
    ppermute x30, waiting for transfers between devices: 54.9 us -> 63 us  [swap(): return lax.ppermute(block, 'people', [(i, i ^ hop) for i in range(count)])]
    ppermute x30, starting transfers between devices: 54.1 us -> 46.6 us  [swap(): return lax.ppermute(block, 'people', [(i, i ^ hop) for i in range(count)])]
    pallas_call x2 -> x6, Pallas kernels: 24.7 us -> 19.9 us  [the longest x3 16.7 us: local_grad(): pl.pallas_call(functools.partial(turn_kernel, parts, len(pieces), prior i...]
    convert_element_type x4 -> x0, other arithmetic: 3.68 us -> none  [the longest x1 2.36 us: on_device(): coef = (mask * coef_start).astype(jnp.bfloat16)]
    ppermute x1 -> x2, starting transfers between devices: 2.08 us -> 5.56 us  [on_device(): high = lax.ppermute(left, 'genome', back)]
  transfers between devices with their start and end apart: 32 -> 34, of which waited for: 20 -> 25; matrix products, arithmetic and copies ran while one was open for 3% -> 2% of each run, Pallas kernels for 0% -> 4%
where the time goes in v2:
time: 186 us; the launch traced here: 182 us
  waiting for transfers between devices  87.3 us (47%)
  starting transfers between devices  62.7 us (34%)
  Pallas kernels  21.3 us (11%)
  local copies, waits for them, and re-layouts  9.52 us (5%)
    ppermute x30, waiting for transfers between devices, swap(): return lax.ppermute(block, 'people', [(i, i ^ hop) for i in range(count)])  63 us
    ppermute x30, starting transfers between devices, swap(): return lax.ppermute(block, 'people', [(i, i ^ hop) for i in range(count)])  46.6 us
    ppermute x2, waiting for transfers between devices, on_device(): low = lax.ppermute(right, 'genome', chain)  20.1 us
    pallas_call x3, Pallas kernels, local_grad(): pl.pallas_call(functools.partial(turn_kernel, parts, len(pieces), prior i...  16.7 us
    ppermute x2, starting transfers between devices, on_device(): low = lax.ppermute(right, 'genome', chain)  10.5 us
    slice x4, local copies, waits for them, and re-layouts, split(): piece = genotypes[first:first + count, column:column + reach]  7.44 us
    ppermute x2, starting transfers between devices, on_device(): high = lax.ppermute(left, 'genome', back)  5.56 us
    ppermute x2, waiting for transfers between devices, on_device(): high = lax.ppermute(left, 'genome', back)  4.19 us
  transfers between devices with their start and end apart: 34, of which 25 were waited for; matrix products, arithmetic and copies ran while one was open for 2% of the time, Pallas kernels for 4%

profile of v2, /device:TPU:56, one launch (start us, length us, event | category | flops | bytes accessed | tf_op | source)
XLA Modules:
  0.0 182.2 jit_solution(1396637851361943328)
XLA Ops:
  0.6 1.8 slice.56.refs_3_
  2.5 3.2 %slice.57.refs_2_ = bf16[2304,512]{1,0:T(8,128)(2,1)} slice(bf16[3072,1024]{1,0:T(8,128)(2,1)} %param.8), slice={[0:2304], [0:512]} | slice | bytes 4718592 | tf_op jit(solution)/shard_map/slice | solution.py:192
  5.8 2.2 %collective-permute-start = (bf16[2304,512]{1,0:T(8,128)(2,1)S(1)}, bf16[2304,512]{1,0:T(8,128)(2,1)S(1)}, u32[]{:S(2)}, u32[]{:S(2)}) collective-permute-start(bf16[2304,512]{1,0:T(8,128)(2,1)S(1)} %slice.56.refs_3_), channel_id=1, source_target_pairs={{0,16},{16,32},{32,48},{48,64},{64,80},{80,96},{96,112},{112,128},... | collective-permute-start | bytes 7077896 | tf_op jit(solution)/shard_map/ppermute | solution.py:295
  7.9 3.6 %collective-permute-start.1 = (bf16[2304,512]{1,0:T(8,128)(2,1)}, bf16[2304,512]{1,0:T(8,128)(2,1)S(1)}, u32[]{:S(2)}, u32[]{:S(2)}) collective-permute-start(bf16[2304,512]{1,0:T(8,128)(2,1)} %slice.57.refs_2_), channel_id=1, source_target_pairs={{16,0},{32,16},{48,32},{64,48},{80,64},{96,80},{112,96},{128,112},... | collective-permute-start | bytes 7077896 | tf_op jit(solution)/shard_map/ppermute | solution.py:296
  11.6 1.2 slice.58.refs_3_.refs_7_
  12.8 1.2 slice.59.refs_2_.refs_6_
  14.0 2.0 %shard_map.95 = (f32[256,128]{1,0:T(8,128)S(1)}, bf16[256,2048]{1,0:T(8,128)(2,1)S(1)}, f32[16,2048]{1,0:T(8,128)S(1)}) custom-call(s32[1]{0:T(128)} %bitcast.where.refs_0_, s32[16,256]{1,0:T(8,128)S(1)} %bitcast.8, s32[1,256]{1,0:T(1,128)S(1)} %bitcast.9, s32[1,256]{1,0:T(1,128)S(1)} %bitcast.10, f32[1,256]{1,0:T(1,128)S(1)} %bitcast.11, ...), custom_call_target="tpu_custom_call" | custom-call | tf_op jit(solution)/shard_map/pallas_call | solution.py:234
  16.1 20.1 %collective-permute-done.refs_1_ = bf16[2304,512]{1,0:T(8,128)(2,1)S(1)} collective-permute-done((bf16[2304,512]{1,0:T(8,128)(2,1)S(1)}, bf16[2304,512]{1,0:T(8,128)(2,1)S(1)}, u32[]{:S(2)}, u32[]{:S(2)}) %collective-permute-start) | collective-permute-done | bytes 2359328 | tf_op jit(solution)/shard_map/ppermute | solution.py:295
  36.2 2.1 %collective-permute-done.1.refs_4_ = bf16[2304,512]{1,0:T(8,128)(2,1)S(1)} collective-permute-done((bf16[2304,512]{1,0:T(8,128)(2,1)}, bf16[2304,512]{1,0:T(8,128)(2,1)S(1)}, u32[]{:S(2)}, u32[]{:S(2)}) %collective-permute-start.1) | collective-permute-done | bytes 2359328 | tf_op jit(solution)/shard_map/ppermute | solution.py:296
  38.3 8.4 %collective-permute-start.2 = (bf16[768,512]{1,0:T(8,128)(2,1)S(1)}, bf16[768,512]{1,0:T(8,128)(2,1)S(1)}, u32[]{:S(2)}, u32[]{:S(2)}) collective-permute-start(bf16[768,512]{1,0:T(8,128)(2,1)S(1)} %slice.58.refs_3_.refs_7_), channel_id=1, source_target_pairs={{0,16},{16,32},{32,48},{48,64},{64,80},{80,96},{96,112},{112,128},... | collective-permute-start | bytes 2359304 | tf_op jit(solution)/shard_map/ppermute | solution.py:295
  46.6 1.9 %collective-permute-start.3 = (bf16[768,512]{1,0:T(8,128)(2,1)S(1)}, bf16[768,512]{1,0:T(8,128)(2,1)S(1)}, u32[]{:S(2)}, u32[]{:S(2)}) collective-permute-start(bf16[768,512]{1,0:T(8,128)(2,1)S(1)} %slice.59.refs_2_.refs_6_), channel_id=1, source_target_pairs={{16,0},{32,16},{48,32},{64,48},{80,64},{96,80},{112,96},{128,112},... | collective-permute-start | bytes 2359304 | tf_op jit(solution)/shard_map/ppermute | solution.py:296
  48.6 1.4 copy-done.2
  50.0 5.9 %shard_map.96.refs_7_ = f32[256,2048]{1,0:T(8,128)S(1)} custom-call(s32[1]{0:T(128)} %bitcast.where.refs_0_, bf16[2304,512]{1,0:T(8,128)(2,1)S(1)} %collective-permute-done.refs_1_, bf16[2304,512]{1,0:T(8,128)(2,1)S(1)} %copy-done, bf16[2304,512]{1,0:T(8,128)(2,1)S(1)} %slice.56.refs_3_, bf16[2304,512]{1,0:T(8,128)(2,1)S(1)} %collective-permute-done.1.refs_4_, ...), custom_call_target="tpu_custom_call" | custom-call | flops 4831838208 | tf_op jit(solution)/shard_map/pallas_call | solution.py:220
  55.9 2.1 %collective-permute-done.3.refs_4_.refs_8_ = bf16[768,512]{1,0:T(8,128)(2,1)S(1)} collective-permute-done((bf16[768,512]{1,0:T(8,128)(2,1)S(1)}, bf16[768,512]{1,0:T(8,128)(2,1)S(1)}, u32[]{:S(2)}, u32[]{:S(2)}) %collective-permute-start.3) | collective-permute-done | bytes 786464 | tf_op jit(solution)/shard_map/ppermute | solution.py:296
  58.0 3.7 %shard_map.97 = (f32[128,2048]{1,0:T(8,128)S(1)}, bf16[32,2048]{1,0:T(8,128)(2,1)S(1)}, bf16[64,2048]{1,0:T(8,128)(2,1)S(1)}, bf16[32,2048]{1,0:T(8,128)(2,1)S(1)}) custom-call(s32[1]{0:T(128)} %bitcast.where.refs_0_, bf16[768,512]{1,0:T(8,128)(2,1)S(1)} %collective-permute-done.2.refs_1_.refs_5_, bf16[768,512]{1,0:T(8,128)(2,1)S(1)} %slice.59.refs_2_.refs_6_, ...), custom_call_target="tpu_custom_call" | custom-call | flops 1610612736 | tf_op jit(solution)/shard_map/pallas_call | solution.py:220
  61.8 0.7 collective-permute-start.7
  62.5 1.4 collective-permute-start.5
  64.5 5.2 %collective-permute-done.5 = bf16[32,2048]{1,0:T(8,128)(2,1)S(1)} collective-permute-done((bf16[32,2048]{1,0:T(8,128)(2,1)S(1)}, bf16[32,2048]{1,0:T(8,128)(2,1)S(1)}, u32[]{:S(2)}, u32[]{:S(2)}) %collective-permute-start.5) | collective-permute-done | bytes 131104 | tf_op jit(solution)/shard_map/ppermute | solution.py:246
  69.7 3.4 %collective-permute-start.8 = (bf16[32,2048]{1,0:T(8,128)(2,1)S(1)}, bf16[32,2048]{1,0:T(8,128)(2,1)S(1)}, u32[]{:S(2)}, u32[]{:S(2)}) collective-permute-start(bf16[32,2048]{1,0:T(8,128)(2,1)S(1)} %get-tuple-element.54), channel_id=1, source_target_pairs={{0,4},{1,5},{2,6},{3,7},{4,0},{5,1},{6,2},{7,3},{8,12},{9,13},{10,... | collective-permute-start | bytes 393224 | tf_op jit(solution)/shard_map/ppermute | solution.py:246
  73.2 0.7 collective-permute-start.6
  74.0 2.6 %collective-permute-done.8 = bf16[32,2048]{1,0:T(8,128)(2,1)S(1)} collective-permute-done((bf16[32,2048]{1,0:T(8,128)(2,1)S(1)}, bf16[32,2048]{1,0:T(8,128)(2,1)S(1)}, u32[]{:S(2)}, u32[]{:S(2)}) %collective-permute-start.8) | collective-permute-done | bytes 131104 | tf_op jit(solution)/shard_map/ppermute | solution.py:246
  76.5 1.5 collective-permute-done.9
  78.1 3.4 %collective-permute-done.6 = bf16[32,2048]{1,0:T(8,128)(2,1)S(1)} collective-permute-done((bf16[32,2048]{1,0:T(8,128)(2,1)S(1)}, bf16[32,2048]{1,0:T(8,128)(2,1)S(1)}, u32[]{:S(2)}, u32[]{:S(2)}) %collective-permute-start.6) | collective-permute-done | bytes 131104 | tf_op jit(solution)/shard_map/ppermute | solution.py:246
  81.6 6.0 %collective-permute-start.10 = (bf16[16,2048]{1,0:T(8,128)(2,1)S(1)}, bf16[16,2048]{1,0:T(8,128)(2,1)S(1)}, u32[]{:S(2)}, u32[]{:S(2)}) collective-permute-start(bf16[16,2048]{1,0:T(8,128)(2,1)S(1)} %slice.95), channel_id=1, source_target_pairs={{0,14},{1,15},{2,12},{3,13},{4,10},{5,11},{6,8},{7,9},{8,6},{9,7},... | collective-permute-start | bytes 196616 | tf_op jit(solution)/shard_map/ppermute | solution.py:246
  87.6 2.2 %collective-permute-done.10.far = bf16[16,2048]{1,0:T(8,128)(2,1)S(1)} collective-permute-done((bf16[16,2048]{1,0:T(8,128)(2,1)S(1)}, bf16[16,2048]{1,0:T(8,128)(2,1)S(1)}, u32[]{:S(2)}, u32[]{:S(2)}) %collective-permute-start.10) | collective-permute-done | bytes 65568 | tf_op jit(solution)/shard_map/ppermute | solution.py:246
  89.8 1.0 shard_map.98
  90.8 5.1 %collective-permute-start.11 = (bf16[16,2176]{1,0:T(8,128)(2,1)S(1)}, bf16[16,2176]{1,0:T(8,128)(2,1)S(1)}, u32[]{:S(2)}, u32[]{:S(2)}) collective-permute-start(bf16[16,2176]{1,0:T(8,128)(2,1)S(1)} %get-tuple-element.45.base), channel_id=1, source_target_pairs={{0,14},{1,15},{2,12},{3,13},{4,10},{5,11},{6,8},{7,9},{8,6},{9,7},... | collective-permute-start | bytes 208904 | tf_op jit(solution)/shard_map/ppermute | solution.py:246
  96.0 2.3 %collective-permute-done.11 = bf16[16,2176]{1,0:T(8,128)(2,1)S(1)} collective-permute-done((bf16[16,2176]{1,0:T(8,128)(2,1)S(1)}, bf16[16,2176]{1,0:T(8,128)(2,1)S(1)}, u32[]{:S(2)}, u32[]{:S(2)}) %collective-permute-start.11) | collective-permute-done | bytes 69664 | tf_op jit(solution)/shard_map/ppermute | solution.py:246
  98.3 1.6 collective-permute-start.14
  99.9 2.0 %collective-permute-start.12 = (bf16[32,2176]{1,0:T(8,128)(2,1)S(1)}, bf16[32,2176]{1,0:T(8,128)(2,1)S(1)}, u32[]{:S(2)}, u32[]{:S(2)}) collective-permute-start(bf16[32,2176]{1,0:T(8,128)(2,1)S(1)} %constant_dynamic-update-slice_fusion.refs_10_), channel_id=1, source_target_pairs={{0,2},{1,3},{2,0},{3,1},{4,6},{5,7},{6,4},{7,5},{8,10},{9,11},{10,... | collective-permute-start | bytes 417800 | tf_op jit(solution)/shard_map/ppermute | solution.py:246
  101.9 0.6 collective-permute-start.15
  102.5 6.4 %collective-permute-done.14.refs_13_ = bf16[32,2176]{1,0:T(8,128)(2,1)S(1)} collective-permute-done((bf16[32,2176]{1,0:T(8,128)(2,1)S(1)}, bf16[32,2176]{1,0:T(8,128)(2,1)S(1)}, u32[]{:S(2)}, u32[]{:S(2)}) %collective-permute-start.14) | collective-permute-done | bytes 139296 | tf_op jit(solution)/shard_map/ppermute | solution.py:246
  108.9 0.6 collective-permute-start.18
  109.9 1.0 collective-permute-start.17
  110.9 1.0 collective-permute-start.16
  112.0 3.5 %collective-permute-done.18.refs_17_ = bf16[32,2176]{1,0:T(8,128)(2,1)S(1)} collective-permute-done((bf16[32,2176]{1,0:T(8,128)(2,1)S(1)}, bf16[32,2176]{1,0:T(8,128)(2,1)S(1)}, u32[]{:S(2)}, u32[]{:S(2)}) %collective-permute-start.18) | collective-permute-done | bytes 139296 | tf_op jit(solution)/shard_map/ppermute | solution.py:246
  115.4 3.0 %collective-permute-done.17.refs_16_ = bf16[32,2176]{1,0:T(8,128)(2,1)S(1)} collective-permute-done((bf16[32,2176]{1,0:T(8,128)(2,1)S(1)}, bf16[32,2176]{1,0:T(8,128)(2,1)S(1)}, u32[]{:S(2)}, u32[]{:S(2)}) %collective-permute-start.17) | collective-permute-done | bytes 139296 | tf_op jit(solution)/shard_map/ppermute | solution.py:246
  118.4 2.2 %collective-permute-done.16.refs_15_ = bf16[32,2176]{1,0:T(8,128)(2,1)S(1)} collective-permute-done((bf16[32,2176]{1,0:T(8,128)(2,1)S(1)}, bf16[32,2176]{1,0:T(8,128)(2,1)S(1)}, u32[]{:S(2)}, u32[]{:S(2)}) %collective-permute-start.16) | collective-permute-done | bytes 139296 | tf_op jit(solution)/shard_map/ppermute | solution.py:246
  120.6 7.0 %shard_map.99 = (f32[128,2048]{1,0:T(8,128)S(1)}, bf16[32,2048]{1,0:T(8,128)(2,1)S(1)}, bf16[64,2048]{1,0:T(8,128)(2,1)S(1)}, bf16[32,2048]{1,0:T(8,128)(2,1)S(1)}, f32[16,256]{1,0:T(8,128)S(1)}) custom-call(s32[1]{0:T(128)} %bitcast.where.refs_0_, bf16[2304,512]{1,0:T(8,128)(2,1)S(1)} %collective-permute-done.refs_1_, bf16[2304,512]{1,0:T(8,128)(2,1)S(1)} %copy-done, ...), custom_call_target="tpu_custom_call" | custom-call | flops 6442450944 | tf_op jit(solution)/shard_map/pallas_call | solution.py:220
  127.7 0.7 collective-permute-start.22
  128.4 1.4 collective-permute-start.20
  130.4 9.2 %collective-permute-done.20 = bf16[32,2048]{1,0:T(8,128)(2,1)S(1)} collective-permute-done((bf16[32,2048]{1,0:T(8,128)(2,1)S(1)}, bf16[32,2048]{1,0:T(8,128)(2,1)S(1)}, u32[]{:S(2)}, u32[]{:S(2)}) %collective-permute-start.20) | collective-permute-done | bytes 131104 | tf_op jit(solution)/shard_map/ppermute | solution.py:246
  139.7 1.6 collective-permute-start.23
  141.2 0.7 collective-permute-start.24
  141.9 1.6 collective-permute-start.21
  143.5 4.7 %collective-permute-done.23 = bf16[32,2048]{1,0:T(8,128)(2,1)S(1)} collective-permute-done((bf16[32,2048]{1,0:T(8,128)(2,1)S(1)}, bf16[32,2048]{1,0:T(8,128)(2,1)S(1)}, u32[]{:S(2)}, u32[]{:S(2)}) %collective-permute-start.23) | collective-permute-done | bytes 131104 | tf_op jit(solution)/shard_map/ppermute | solution.py:246
  148.2 3.3 %collective-permute-done.21 = bf16[32,2048]{1,0:T(8,128)(2,1)S(1)} collective-permute-done((bf16[32,2048]{1,0:T(8,128)(2,1)S(1)}, bf16[32,2048]{1,0:T(8,128)(2,1)S(1)}, u32[]{:S(2)}, u32[]{:S(2)}) %collective-permute-start.21) | collective-permute-done | bytes 131104 | tf_op jit(solution)/shard_map/ppermute | solution.py:246
  151.6 4.2 %collective-permute-start.25 = (bf16[16,2048]{1,0:T(8,128)(2,1)S(1)}, bf16[16,2048]{1,0:T(8,128)(2,1)S(1)}, u32[]{:S(2)}, u32[]{:S(2)}) collective-permute-start(bf16[16,2048]{1,0:T(8,128)(2,1)S(1)} %slice.94), channel_id=1, source_target_pairs={{0,14},{1,15},{2,12},{3,13},{4,10},{5,11},{6,8},{7,9},{8,6},{9,7},... | collective-permute-start | bytes 196616 | tf_op jit(solution)/shard_map/ppermute | solution.py:246
  155.8 3.1 %collective-permute-done.25.far = bf16[16,2048]{1,0:T(8,128)(2,1)S(1)} collective-permute-done((bf16[16,2048]{1,0:T(8,128)(2,1)S(1)}, bf16[16,2048]{1,0:T(8,128)(2,1)S(1)}, u32[]{:S(2)}, u32[]{:S(2)}) %collective-permute-start.25) | collective-permute-done | bytes 65568 | tf_op jit(solution)/shard_map/ppermute | solution.py:246
  159.1 4.2 %collective-permute-start.26 = (bf16[16,2048]{1,0:T(8,128)(2,1)S(1)}, bf16[16,2048]{1,0:T(8,128)(2,1)S(1)}, u32[]{:S(2)}, u32[]{:S(2)}) collective-permute-start(bf16[16,2048]{1,0:T(8,128)(2,1)S(1)} %shard_map.100), channel_id=1, source_target_pairs={{0,14},{1,15},{2,12},{3,13},{4,10},{5,11},{6,8},{7,9},{8,6},{9,7},... | collective-permute-start | bytes 196616 | tf_op jit(solution)/shard_map/ppermute | solution.py:246
  163.4 3.5 %collective-permute-done.26 = bf16[16,2048]{1,0:T(8,128)(2,1)S(1)} collective-permute-done((bf16[16,2048]{1,0:T(8,128)(2,1)S(1)}, bf16[16,2048]{1,0:T(8,128)(2,1)S(1)}, u32[]{:S(2)}, u32[]{:S(2)}) %collective-permute-start.26) | collective-permute-done | bytes 65568 | tf_op jit(solution)/shard_map/ppermute | solution.py:246
  166.8 1.3 collective-permute-start.29
  168.1 2.3 %collective-permute-start.27 = (bf16[32,2048]{1,0:T(8,128)(2,1)S(1)}, bf16[32,2048]{1,0:T(8,128)(2,1)S(1)}, u32[]{:S(2)}, u32[]{:S(2)}) collective-permute-start(bf16[32,2048]{1,0:T(8,128)(2,1)S(1)} %pad_maximum_fusion.refs_0_), channel_id=1, source_target_pairs={{0,2},{1,3},{2,0},{3,1},{4,6},{5,7},{6,4},{7,5},{8,10},{9,11},{10,... | collective-permute-start | bytes 393224 | tf_op jit(solution)/shard_map/ppermute | solution.py:246
  170.4 0.7 collective-permute-start.30
  171.1 0.9 collective-permute-done.29.refs_3_
  172.0 0.6 collective-permute-start.33
  172.6 1.5 collective-permute-done.28.refs_2_
  174.1 0.7 collective-permute-start.32
  174.8 1.3 collective-permute-start.31
  176.1 0.6 copy.11
  176.7 1.2 collective-permute-done.33.refs_7_
  177.9 1.4 collective-permute-done.32.refs_6_
  179.3 1.4 collective-permute-done.31.refs_5_
  180.7 1.5 shard_map.101
  (43 shorter events, 2.4 us)
Async XLA Ops:
  5.7 8.3 %copy-start.4 = (s32[256,16]{0,1:T(8,128)S(1)}, s32[256,16]{0,1:T(8,128)}, u32[]{:S(2)}) copy-start(s32[256,16]{0,1:T(8,128)} %param.15) | copy-start | bytes 49156
  5.7 8.3 %copy-start.5 = (s32[256]{0:T(256)S(1)}, s32[256]{0:T(256)}, u32[]{:S(2)}) copy-start(s32[256]{0:T(256)} %param.13) | copy-start | bytes 3076
  5.7 8.3 %copy-start.6 = (s32[256]{0:T(256)S(1)}, s32[256]{0:T(256)}, u32[]{:S(2)}) copy-start(s32[256]{0:T(256)} %param.14) | copy-start | bytes 3076
  5.7 8.3 %copy-start.7 = (f32[256]{0:T(256)S(1)}, f32[256]{0:T(256)}, u32[]{:S(2)}) copy-start(f32[256]{0:T(256)} %param.11) | copy-start | bytes 3076
  5.7 8.3 %copy-start.8 = (f32[256]{0:T(256)S(1)}, f32[256]{0:T(256)}, u32[]{:S(2)}) copy-start(f32[256]{0:T(256)} %param.12) | copy-start | bytes 3076
  5.7 8.3 %copy-start.1 = (f32[256,2048]{1,0:T(8,128)S(1)}, f32[256,2048]{1,0:T(8,128)}, u32[]{:S(2)}) copy-start(f32[256,2048]{1,0:T(8,128)} %refs_4_.1) | copy-start | bytes 6291460
  5.7 42.8 %copy-start = (bf16[2304,512]{1,0:T(8,128)(2,1)S(1)}, bf16[2304,512]{1,0:T(8,128)(2,1)}, u32[]{:S(2)}) copy-start(bf16[2304,512]{1,0:T(8,128)(2,1)} %slice.57.refs_2_) | copy-start | bytes 7077892
  5.8 30.4 %collective-permute-start = (bf16[2304,512]{1,0:T(8,128)(2,1)S(1)}, bf16[2304,512]{1,0:T(8,128)(2,1)S(1)}, u32[]{:S(2)}, u32[]{:S(2)}) collective-permute-start(bf16[2304,512]{1,0:T(8,128)(2,1)S(1)} %slice.56.refs_3_), channel_id=1, source_target_pairs={{0,16},{16,32},{32,48},{48,64},{64,80},{80,96},{96,112},{112,128},... | collective-permute-start | bytes 7077896 | tf_op jit(solution)/shard_map/ppermute | solution.py:295
  7.9 30.3 %collective-permute-start.1 = (bf16[2304,512]{1,0:T(8,128)(2,1)}, bf16[2304,512]{1,0:T(8,128)(2,1)S(1)}, u32[]{:S(2)}, u32[]{:S(2)}) collective-permute-start(bf16[2304,512]{1,0:T(8,128)(2,1)} %slice.57.refs_2_), channel_id=1, source_target_pairs={{16,0},{32,16},{48,32},{64,48},{80,64},{96,80},{112,96},{128,112},... | collective-permute-start | bytes 7077896 | tf_op jit(solution)/shard_map/ppermute | solution.py:296
  38.3 17.7 %collective-permute-start.2 = (bf16[768,512]{1,0:T(8,128)(2,1)S(1)}, bf16[768,512]{1,0:T(8,128)(2,1)S(1)}, u32[]{:S(2)}, u32[]{:S(2)}) collective-permute-start(bf16[768,512]{1,0:T(8,128)(2,1)S(1)} %slice.58.refs_3_.refs_7_), channel_id=1, source_target_pairs={{0,16},{16,32},{32,48},{48,64},{64,80},{80,96},{96,112},{112,128},... | collective-permute-start | bytes 2359304 | tf_op jit(solution)/shard_map/ppermute | solution.py:295
  46.6 11.4 %collective-permute-start.3 = (bf16[768,512]{1,0:T(8,128)(2,1)S(1)}, bf16[768,512]{1,0:T(8,128)(2,1)S(1)}, u32[]{:S(2)}, u32[]{:S(2)}) collective-permute-start(bf16[768,512]{1,0:T(8,128)(2,1)S(1)} %slice.59.refs_2_.refs_6_), channel_id=1, source_target_pairs={{16,0},{32,16},{48,32},{64,48},{80,64},{96,80},{112,96},{128,112},... | collective-permute-start | bytes 2359304 | tf_op jit(solution)/shard_map/ppermute | solution.py:296
  48.6 1.4 copy-start.2
  61.8 58.9 %copy-start.3 = (bf16[3072,256]{1,0:T(8,128)(2,1)S(1)}, bf16[3072,256]{1,0:T(8,128)(2,1)}, u32[]{:S(2)}) copy-start(bf16[3072,256]{1,0:T(8,128)(2,1)} %refs_9_.1) | copy-start | bytes 4718596
  61.8 7.9 %collective-permute-start.7 = (bf16[64,2048]{1,0:T(8,128)(2,1)S(1)}, bf16[64,2048]{1,0:T(8,128)(2,1)S(1)}, u32[]{:S(2)}, u32[]{:S(2)}) collective-permute-start(bf16[64,2048]{1,0:T(8,128)(2,1)S(1)} %get-tuple-element.43), channel_id=1, source_target_pairs={{0,1},{1,0},{2,3},{3,2},{4,5},{5,4},{6,7},{7,6},{8,9},{9,8},{10,11... | collective-permute-start | bytes 786440 | tf_op jit(solution)/shard_map/ppermute | solution.py:246
  62.5 7.2 %collective-permute-start.5 = (bf16[32,2048]{1,0:T(8,128)(2,1)S(1)}, bf16[32,2048]{1,0:T(8,128)(2,1)S(1)}, u32[]{:S(2)}, u32[]{:S(2)}) collective-permute-start(bf16[32,2048]{1,0:T(8,128)(2,1)S(1)} %get-tuple-element.42), channel_id=1, source_target_pairs={{0,1},{1,0},{2,3},{3,2},{4,5},{5,4},{6,7},{7,6},{8,9},{9,8},{10,11... | collective-permute-start | bytes 393224 | tf_op jit(solution)/shard_map/ppermute | solution.py:246
  63.9 10.1 %collective-permute-start.4 = (bf16[32,2048]{1,0:T(8,128)(2,1)S(1)}, bf16[32,2048]{1,0:T(8,128)(2,1)S(1)}, u32[]{:S(2)}, u32[]{:S(2)}) collective-permute-start(bf16[32,2048]{1,0:T(8,128)(2,1)S(1)} %get-tuple-element.41), channel_id=1, source_target_pairs={{0,1},{1,0},{2,3},{3,2},{4,5},{5,4},{6,7},{7,6},{8,9},{9,8},{10,11... | collective-permute-start | bytes 393224 | tf_op jit(solution)/shard_map/ppermute | solution.py:246
  69.7 6.8 %collective-permute-start.8 = (bf16[32,2048]{1,0:T(8,128)(2,1)S(1)}, bf16[32,2048]{1,0:T(8,128)(2,1)S(1)}, u32[]{:S(2)}, u32[]{:S(2)}) collective-permute-start(bf16[32,2048]{1,0:T(8,128)(2,1)S(1)} %get-tuple-element.54), channel_id=1, source_target_pairs={{0,4},{1,5},{2,6},{3,7},{4,0},{5,1},{6,2},{7,3},{8,12},{9,13},{10,... | collective-permute-start | bytes 393224 | tf_op jit(solution)/shard_map/ppermute | solution.py:246
  73.1 5.0 %collective-permute-start.9 = (bf16[32,2048]{1,0:T(8,128)(2,1)S(1)}, bf16[32,2048]{1,0:T(8,128)(2,1)S(1)}, u32[]{:S(2)}, u32[]{:S(2)}) collective-permute-start(bf16[32,2048]{1,0:T(8,128)(2,1)S(1)} %get-tuple-element.55), channel_id=1, source_target_pairs={{0,2},{1,3},{2,0},{3,1},{4,6},{5,7},{6,4},{7,5},{8,10},{9,11},{10,... | collective-permute-start | bytes 393224 | tf_op jit(solution)/shard_map/ppermute | solution.py:246
  73.2 8.3 %collective-permute-start.6 = (bf16[32,2048]{1,0:T(8,128)(2,1)S(1)}, bf16[32,2048]{1,0:T(8,128)(2,1)S(1)}, u32[]{:S(2)}, u32[]{:S(2)}) collective-permute-start(bf16[32,2048]{1,0:T(8,128)(2,1)S(1)} %get-tuple-element.57), channel_id=1, source_target_pairs={{0,6},{1,7},{2,4},{3,5},{4,2},{5,3},{6,0},{7,1},{8,14},{9,15},{10,... | collective-permute-start | bytes 393224 | tf_op jit(solution)/shard_map/ppermute | solution.py:246
  81.6 8.3 %collective-permute-start.10 = (bf16[16,2048]{1,0:T(8,128)(2,1)S(1)}, bf16[16,2048]{1,0:T(8,128)(2,1)S(1)}, u32[]{:S(2)}, u32[]{:S(2)}) collective-permute-start(bf16[16,2048]{1,0:T(8,128)(2,1)S(1)} %slice.95), channel_id=1, source_target_pairs={{0,14},{1,15},{2,12},{3,13},{4,10},{5,11},{6,8},{7,9},{8,6},{9,7},... | collective-permute-start | bytes 196616 | tf_op jit(solution)/shard_map/ppermute | solution.py:246
  90.8 7.5 %collective-permute-start.11 = (bf16[16,2176]{1,0:T(8,128)(2,1)S(1)}, bf16[16,2176]{1,0:T(8,128)(2,1)S(1)}, u32[]{:S(2)}, u32[]{:S(2)}) collective-permute-start(bf16[16,2176]{1,0:T(8,128)(2,1)S(1)} %get-tuple-element.45.base), channel_id=1, source_target_pairs={{0,14},{1,15},{2,12},{3,13},{4,10},{5,11},{6,8},{7,9},{8,6},{9,7},... | collective-permute-start | bytes 208904 | tf_op jit(solution)/shard_map/ppermute | solution.py:246
  98.3 10.6 %collective-permute-start.14 = (bf16[32,2176]{1,0:T(8,128)(2,1)S(1)}, bf16[32,2176]{1,0:T(8,128)(2,1)S(1)}, u32[]{:S(2)}, u32[]{:S(2)}) collective-permute-start(bf16[32,2176]{1,0:T(8,128)(2,1)S(1)} %constant_dynamic-update-slice_fusion.refs_10_), channel_id=1, source_target_pairs={{0,6},{1,7},{2,4},{3,5},{4,2},{5,3},{6,0},{7,1},{8,14},{9,15},{10,... | collective-permute-start | bytes 417800 | tf_op jit(solution)/shard_map/ppermute | solution.py:246
  99.9 10.0 %collective-permute-start.13 = (bf16[32,2176]{1,0:T(8,128)(2,1)S(1)}, bf16[32,2176]{1,0:T(8,128)(2,1)S(1)}, u32[]{:S(2)}, u32[]{:S(2)}) collective-permute-start(bf16[32,2176]{1,0:T(8,128)(2,1)S(1)} %constant_dynamic-update-slice_fusion.refs_10_), channel_id=1, source_target_pairs={{0,4},{1,5},{2,6},{3,7},{4,0},{5,1},{6,2},{7,3},{8,12},{9,13},{10,... | collective-permute-start | bytes 417800 | tf_op jit(solution)/shard_map/ppermute | solution.py:246
  99.9 11.0 %collective-permute-start.12 = (bf16[32,2176]{1,0:T(8,128)(2,1)S(1)}, bf16[32,2176]{1,0:T(8,128)(2,1)S(1)}, u32[]{:S(2)}, u32[]{:S(2)}) collective-permute-start(bf16[32,2176]{1,0:T(8,128)(2,1)S(1)} %constant_dynamic-update-slice_fusion.refs_10_), channel_id=1, source_target_pairs={{0,2},{1,3},{2,0},{3,1},{4,6},{5,7},{6,4},{7,5},{8,10},{9,11},{10,... | collective-permute-start | bytes 417800 | tf_op jit(solution)/shard_map/ppermute | solution.py:246
  101.9 10.1 %collective-permute-start.15 = (bf16[32,2176]{1,0:T(8,128)(2,1)S(1)}, bf16[32,2176]{1,0:T(8,128)(2,1)S(1)}, u32[]{:S(2)}, u32[]{:S(2)}) collective-permute-start(bf16[32,2176]{1,0:T(8,128)(2,1)S(1)} %constant_dynamic-update-slice_fusion.refs_10_), channel_id=1, source_target_pairs={{0,1},{1,0},{2,3},{3,2},{4,5},{5,4},{6,7},{7,6},{8,9},{9,8},{10,11... | collective-permute-start | bytes 417800 | tf_op jit(solution)/shard_map/ppermute | solution.py:246
  108.9 6.5 %collective-permute-start.18 = (bf16[32,2176]{1,0:T(8,128)(2,1)S(1)}, bf16[32,2176]{1,0:T(8,128)(2,1)S(1)}, u32[]{:S(2)}, u32[]{:S(2)}) collective-permute-start(bf16[32,2176]{1,0:T(8,128)(2,1)S(1)} %collective-permute-done.14.refs_13_), channel_id=1, source_target_pairs={{0,1},{1,0},{2,3},{3,2},{4,5},{5,4},{6,7},{7,6},{8,9},{9,8},{10,11... | collective-permute-start | bytes 417800 | tf_op jit(solution)/shard_map/ppermute | solution.py:246
  109.9 8.5 %collective-permute-start.17 = (bf16[32,2176]{1,0:T(8,128)(2,1)S(1)}, bf16[32,2176]{1,0:T(8,128)(2,1)S(1)}, u32[]{:S(2)}, u32[]{:S(2)}) collective-permute-start(bf16[32,2176]{1,0:T(8,128)(2,1)S(1)} %collective-permute-done.13.refs_12_), channel_id=1, source_target_pairs={{0,1},{1,0},{2,3},{3,2},{4,5},{5,4},{6,7},{7,6},{8,9},{9,8},{10,11... | collective-permute-start | bytes 417800 | tf_op jit(solution)/shard_map/ppermute | solution.py:246
  110.9 9.7 %collective-permute-start.16 = (bf16[32,2176]{1,0:T(8,128)(2,1)S(1)}, bf16[32,2176]{1,0:T(8,128)(2,1)S(1)}, u32[]{:S(2)}, u32[]{:S(2)}) collective-permute-start(bf16[32,2176]{1,0:T(8,128)(2,1)S(1)} %collective-permute-done.12.refs_11_), channel_id=1, source_target_pairs={{0,1},{1,0},{2,3},{3,2},{4,5},{5,4},{6,7},{7,6},{8,9},{9,8},{10,11... | collective-permute-start | bytes 417800 | tf_op jit(solution)/shard_map/ppermute | solution.py:246
  127.7 11.9 %collective-permute-start.22 = (bf16[64,2048]{1,0:T(8,128)(2,1)S(1)}, bf16[64,2048]{1,0:T(8,128)(2,1)S(1)}, u32[]{:S(2)}, u32[]{:S(2)}) collective-permute-start(bf16[64,2048]{1,0:T(8,128)(2,1)S(1)} %get-tuple-element.49), channel_id=1, source_target_pairs={{0,1},{1,0},{2,3},{3,2},{4,5},{5,4},{6,7},{7,6},{8,9},{9,8},{10,11... | collective-permute-start | bytes 786440 | tf_op jit(solution)/shard_map/ppermute | solution.py:246
  128.4 11.2 %collective-permute-start.20 = (bf16[32,2048]{1,0:T(8,128)(2,1)S(1)}, bf16[32,2048]{1,0:T(8,128)(2,1)S(1)}, u32[]{:S(2)}, u32[]{:S(2)}) collective-permute-start(bf16[32,2048]{1,0:T(8,128)(2,1)S(1)} %get-tuple-element.48), channel_id=1, source_target_pairs={{0,1},{1,0},{2,3},{3,2},{4,5},{5,4},{6,7},{7,6},{8,9},{9,8},{10,11... | collective-permute-start | bytes 393224 | tf_op jit(solution)/shard_map/ppermute | solution.py:246
  129.8 13.7 %collective-permute-start.19 = (bf16[32,2048]{1,0:T(8,128)(2,1)S(1)}, bf16[32,2048]{1,0:T(8,128)(2,1)S(1)}, u32[]{:S(2)}, u32[]{:S(2)}) collective-permute-start(bf16[32,2048]{1,0:T(8,128)(2,1)S(1)} %get-tuple-element.47), channel_id=1, source_target_pairs={{0,1},{1,0},{2,3},{3,2},{4,5},{5,4},{6,7},{7,6},{8,9},{9,8},{10,11... | collective-permute-start | bytes 393224 | tf_op jit(solution)/shard_map/ppermute | solution.py:246
  139.7 8.5 %collective-permute-start.23 = (bf16[32,2048]{1,0:T(8,128)(2,1)S(1)}, bf16[32,2048]{1,0:T(8,128)(2,1)S(1)}, u32[]{:S(2)}, u32[]{:S(2)}) collective-permute-start(bf16[32,2048]{1,0:T(8,128)(2,1)S(1)} %get-tuple-element.52), channel_id=1, source_target_pairs={{0,4},{1,5},{2,6},{3,7},{4,0},{5,1},{6,2},{7,3},{8,12},{9,13},{10,... | collective-permute-start | bytes 393224 | tf_op jit(solution)/shard_map/ppermute | solution.py:246
  141.2 7.0 %collective-permute-start.24 = (bf16[32,2048]{1,0:T(8,128)(2,1)S(1)}, bf16[32,2048]{1,0:T(8,128)(2,1)S(1)}, u32[]{:S(2)}, u32[]{:S(2)}) collective-permute-start(bf16[32,2048]{1,0:T(8,128)(2,1)S(1)} %get-tuple-element.53), channel_id=1, source_target_pairs={{0,2},{1,3},{2,0},{3,1},{4,6},{5,7},{6,4},{7,5},{8,10},{9,11},{10,... | collective-permute-start | bytes 393224 | tf_op jit(solution)/shard_map/ppermute | solution.py:246
  141.9 9.6 %collective-permute-start.21 = (bf16[32,2048]{1,0:T(8,128)(2,1)S(1)}, bf16[32,2048]{1,0:T(8,128)(2,1)S(1)}, u32[]{:S(2)}, u32[]{:S(2)}) collective-permute-start(bf16[32,2048]{1,0:T(8,128)(2,1)S(1)} %get-tuple-element.56), channel_id=1, source_target_pairs={{0,6},{1,7},{2,4},{3,5},{4,2},{5,3},{6,0},{7,1},{8,14},{9,15},{10,... | collective-permute-start | bytes 393224 | tf_op jit(solution)/shard_map/ppermute | solution.py:246
  151.6 7.4 %collective-permute-start.25 = (bf16[16,2048]{1,0:T(8,128)(2,1)S(1)}, bf16[16,2048]{1,0:T(8,128)(2,1)S(1)}, u32[]{:S(2)}, u32[]{:S(2)}) collective-permute-start(bf16[16,2048]{1,0:T(8,128)(2,1)S(1)} %slice.94), channel_id=1, source_target_pairs={{0,14},{1,15},{2,12},{3,13},{4,10},{5,11},{6,8},{7,9},{8,6},{9,7},... | collective-permute-start | bytes 196616 | tf_op jit(solution)/shard_map/ppermute | solution.py:246
  159.1 7.7 %collective-permute-start.26 = (bf16[16,2048]{1,0:T(8,128)(2,1)S(1)}, bf16[16,2048]{1,0:T(8,128)(2,1)S(1)}, u32[]{:S(2)}, u32[]{:S(2)}) collective-permute-start(bf16[16,2048]{1,0:T(8,128)(2,1)S(1)} %shard_map.100), channel_id=1, source_target_pairs={{0,14},{1,15},{2,12},{3,13},{4,10},{5,11},{6,8},{7,9},{8,6},{9,7},... | collective-permute-start | bytes 196616 | tf_op jit(solution)/shard_map/ppermute | solution.py:246
  166.8 5.1 %collective-permute-start.29 = (bf16[32,2048]{1,0:T(8,128)(2,1)S(1)}, bf16[32,2048]{1,0:T(8,128)(2,1)S(1)}, u32[]{:S(2)}, u32[]{:S(2)}) collective-permute-start(bf16[32,2048]{1,0:T(8,128)(2,1)S(1)} %pad_maximum_fusion.refs_0_), channel_id=1, source_target_pairs={{0,6},{1,7},{2,4},{3,5},{4,2},{5,3},{6,0},{7,1},{8,14},{9,15},{10,... | collective-permute-start | bytes 393224 | tf_op jit(solution)/shard_map/ppermute | solution.py:246
  168.1 6.0 %collective-permute-start.28 = (bf16[32,2048]{1,0:T(8,128)(2,1)S(1)}, bf16[32,2048]{1,0:T(8,128)(2,1)S(1)}, u32[]{:S(2)}, u32[]{:S(2)}) collective-permute-start(bf16[32,2048]{1,0:T(8,128)(2,1)S(1)} %pad_maximum_fusion.refs_0_), channel_id=1, source_target_pairs={{0,4},{1,5},{2,6},{3,7},{4,0},{5,1},{6,2},{7,3},{8,12},{9,13},{10,... | collective-permute-start | bytes 393224 | tf_op jit(solution)/shard_map/ppermute | solution.py:246
  168.1 6.7 %collective-permute-start.27 = (bf16[32,2048]{1,0:T(8,128)(2,1)S(1)}, bf16[32,2048]{1,0:T(8,128)(2,1)S(1)}, u32[]{:S(2)}, u32[]{:S(2)}) collective-permute-start(bf16[32,2048]{1,0:T(8,128)(2,1)S(1)} %pad_maximum_fusion.refs_0_), channel_id=1, source_target_pairs={{0,2},{1,3},{2,0},{3,1},{4,6},{5,7},{6,4},{7,5},{8,10},{9,11},{10,... | collective-permute-start | bytes 393224 | tf_op jit(solution)/shard_map/ppermute | solution.py:246
  170.4 6.3 %collective-permute-start.30 = (bf16[32,2048]{1,0:T(8,128)(2,1)S(1)}, bf16[32,2048]{1,0:T(8,128)(2,1)S(1)}, u32[]{:S(2)}, u32[]{:S(2)}) collective-permute-start(bf16[32,2048]{1,0:T(8,128)(2,1)S(1)} %pad_maximum_fusion.refs_0_), channel_id=1, source_target_pairs={{0,1},{1,0},{2,3},{3,2},{4,5},{5,4},{6,7},{7,6},{8,9},{9,8},{10,11... | collective-permute-start | bytes 393224 | tf_op jit(solution)/shard_map/ppermute | solution.py:246
  172.0 5.9 %collective-permute-start.33 = (bf16[32,2048]{1,0:T(8,128)(2,1)S(1)}, bf16[32,2048]{1,0:T(8,128)(2,1)S(1)}, u32[]{:S(2)}, u32[]{:S(2)}) collective-permute-start(bf16[32,2048]{1,0:T(8,128)(2,1)S(1)} %collective-permute-done.29.refs_3_), channel_id=1, source_target_pairs={{0,1},{1,0},{2,3},{3,2},{4,5},{5,4},{6,7},{7,6},{8,9},{9,8},{10,11... | collective-permute-start | bytes 393224 | tf_op jit(solution)/shard_map/ppermute | solution.py:246
  174.1 5.2 %collective-permute-start.32 = (bf16[32,2048]{1,0:T(8,128)(2,1)S(1)}, bf16[32,2048]{1,0:T(8,128)(2,1)S(1)}, u32[]{:S(2)}, u32[]{:S(2)}) collective-permute-start(bf16[32,2048]{1,0:T(8,128)(2,1)S(1)} %collective-permute-done.28.refs_2_), channel_id=1, source_target_pairs={{0,1},{1,0},{2,3},{3,2},{4,5},{5,4},{6,7},{7,6},{8,9},{9,8},{10,11... | collective-permute-start | bytes 393224 | tf_op jit(solution)/shard_map/ppermute | solution.py:246
  174.8 5.9 %collective-permute-start.31 = (bf16[32,2048]{1,0:T(8,128)(2,1)S(1)}, bf16[32,2048]{1,0:T(8,128)(2,1)S(1)}, u32[]{:S(2)}, u32[]{:S(2)}) collective-permute-start(bf16[32,2048]{1,0:T(8,128)(2,1)S(1)} %collective-permute-done.27.refs_1_), channel_id=1, source_target_pairs={{0,1},{1,0},{2,3},{3,2},{4,5},{5,4},{6,7},{7,6},{8,9},{9,8},{10,11... | collective-permute-start | bytes 393224 | tf_op jit(solution)/shard_map/ppermute | solution.py:246

commit v3 on v2

--- a/solution.py
+++ b/solution.py
@@ -17,7 +17,7 @@
 START, END, PENALTY, STEP = 16, 17, 18, 19
 
 TILE = 768
-PARTS = (2304, 768)
+COPIES = 4
 CUT = 256
 
 
@@ -44,24 +44,55 @@
         put(rows_of(me, hop ^ MIRROR), piece[OWN:, :])
 
 
-def turn_kernel(parts, n_pieces, add, pack, *refs):
+def cut_kernel(where, whole, away, beside, sems):
+    people, reach = away.shape
+    count = people // COPIES
+    core = where[0] // PEOPLE % 2
+    copies = []
+    for n, (out, half) in enumerate(((away, core), (beside, 1 - core))):
+        cols = pl.ds(pl.multiple_of(half * reach, reach), reach)
+        for k in range(COPIES):
+            rows = pl.ds(k * count, count)
+            sem = sems.at[n * COPIES + k]
+            copies.append(pltpu.make_async_copy(whole.at[rows, cols], out.at[rows, :], sem))
+    for copy in copies:
+        copy.start()
+    for copy in copies:
+        copy.wait()
+
+
+def column_of(where, block, reach):
+    core = where[0] // PEOPLE % 2
+    return pl.multiple_of((block + core * (3 - 2 * block)) * reach, reach)
+
+
+def fit(where, rows, blocks, coef):
+    fitted = 0.0
+    for i, block in blocks.items():
+        reach = block.shape[1]
+        fitted += dot_t(block[rows, :], coef[:, pl.ds(column_of(where, i, reach), reach)])
+    return fitted
+
+
+def early_kernel(where, second, third, fourth, target, coef, part):
+    blocks = {1: second, 2: third, 3: fourth}
+    for step in range(0, target.shape[0], TILE):
+        rows = pl.ds(step, TILE)
+        part[rows, :] = target[rows, :].astype(jnp.float32) - fit(where, rows, blocks, coef)
+
+
+def turn_kernel(n_pieces, *refs):
     where, *refs = refs
-    blocks, refs = refs[: 4 * len(parts)], refs[4 * len(parts) :]
+    blocks, refs = refs[:4], refs[4:]
     target, *refs = refs
     pieces, refs = refs[:n_pieces], refs[n_pieces:]
-    if add:
-        prior, *refs = refs
+    keep, *refs = refs
+    gives, refs = refs[: len(GIVE)], refs[len(GIVE) :]
     reach = blocks[0].shape[1]
     width = 4 * reach
     me = person(where)
-    if pack:
-        keep, *refs = refs
-        gives, refs = refs[: len(GIVE)], refs[len(GIVE) :]
     if n_pieces > 1:
-        peaks, *refs = refs
-    grad, resid_t, *refs = refs
-    if n_pieces > 1:
-        coef, tail = refs
+        peaks, grad, resid_t, coef, tail = refs
 
         def put(rows, piece):
             coef[rows, :] = piece[:, :width]
@@ -73,31 +104,18 @@
         peaks[...] = flat[:count, :] + flat[count : 2 * count, :]
     else:
         (coef,) = pieces
-
-    done = 0
-    for k, (first, count) in enumerate(parts):
-        for step in range(0, count, TILE):
-            rows = pl.ds(step, TILE)
-            fitted = 0.0
-            for i in range(4):
-                weights = coef[:, i * reach : (i + 1) * reach]
-                fitted += dot_t(blocks[4 * k + i][rows, :], weights)
-            goal = target[pl.ds(first + step, TILE), :].astype(jnp.float32)
-            resid_t[:, pl.ds(done, TILE)] = (goal - fitted).astype(jnp.bfloat16).T
-            done += TILE
-
-    for i in range(4):
+        grad, resid_t = refs
+
+    last = {0: blocks[0]} if n_pieces == 1 else dict(enumerate(blocks))
+    for step in range(0, target.shape[0], TILE):
+        rows = pl.ds(step, TILE)
+        resid = target[rows, :].astype(jnp.float32) - fit(where, rows, last, coef)
+        resid_t[:, rows] = resid.astype(jnp.bfloat16).T
+
+    for i, block in enumerate(blocks):
         for j in range(0, reach, CUT):
-            at = i * reach + j
-            total = prior[:, at : at + CUT] if add else 0.0
-            done = 0
-            for k, (first, count) in enumerate(parts):
-                block = blocks[4 * k + i]
-                total += dot(resid_t[:, pl.ds(done, count)], block[:, j : j + CUT])
-                done += count
-            grad[:, at : at + CUT] = total
-    if not pack:
-        return
+            cols = pl.ds(pl.multiple_of(column_of(where, i, reach) + j, CUT), CUT)
+            grad[:, cols] = dot(resid_t[...], block[:, j : j + CUT])
 
     def read(hop):
         rows = rows_of(me, hop)
@@ -185,48 +203,54 @@
     return [pl.BlockSpec(memory_space=pltpu.SMEM)] + [vmem] * count
 
 
-def split(genotypes, reach):
-    out, first = [], 0
-    for count in PARTS:
-        for column in (reach, 0):
-            piece = genotypes[first : first + count, column : column + reach]
-            piece, genotypes = lax.optimization_barrier((piece, genotypes))
-            out.append(in_vmem(piece))
-        first += count
-    return out
-
-
-def local_grad(where, chosen, blocks, target, pieces, prior=None, pack=True):
-    genes = target.shape[1]
-    reach = blocks[0][0].shape[1]
-    width = 4 * reach
-    parts = [(sum(PARTS[:k]), PARTS[k]) for k in chosen]
-    people = sum(count for _, count in parts)
-    given = [block for k in chosen for block in blocks[k]]
-    operands = [*given, target, *pieces] + ([] if prior is None else [prior])
-    operands = [in_vmem(v) for v in operands]
-    local = pltpu.VMEM((genes, width), jnp.float32)
-    outs, scratch = [], [pltpu.VMEM((genes, people), jnp.bfloat16)]
-    if pack:
-        outs.append(pltpu.VMEM((2 * OWN * len(NEAR), width), jnp.float32))
-        outs += [pltpu.VMEM((2 * OWN * len(hops), width), jnp.bfloat16) for hops in GIVE]
-        scratch = [local, *scratch]
-    else:
-        outs.append(local)
+def cut_columns(where, genotypes, reach):
+    half = pltpu.VMEM((genotypes.shape[0], reach), genotypes.dtype)
+    return pl.pallas_call(
+        cut_kernel,
+        out_shape=[half, half],
+        in_specs=[pl.BlockSpec(memory_space=pltpu.SMEM), pl.BlockSpec(memory_space=pltpu.HBM)],
+        out_specs=[pl.BlockSpec(memory_space=pltpu.VMEM)] * 2,
+        scratch_shapes=[pltpu.SemaphoreType.DMA((2 * COPIES,))],
+        compiler_params=pltpu.CompilerParams(vmem_limit_bytes=8 << 20),
+    )(where, pltpu.with_memory_space_constraint(genotypes, pltpu.HBM))
+
+
+def cost(people, blocks, products):
+    flops = 2 * products * people * blocks.shape[0] * blocks.shape[1]
+    return pl.CostEstimate(flops=flops, bytes_accessed=0, transcendentals=0)
+
+
+def early_part(where, blocks, target, coef):
+    operands = [in_vmem(v) for v in (*blocks, target, coef)]
+    return pl.pallas_call(
+        early_kernel,
+        out_shape=pltpu.VMEM(target.shape, jnp.float32),
+        in_specs=specs(len(operands)),
+        out_specs=pl.BlockSpec(memory_space=pltpu.VMEM),
+        compiler_params=pltpu.CompilerParams(vmem_limit_bytes=8 << 20),
+        cost_estimate=pl.CostEstimate(flops=0, bytes_accessed=0, transcendentals=0),
+    )(where, *operands)
+
+
+def local_grad(where, blocks, target, pieces):
+    people, genes = target.shape
+    width = 4 * blocks[0].shape[1]
+    operands = [in_vmem(v) for v in (*blocks, target, *pieces)]
+    outs = [pltpu.VMEM((2 * OWN * len(NEAR), width), jnp.float32)]
+    outs += [pltpu.VMEM((2 * OWN * len(hops), width), jnp.bfloat16) for hops in GIVE]
+    scratch = [pltpu.VMEM((genes, width), jnp.float32), pltpu.VMEM((genes, people), jnp.bfloat16)]
     if len(pieces) > 1:
         outs.append(pltpu.VMEM((width // LANES, genes), jnp.float32))
         scratch.append(pltpu.VMEM((genes, width), jnp.bfloat16))
         scratch.append(pltpu.VMEM((genes, LANES), jnp.bfloat16))
     return pl.pallas_call(
-        functools.partial(turn_kernel, parts, len(pieces), prior is not None, pack),
+        functools.partial(turn_kernel, len(pieces)),
         out_shape=outs,
         in_specs=specs(len(operands)),
         out_specs=[pl.BlockSpec(memory_space=pltpu.VMEM)] * len(outs),
         scratch_shapes=scratch,
         compiler_params=pltpu.CompilerParams(vmem_limit_bytes=20 << 20),
-        cost_estimate=pl.CostEstimate(
-            flops=4 * people * width * genes, bytes_accessed=0, transcendentals=0
-        ),
+        cost_estimate=cost(people, jax.ShapeDtypeStruct((genes, width), jnp.bfloat16), 2),
     )(where, *operands)
 
 
@@ -274,8 +298,10 @@
     total = genotypes.shape[0] * lax.axis_size("people")
     genes, width = coef_start.shape
     reach = (width - v_local) // 2
-    chain = [(i, i + 1) for i in range(lax.axis_size("genome") - 1)]
-    back = [(target, source) for source, target in chain]
+    count = lax.axis_size("genome")
+    sibling = [(i, i ^ 1) for i in range(count)]
+    beyond = [(i, i + 1 if i % 2 else i - 1) for i in range(count)]
+    beyond = [(source, target) for source, target in beyond if 0 <= target < count]
     where = lax.axis_index(("genome", "people")).astype(jnp.int32)[None]
     vectors = [v[None] for v in (window_start, window_end, penalty, step_size)]
     by_gene, coef, coef_own = small_call(
@@ -286,18 +312,12 @@
         [pltpu.VMEM((LANES, genes), jnp.float32)],
     )
 
-    halves = split(genotypes, reach)
-    blocks = []
-    for k in range(len(PARTS)):
-        right, left = halves[2 * k], halves[2 * k + 1]
-        before = (blocks[0][0], blocks[0][3], coef) if k else (where,)
-        right, left, *_ = lax.optimization_barrier((right, left, *before))
-        low = lax.ppermute(right, "genome", chain)
-        high = lax.ppermute(left, "genome", back)
-        blocks.append((low, left, right, high))
-
-    (prior,) = local_grad(where, (0,), blocks, expression, [coef], pack=False)
-    keep, *gives = local_grad(where, (1,), blocks, expression, [coef], prior)
+    away, beside = cut_columns(where, genotypes, reach)
+    slow = lax.ppermute(away, "genome", beyond)
+    fast = lax.ppermute(beside, "genome", sibling)
+    blocks = [slow, away, beside, fast]
+    part = early_part(where, blocks[1:], expression, coef)
+    keep, *gives = local_grad(where, blocks, part, [coef])
     near, far = sum_to_owner(keep, gives)
     coef_own, sent = small_call(
         functools.partial(update_kernel, total, True),
@@ -307,7 +327,7 @@
     )
     pieces = gather_rows(sent)
 
-    keep, *gives, peaks = local_grad(where, (0, 1), blocks, expression, pieces)
+    keep, *gives, peaks = local_grad(where, blocks, expression, pieces)
     near, far = sum_to_owner(keep, gives)
     (last,) = small_call(
         functools.partial(update_kernel, total, False),

time: 186 us -> 172 us (0.925); the launches traced: 182 us -> 170 us
  local copies, waits for them, and re-layouts: 9.52 us -> 0.67 us
  starting transfers between devices: 62.7 us -> 55.3 us
  waiting for transfers between devices: 87.3 us -> 91.1 us
    ppermute x4 -> x2, starting transfers between devices: 16.1 us -> 2.83 us  [the longest x1 2.74 us: on_device(): slow = lax.ppermute(away, 'genome', beyond)]
    slice x4 -> x0, local copies, waits for them, and re-layouts: 7.44 us -> none  [split(): piece = genotypes[first:first + count, column:column + reach]]
    ppermute x4 -> x2, waiting for transfers between devices: 24.3 us -> 31.1 us  [the longest x1 30.3 us: on_device(): slow = lax.ppermute(away, 'genome', beyond)]
    ppermute x30, starting transfers between devices: 46.6 us -> 52.4 us  [swap(): return lax.ppermute(block, 'people', [(i, i ^ hop) for i in range(count)])]
    ppermute x30, waiting for transfers between devices: 63 us -> 60 us  [swap(): return lax.ppermute(block, 'people', [(i, i ^ hop) for i in range(count)])]
    pallas_call x3 -> x4, Pallas kernels: 16.7 us -> 17.4 us  [the longest x2 11.7 us: local_grad(): pl.pallas_call(functools.partial(turn_kernel, len(pieces)), out_shape=out...]
  transfers between devices with their start and end apart: 34 -> 32, of which waited for: 25 -> 22; matrix products, arithmetic and copies ran while one was open for 2% -> 0% of each run, Pallas kernels for 4% -> 3%
where the time goes in v3:
time: 172 us; the launch traced here: 170 us
  waiting for transfers between devices  91.1 us (53%)
  starting transfers between devices  55.3 us (32%)
  Pallas kernels  22.1 us (13%)
    ppermute x30, waiting for transfers between devices, swap(): return lax.ppermute(block, 'people', [(i, i ^ hop) for i in range(count)])  60 us
    ppermute x30, starting transfers between devices, swap(): return lax.ppermute(block, 'people', [(i, i ^ hop) for i in range(count)])  52.4 us
    ppermute x1, waiting for transfers between devices, on_device(): slow = lax.ppermute(away, 'genome', beyond)  30.3 us
    pallas_call x2, Pallas kernels, local_grad(): pl.pallas_call(functools.partial(turn_kernel, len(pieces)), out_shape=out...  11.7 us
  transfers between devices with their start and end apart: 32, of which 22 were waited for; matrix products, arithmetic and copies ran while one was open for 0% of the time, Pallas kernels for 3%

profile of v3, /device:TPU:56, one launch (start us, length us, event | category | flops | bytes accessed | tf_op | source)
XLA Modules:
  0.0 170.3 jit_solution(2016466672590556019)
XLA Ops:
  0.7 3.0 %shard_map.96 = (bf16[3072,512]{1,0:T(8,128)(2,1)S(1)}, bf16[3072,512]{1,0:T(8,128)(2,1)S(1)}) custom-call(s32[1]{0:T(128)} %bitcast.where.refs_0_, bf16[3072,1024]{1,0:T(8,128)(2,1)} %whole.1), custom_call_target="tpu_custom_call" | custom-call | tf_op jit(solution)/shard_map/pallas_call | solution.py:208
  3.7 0.1 collective-permute-start.1
  3.8 2.7 %collective-permute-start = (bf16[3072,512]{1,0:T(8,128)(2,1)S(1)}, bf16[3072,512]{1,0:T(8,128)(2,1)S(1)}, u32[]{:S(2)}, u32[]{:S(2)}) collective-permute-start(bf16[3072,512]{1,0:T(8,128)(2,1)S(1)} %get-tuple-element.19.second.refs_2_), channel_id=1, source_target_pairs={{16,32},{32,16},{48,64},{64,48},{80,96},{96,80},{112,128},{128,112... | collective-permute-start | bytes 9437192 | tf_op jit(solution)/shard_map/ppermute | solution.py:316
  6.6 2.1 %shard_map.95 = (f32[256,128]{1,0:T(8,128)S(1)}, bf16[256,2048]{1,0:T(8,128)(2,1)S(1)}, f32[16,2048]{1,0:T(8,128)S(1)}) custom-call(s32[1]{0:T(128)} %bitcast.where.refs_0_, s32[16,256]{1,0:T(8,128)S(1)} %bitcast.8, s32[1,256]{1,0:T(1,128)S(1)} %bitcast.9, s32[1,256]{1,0:T(1,128)S(1)} %bitcast.10, f32[1,256]{1,0:T(1,128)S(1)} %bitcast.11, ...), custom_call_target="tpu_custom_call" | custom-call | tf_op jit(solution)/shard_map/pallas_call | solution.py:258
  8.7 0.8 collective-permute-done.1.fourth.refs_4_
  9.5 2.6 %shard_map.97.refs_5_ = f32[3072,256]{1,0:T(8,128)S(1)} custom-call(s32[1]{0:T(128)} %bitcast.where.refs_0_, bf16[3072,512]{1,0:T(8,128)(2,1)S(1)} %get-tuple-element.19.second.refs_2_, bf16[3072,512]{1,0:T(8,128)(2,1)S(1)} %get-tuple-element.20.third.refs_3_, bf16[3072,512]{1,0:T(8,128)(2,1)S(1)} %collective-permute-done.1.fourth.refs_4_, ...), custom_call_target="tpu_custom_call" | custom-call | tf_op jit(solution)/shard_map/pallas_call | solution.py:225
  12.1 30.3 %collective-permute-done.refs_1_ = bf16[3072,512]{1,0:T(8,128)(2,1)S(1)} collective-permute-done((bf16[3072,512]{1,0:T(8,128)(2,1)S(1)}, bf16[3072,512]{1,0:T(8,128)(2,1)S(1)}, u32[]{:S(2)}, u32[]{:S(2)}) %collective-permute-start) | collective-permute-done | bytes 3145760 | tf_op jit(solution)/shard_map/ppermute | solution.py:316
  42.4 4.6 %shard_map.98 = (f32[128,2048]{1,0:T(8,128)S(1)}, bf16[32,2048]{1,0:T(8,128)(2,1)S(1)}, bf16[64,2048]{1,0:T(8,128)(2,1)S(1)}, bf16[32,2048]{1,0:T(8,128)(2,1)S(1)}) custom-call(s32[1]{0:T(128)} %bitcast.where.refs_0_, bf16[3072,512]{1,0:T(8,128)(2,1)S(1)} %collective-permute-done.refs_1_, bf16[3072,512]{1,0:T(8,128)(2,1)S(1)} %get-tuple-element.19.second.refs_2_, ...), custom_call_target="tpu_custom_call" | custom-call | flops 6442450944 | tf_op jit(solution)/shard_map/pallas_call | solution.py:246
  47.0 1.6 collective-permute-start.5
  48.6 0.5 collective-permute-start.3
  49.1 1.5 collective-permute-start.2
  50.6 5.3 %collective-permute-done.3 = bf16[32,2048]{1,0:T(8,128)(2,1)S(1)} collective-permute-done((bf16[32,2048]{1,0:T(8,128)(2,1)S(1)}, bf16[32,2048]{1,0:T(8,128)(2,1)S(1)}, u32[]{:S(2)}, u32[]{:S(2)}) %collective-permute-start.3) | collective-permute-done | bytes 131104 | tf_op jit(solution)/shard_map/ppermute | solution.py:270
  55.9 0.1 add_convert_fusion.4
  56.0 3.4 %collective-permute-start.6 = (bf16[32,2048]{1,0:T(8,128)(2,1)S(1)}, bf16[32,2048]{1,0:T(8,128)(2,1)S(1)}, u32[]{:S(2)}, u32[]{:S(2)}) collective-permute-start(bf16[32,2048]{1,0:T(8,128)(2,1)S(1)} %get-tuple-element.36), channel_id=1, source_target_pairs={{0,4},{1,5},{2,6},{3,7},{4,0},{5,1},{6,2},{7,3},{8,12},{9,13},{10,... | collective-permute-start | bytes 393224 | tf_op jit(solution)/shard_map/ppermute | solution.py:270
  59.4 0.1 collective-permute-start.7
  59.5 0.6 collective-permute-start.4
  60.0 2.7 %collective-permute-done.6 = bf16[32,2048]{1,0:T(8,128)(2,1)S(1)} collective-permute-done((bf16[32,2048]{1,0:T(8,128)(2,1)S(1)}, bf16[32,2048]{1,0:T(8,128)(2,1)S(1)}, u32[]{:S(2)}, u32[]{:S(2)}) %collective-permute-start.6) | collective-permute-done | bytes 131104 | tf_op jit(solution)/shard_map/ppermute | solution.py:270
  62.8 1.6 collective-permute-done.7
  64.3 4.0 %collective-permute-done.4 = bf16[32,2048]{1,0:T(8,128)(2,1)S(1)} collective-permute-done((bf16[32,2048]{1,0:T(8,128)(2,1)S(1)}, bf16[32,2048]{1,0:T(8,128)(2,1)S(1)}, u32[]{:S(2)}, u32[]{:S(2)}) %collective-permute-start.4) | collective-permute-done | bytes 131104 | tf_op jit(solution)/shard_map/ppermute | solution.py:270
  68.5 5.4 %collective-permute-start.8 = (bf16[16,2048]{1,0:T(8,128)(2,1)S(1)}, bf16[16,2048]{1,0:T(8,128)(2,1)S(1)}, u32[]{:S(2)}, u32[]{:S(2)}) collective-permute-start(bf16[16,2048]{1,0:T(8,128)(2,1)S(1)} %slice.79), channel_id=1, source_target_pairs={{0,14},{1,15},{2,12},{3,13},{4,10},{5,11},{6,8},{7,9},{8,6},{9,7},... | collective-permute-start | bytes 196616 | tf_op jit(solution)/shard_map/ppermute | solution.py:270
  73.8 2.2 %collective-permute-done.8.far = bf16[16,2048]{1,0:T(8,128)(2,1)S(1)} collective-permute-done((bf16[16,2048]{1,0:T(8,128)(2,1)S(1)}, bf16[16,2048]{1,0:T(8,128)(2,1)S(1)}, u32[]{:S(2)}, u32[]{:S(2)}) %collective-permute-start.8) | collective-permute-done | bytes 65568 | tf_op jit(solution)/shard_map/ppermute | solution.py:270
  76.1 1.0 shard_map.99
  77.1 5.3 %collective-permute-start.9 = (bf16[16,2176]{1,0:T(8,128)(2,1)S(1)}, bf16[16,2176]{1,0:T(8,128)(2,1)S(1)}, u32[]{:S(2)}, u32[]{:S(2)}) collective-permute-start(bf16[16,2176]{1,0:T(8,128)(2,1)S(1)} %get-tuple-element.27.base), channel_id=1, source_target_pairs={{0,14},{1,15},{2,12},{3,13},{4,10},{5,11},{6,8},{7,9},{8,6},{9,7},... | collective-permute-start | bytes 208904 | tf_op jit(solution)/shard_map/ppermute | solution.py:270
  82.4 2.3 %collective-permute-done.9 = bf16[16,2176]{1,0:T(8,128)(2,1)S(1)} collective-permute-done((bf16[16,2176]{1,0:T(8,128)(2,1)S(1)}, bf16[16,2176]{1,0:T(8,128)(2,1)S(1)}, u32[]{:S(2)}, u32[]{:S(2)}) %collective-permute-start.9) | collective-permute-done | bytes 69664 | tf_op jit(solution)/shard_map/ppermute | solution.py:270
  84.7 3.6 %collective-permute-start.12 = (bf16[32,2176]{1,0:T(8,128)(2,1)S(1)}, bf16[32,2176]{1,0:T(8,128)(2,1)S(1)}, u32[]{:S(2)}, u32[]{:S(2)}) collective-permute-start(bf16[32,2176]{1,0:T(8,128)(2,1)S(1)} %constant_dynamic-update-slice_fusion.refs_6_), channel_id=1, source_target_pairs={{0,6},{1,7},{2,4},{3,5},{4,2},{5,3},{6,0},{7,1},{8,14},{9,15},{10,... | collective-permute-start | bytes 417800 | tf_op jit(solution)/shard_map/ppermute | solution.py:270
  88.3 1.6 collective-permute-start.10
  89.9 1.5 collective-permute-start.13
  91.4 5.0 %collective-permute-done.12.refs_9_ = bf16[32,2176]{1,0:T(8,128)(2,1)S(1)} collective-permute-done((bf16[32,2176]{1,0:T(8,128)(2,1)S(1)}, bf16[32,2176]{1,0:T(8,128)(2,1)S(1)}, u32[]{:S(2)}, u32[]{:S(2)}) %collective-permute-start.12) | collective-permute-done | bytes 139296 | tf_op jit(solution)/shard_map/ppermute | solution.py:270
  96.5 1.5 collective-permute-start.16
  97.9 0.8 collective-permute-start.15
  98.7 1.3 collective-permute-start.14
  100.0 3.0 %collective-permute-done.16.refs_13_ = bf16[32,2176]{1,0:T(8,128)(2,1)S(1)} collective-permute-done((bf16[32,2176]{1,0:T(8,128)(2,1)S(1)}, bf16[32,2176]{1,0:T(8,128)(2,1)S(1)}, u32[]{:S(2)}, u32[]{:S(2)}) %collective-permute-start.16) | collective-permute-done | bytes 139296 | tf_op jit(solution)/shard_map/ppermute | solution.py:270
  103.0 3.0 %collective-permute-done.15.refs_12_ = bf16[32,2176]{1,0:T(8,128)(2,1)S(1)} collective-permute-done((bf16[32,2176]{1,0:T(8,128)(2,1)S(1)}, bf16[32,2176]{1,0:T(8,128)(2,1)S(1)}, u32[]{:S(2)}, u32[]{:S(2)}) %collective-permute-start.15) | collective-permute-done | bytes 139296 | tf_op jit(solution)/shard_map/ppermute | solution.py:270
  106.0 2.0 %collective-permute-done.14.refs_11_ = bf16[32,2176]{1,0:T(8,128)(2,1)S(1)} collective-permute-done((bf16[32,2176]{1,0:T(8,128)(2,1)S(1)}, bf16[32,2176]{1,0:T(8,128)(2,1)S(1)}, u32[]{:S(2)}, u32[]{:S(2)}) %collective-permute-start.14) | collective-permute-done | bytes 139296 | tf_op jit(solution)/shard_map/ppermute | solution.py:270
  108.0 7.1 %shard_map.100 = (f32[128,2048]{1,0:T(8,128)S(1)}, bf16[32,2048]{1,0:T(8,128)(2,1)S(1)}, bf16[64,2048]{1,0:T(8,128)(2,1)S(1)}, bf16[32,2048]{1,0:T(8,128)(2,1)S(1)}, f32[16,256]{1,0:T(8,128)S(1)}) custom-call(s32[1]{0:T(128)} %bitcast.where.refs_0_, bf16[3072,512]{1,0:T(8,128)(2,1)S(1)} %collective-permute-done.refs_1_, ...), custom_call_target="tpu_custom_call" | custom-call | flops 6442450944 | tf_op jit(solution)/shard_map/pallas_call | solution.py:246
  115.1 1.5 collective-permute-start.20
  116.6 0.6 collective-permute-start.18
  117.2 1.5 collective-permute-start.17
  118.7 8.0 %collective-permute-done.18 = bf16[32,2048]{1,0:T(8,128)(2,1)S(1)} collective-permute-done((bf16[32,2048]{1,0:T(8,128)(2,1)S(1)}, bf16[32,2048]{1,0:T(8,128)(2,1)S(1)}, u32[]{:S(2)}, u32[]{:S(2)}) %collective-permute-start.18) | collective-permute-done | bytes 131104 | tf_op jit(solution)/shard_map/ppermute | solution.py:270
  126.7 0.1 add_convert_fusion.1
  126.8 0.1 collective-permute-start.21
  126.9 2.0 %collective-permute-start.22 = (bf16[32,2048]{1,0:T(8,128)(2,1)S(1)}, bf16[32,2048]{1,0:T(8,128)(2,1)S(1)}, u32[]{:S(2)}, u32[]{:S(2)}) collective-permute-start(bf16[32,2048]{1,0:T(8,128)(2,1)S(1)} %get-tuple-element.35), channel_id=1, source_target_pairs={{0,2},{1,3},{2,0},{3,1},{4,6},{5,7},{6,4},{7,5},{8,10},{9,11},{10,... | collective-permute-start | bytes 393224 | tf_op jit(solution)/shard_map/ppermute | solution.py:270
  128.9 1.5 collective-permute-start.19
  130.4 2.5 %collective-permute-done.21 = bf16[32,2048]{1,0:T(8,128)(2,1)S(1)} collective-permute-done((bf16[32,2048]{1,0:T(8,128)(2,1)S(1)}, bf16[32,2048]{1,0:T(8,128)(2,1)S(1)}, u32[]{:S(2)}, u32[]{:S(2)}) %collective-permute-start.21) | collective-permute-done | bytes 131104 | tf_op jit(solution)/shard_map/ppermute | solution.py:270
  132.9 1.1 collective-permute-done.22
  134.0 4.4 %collective-permute-done.19 = bf16[32,2048]{1,0:T(8,128)(2,1)S(1)} collective-permute-done((bf16[32,2048]{1,0:T(8,128)(2,1)S(1)}, bf16[32,2048]{1,0:T(8,128)(2,1)S(1)}, u32[]{:S(2)}, u32[]{:S(2)}) %collective-permute-start.19) | collective-permute-done | bytes 131104 | tf_op jit(solution)/shard_map/ppermute | solution.py:270
  138.4 0.1 convert_add_fusion.near
  138.5 4.2 %collective-permute-start.23 = (bf16[16,2048]{1,0:T(8,128)(2,1)S(1)}, bf16[16,2048]{1,0:T(8,128)(2,1)S(1)}, u32[]{:S(2)}, u32[]{:S(2)}) collective-permute-start(bf16[16,2048]{1,0:T(8,128)(2,1)S(1)} %slice.78), channel_id=1, source_target_pairs={{0,14},{1,15},{2,12},{3,13},{4,10},{5,11},{6,8},{7,9},{8,6},{9,7},... | collective-permute-start | bytes 196616 | tf_op jit(solution)/shard_map/ppermute | solution.py:270
  142.8 3.3 %collective-permute-done.23.far = bf16[16,2048]{1,0:T(8,128)(2,1)S(1)} collective-permute-done((bf16[16,2048]{1,0:T(8,128)(2,1)S(1)}, bf16[16,2048]{1,0:T(8,128)(2,1)S(1)}, u32[]{:S(2)}, u32[]{:S(2)}) %collective-permute-start.23) | collective-permute-done | bytes 65568 | tf_op jit(solution)/shard_map/ppermute | solution.py:270
  146.1 0.2 shard_map.101
  146.3 4.1 %collective-permute-start.24 = (bf16[16,2048]{1,0:T(8,128)(2,1)S(1)}, bf16[16,2048]{1,0:T(8,128)(2,1)S(1)}, u32[]{:S(2)}, u32[]{:S(2)}) collective-permute-start(bf16[16,2048]{1,0:T(8,128)(2,1)S(1)} %shard_map.101), channel_id=1, source_target_pairs={{0,14},{1,15},{2,12},{3,13},{4,10},{5,11},{6,8},{7,9},{8,6},{9,7},... | collective-permute-start | bytes 196616 | tf_op jit(solution)/shard_map/ppermute | solution.py:270
  150.4 3.2 %collective-permute-done.24 = bf16[16,2048]{1,0:T(8,128)(2,1)S(1)} collective-permute-done((bf16[16,2048]{1,0:T(8,128)(2,1)S(1)}, bf16[16,2048]{1,0:T(8,128)(2,1)S(1)}, u32[]{:S(2)}, u32[]{:S(2)}) %collective-permute-start.24) | collective-permute-done | bytes 65568 | tf_op jit(solution)/shard_map/ppermute | solution.py:270
  153.7 0.1 collective-permute-start.27
  153.9 3.4 %collective-permute-start.25 = (bf16[32,2048]{1,0:T(8,128)(2,1)S(1)}, bf16[32,2048]{1,0:T(8,128)(2,1)S(1)}, u32[]{:S(2)}, u32[]{:S(2)}) collective-permute-start(bf16[32,2048]{1,0:T(8,128)(2,1)S(1)} %pad_maximum_fusion.refs_0_), channel_id=1, source_target_pairs={{0,2},{1,3},{2,0},{3,1},{4,6},{5,7},{6,4},{7,5},{8,10},{9,11},{10,... | collective-permute-start | bytes 393224 | tf_op jit(solution)/shard_map/ppermute | solution.py:270
  157.2 1.4 collective-permute-start.28
  158.7 2.4 %collective-permute-done.27.refs_3_ = bf16[32,2048]{1,0:T(8,128)(2,1)S(1)} collective-permute-done((bf16[32,2048]{1,0:T(8,128)(2,1)S(1)}, bf16[32,2048]{1,0:T(8,128)(2,1)S(1)}, u32[]{:S(2)}, u32[]{:S(2)}) %collective-permute-start.27) | collective-permute-done | bytes 131104 | tf_op jit(solution)/shard_map/ppermute | solution.py:270
  161.1 1.4 collective-permute-start.31
  162.4 0.7 collective-permute-start.30
  163.1 1.4 collective-permute-start.29
  164.5 0.6 copy.11
  165.1 1.0 collective-permute-done.31.refs_7_
  166.1 1.4 collective-permute-done.30.refs_6_
  167.5 1.4 collective-permute-done.29.refs_5_
  168.9 1.5 shard_map.102
  (32 shorter events, 0.2 us)
Async XLA Ops:
  0.6 5.9 %copy-start = (f32[256,2048]{1,0:T(8,128)S(1)}, f32[256,2048]{1,0:T(8,128)}, u32[]{:S(2)}) copy-start(f32[256,2048]{1,0:T(8,128)} %refs_4_.1) | copy-start | bytes 6291460
  0.6 5.9 %copy-start.2 = (s32[256,16]{0,1:T(8,128)S(1)}, s32[256,16]{0,1:T(8,128)}, u32[]{:S(2)}) copy-start(s32[256,16]{0,1:T(8,128)} %param.15) | copy-start | bytes 49156
  0.7 5.9 %copy-start.3 = (s32[256]{0:T(256)S(1)}, s32[256]{0:T(256)}, u32[]{:S(2)}) copy-start(s32[256]{0:T(256)} %param.13) | copy-start | bytes 3076
  0.7 5.9 %copy-start.4 = (s32[256]{0:T(256)S(1)}, s32[256]{0:T(256)}, u32[]{:S(2)}) copy-start(s32[256]{0:T(256)} %param.14) | copy-start | bytes 3076
  0.7 5.9 %copy-start.5 = (f32[256]{0:T(256)S(1)}, f32[256]{0:T(256)}, u32[]{:S(2)}) copy-start(f32[256]{0:T(256)} %param.11) | copy-start | bytes 3076
  0.7 5.9 %copy-start.6 = (f32[256]{0:T(256)S(1)}, f32[256]{0:T(256)}, u32[]{:S(2)}) copy-start(f32[256]{0:T(256)} %param.12) | copy-start | bytes 3076
  0.7 8.8 %copy-start.1 = (bf16[3072,256]{1,0:T(8,128)(2,1)S(1)}, bf16[3072,256]{1,0:T(8,128)(2,1)}, u32[]{:S(2)}) copy-start(bf16[3072,256]{1,0:T(8,128)(2,1)} %refs_5_.1) | copy-start | bytes 4718596
  3.7 5.7 %collective-permute-start.1 = (bf16[3072,512]{1,0:T(8,128)(2,1)S(1)}, bf16[3072,512]{1,0:T(8,128)(2,1)S(1)}, u32[]{:S(2)}, u32[]{:S(2)}) collective-permute-start(bf16[3072,512]{1,0:T(8,128)(2,1)S(1)} %get-tuple-element.20.third.refs_3_), channel_id=1, source_target_pairs={{0,16},{16,0},{32,48},{48,32},{64,80},{80,64},{96,112},{112,96},{1... | collective-permute-start | bytes 9437192 | tf_op jit(solution)/shard_map/ppermute | solution.py:317
  3.8 38.6 %collective-permute-start = (bf16[3072,512]{1,0:T(8,128)(2,1)S(1)}, bf16[3072,512]{1,0:T(8,128)(2,1)S(1)}, u32[]{:S(2)}, u32[]{:S(2)}) collective-permute-start(bf16[3072,512]{1,0:T(8,128)(2,1)S(1)} %get-tuple-element.19.second.refs_2_), channel_id=1, source_target_pairs={{16,32},{32,16},{48,64},{64,48},{80,96},{96,80},{112,128},{128,112... | collective-permute-start | bytes 9437192 | tf_op jit(solution)/shard_map/ppermute | solution.py:316
  47.0 8.9 %collective-permute-start.5 = (bf16[64,2048]{1,0:T(8,128)(2,1)S(1)}, bf16[64,2048]{1,0:T(8,128)(2,1)S(1)}, u32[]{:S(2)}, u32[]{:S(2)}) collective-permute-start(bf16[64,2048]{1,0:T(8,128)(2,1)S(1)} %get-tuple-element.25), channel_id=1, source_target_pairs={{0,1},{1,0},{2,3},{3,2},{4,5},{5,4},{6,7},{7,6},{8,9},{9,8},{10,11... | collective-permute-start | bytes 786440 | tf_op jit(solution)/shard_map/ppermute | solution.py:270
  48.6 7.3 %collective-permute-start.3 = (bf16[32,2048]{1,0:T(8,128)(2,1)S(1)}, bf16[32,2048]{1,0:T(8,128)(2,1)S(1)}, u32[]{:S(2)}, u32[]{:S(2)}) collective-permute-start(bf16[32,2048]{1,0:T(8,128)(2,1)S(1)} %get-tuple-element.24), channel_id=1, source_target_pairs={{0,1},{1,0},{2,3},{3,2},{4,5},{5,4},{6,7},{7,6},{8,9},{9,8},{10,11... | collective-permute-start | bytes 393224 | tf_op jit(solution)/shard_map/ppermute | solution.py:270
  49.1 10.9 %collective-permute-start.2 = (bf16[32,2048]{1,0:T(8,128)(2,1)S(1)}, bf16[32,2048]{1,0:T(8,128)(2,1)S(1)}, u32[]{:S(2)}, u32[]{:S(2)}) collective-permute-start(bf16[32,2048]{1,0:T(8,128)(2,1)S(1)} %get-tuple-element.23), channel_id=1, source_target_pairs={{0,1},{1,0},{2,3},{3,2},{4,5},{5,4},{6,7},{7,6},{8,9},{9,8},{10,11... | collective-permute-start | bytes 393224 | tf_op jit(solution)/shard_map/ppermute | solution.py:270
  56.0 6.8 %collective-permute-start.6 = (bf16[32,2048]{1,0:T(8,128)(2,1)S(1)}, bf16[32,2048]{1,0:T(8,128)(2,1)S(1)}, u32[]{:S(2)}, u32[]{:S(2)}) collective-permute-start(bf16[32,2048]{1,0:T(8,128)(2,1)S(1)} %get-tuple-element.36), channel_id=1, source_target_pairs={{0,4},{1,5},{2,6},{3,7},{4,0},{5,1},{6,2},{7,3},{8,12},{9,13},{10,... | collective-permute-start | bytes 393224 | tf_op jit(solution)/shard_map/ppermute | solution.py:270
  59.4 5.0 %collective-permute-start.7 = (bf16[32,2048]{1,0:T(8,128)(2,1)S(1)}, bf16[32,2048]{1,0:T(8,128)(2,1)S(1)}, u32[]{:S(2)}, u32[]{:S(2)}) collective-permute-start(bf16[32,2048]{1,0:T(8,128)(2,1)S(1)} %get-tuple-element.37), channel_id=1, source_target_pairs={{0,2},{1,3},{2,0},{3,1},{4,6},{5,7},{6,4},{7,5},{8,10},{9,11},{10,... | collective-permute-start | bytes 393224 | tf_op jit(solution)/shard_map/ppermute | solution.py:270
  59.5 8.9 %collective-permute-start.4 = (bf16[32,2048]{1,0:T(8,128)(2,1)S(1)}, bf16[32,2048]{1,0:T(8,128)(2,1)S(1)}, u32[]{:S(2)}, u32[]{:S(2)}) collective-permute-start(bf16[32,2048]{1,0:T(8,128)(2,1)S(1)} %get-tuple-element.39), channel_id=1, source_target_pairs={{0,6},{1,7},{2,4},{3,5},{4,2},{5,3},{6,0},{7,1},{8,14},{9,15},{10,... | collective-permute-start | bytes 393224 | tf_op jit(solution)/shard_map/ppermute | solution.py:270
  68.5 7.6 %collective-permute-start.8 = (bf16[16,2048]{1,0:T(8,128)(2,1)S(1)}, bf16[16,2048]{1,0:T(8,128)(2,1)S(1)}, u32[]{:S(2)}, u32[]{:S(2)}) collective-permute-start(bf16[16,2048]{1,0:T(8,128)(2,1)S(1)} %slice.79), channel_id=1, source_target_pairs={{0,14},{1,15},{2,12},{3,13},{4,10},{5,11},{6,8},{7,9},{8,6},{9,7},... | collective-permute-start | bytes 196616 | tf_op jit(solution)/shard_map/ppermute | solution.py:270
  77.1 7.6 %collective-permute-start.9 = (bf16[16,2176]{1,0:T(8,128)(2,1)S(1)}, bf16[16,2176]{1,0:T(8,128)(2,1)S(1)}, u32[]{:S(2)}, u32[]{:S(2)}) collective-permute-start(bf16[16,2176]{1,0:T(8,128)(2,1)S(1)} %get-tuple-element.27.base), channel_id=1, source_target_pairs={{0,14},{1,15},{2,12},{3,13},{4,10},{5,11},{6,8},{7,9},{8,6},{9,7},... | collective-permute-start | bytes 208904 | tf_op jit(solution)/shard_map/ppermute | solution.py:270
  84.7 11.7 %collective-permute-start.12 = (bf16[32,2176]{1,0:T(8,128)(2,1)S(1)}, bf16[32,2176]{1,0:T(8,128)(2,1)S(1)}, u32[]{:S(2)}, u32[]{:S(2)}) collective-permute-start(bf16[32,2176]{1,0:T(8,128)(2,1)S(1)} %constant_dynamic-update-slice_fusion.refs_6_), channel_id=1, source_target_pairs={{0,6},{1,7},{2,4},{3,5},{4,2},{5,3},{6,0},{7,1},{8,14},{9,15},{10,... | collective-permute-start | bytes 417800 | tf_op jit(solution)/shard_map/ppermute | solution.py:270
  88.3 9.6 %collective-permute-start.11 = (bf16[32,2176]{1,0:T(8,128)(2,1)S(1)}, bf16[32,2176]{1,0:T(8,128)(2,1)S(1)}, u32[]{:S(2)}, u32[]{:S(2)}) collective-permute-start(bf16[32,2176]{1,0:T(8,128)(2,1)S(1)} %constant_dynamic-update-slice_fusion.refs_6_), channel_id=1, source_target_pairs={{0,4},{1,5},{2,6},{3,7},{4,0},{5,1},{6,2},{7,3},{8,12},{9,13},{10,... | collective-permute-start | bytes 417800 | tf_op jit(solution)/shard_map/ppermute | solution.py:270
  88.3 10.3 %collective-permute-start.10 = (bf16[32,2176]{1,0:T(8,128)(2,1)S(1)}, bf16[32,2176]{1,0:T(8,128)(2,1)S(1)}, u32[]{:S(2)}, u32[]{:S(2)}) collective-permute-start(bf16[32,2176]{1,0:T(8,128)(2,1)S(1)} %constant_dynamic-update-slice_fusion.refs_6_), channel_id=1, source_target_pairs={{0,2},{1,3},{2,0},{3,1},{4,6},{5,7},{6,4},{7,5},{8,10},{9,11},{10,... | collective-permute-start | bytes 417800 | tf_op jit(solution)/shard_map/ppermute | solution.py:270
  89.9 10.1 %collective-permute-start.13 = (bf16[32,2176]{1,0:T(8,128)(2,1)S(1)}, bf16[32,2176]{1,0:T(8,128)(2,1)S(1)}, u32[]{:S(2)}, u32[]{:S(2)}) collective-permute-start(bf16[32,2176]{1,0:T(8,128)(2,1)S(1)} %constant_dynamic-update-slice_fusion.refs_6_), channel_id=1, source_target_pairs={{0,1},{1,0},{2,3},{3,2},{4,5},{5,4},{6,7},{7,6},{8,9},{9,8},{10,11... | collective-permute-start | bytes 417800 | tf_op jit(solution)/shard_map/ppermute | solution.py:270
  96.5 6.5 %collective-permute-start.16 = (bf16[32,2176]{1,0:T(8,128)(2,1)S(1)}, bf16[32,2176]{1,0:T(8,128)(2,1)S(1)}, u32[]{:S(2)}, u32[]{:S(2)}) collective-permute-start(bf16[32,2176]{1,0:T(8,128)(2,1)S(1)} %collective-permute-done.12.refs_9_), channel_id=1, source_target_pairs={{0,1},{1,0},{2,3},{3,2},{4,5},{5,4},{6,7},{7,6},{8,9},{9,8},{10,11... | collective-permute-start | bytes 417800 | tf_op jit(solution)/shard_map/ppermute | solution.py:270
  97.9 8.1 %collective-permute-start.15 = (bf16[32,2176]{1,0:T(8,128)(2,1)S(1)}, bf16[32,2176]{1,0:T(8,128)(2,1)S(1)}, u32[]{:S(2)}, u32[]{:S(2)}) collective-permute-start(bf16[32,2176]{1,0:T(8,128)(2,1)S(1)} %collective-permute-done.11.refs_8_), channel_id=1, source_target_pairs={{0,1},{1,0},{2,3},{3,2},{4,5},{5,4},{6,7},{7,6},{8,9},{9,8},{10,11... | collective-permute-start | bytes 417800 | tf_op jit(solution)/shard_map/ppermute | solution.py:270
  98.7 9.3 %collective-permute-start.14 = (bf16[32,2176]{1,0:T(8,128)(2,1)S(1)}, bf16[32,2176]{1,0:T(8,128)(2,1)S(1)}, u32[]{:S(2)}, u32[]{:S(2)}) collective-permute-start(bf16[32,2176]{1,0:T(8,128)(2,1)S(1)} %collective-permute-done.10.refs_7_), channel_id=1, source_target_pairs={{0,1},{1,0},{2,3},{3,2},{4,5},{5,4},{6,7},{7,6},{8,9},{9,8},{10,11... | collective-permute-start | bytes 417800 | tf_op jit(solution)/shard_map/ppermute | solution.py:270
  115.1 11.6 %collective-permute-start.20 = (bf16[64,2048]{1,0:T(8,128)(2,1)S(1)}, bf16[64,2048]{1,0:T(8,128)(2,1)S(1)}, u32[]{:S(2)}, u32[]{:S(2)}) collective-permute-start(bf16[64,2048]{1,0:T(8,128)(2,1)S(1)} %get-tuple-element.31), channel_id=1, source_target_pairs={{0,1},{1,0},{2,3},{3,2},{4,5},{5,4},{6,7},{7,6},{8,9},{9,8},{10,11... | collective-permute-start | bytes 786440 | tf_op jit(solution)/shard_map/ppermute | solution.py:270
  116.6 10.1 %collective-permute-start.18 = (bf16[32,2048]{1,0:T(8,128)(2,1)S(1)}, bf16[32,2048]{1,0:T(8,128)(2,1)S(1)}, u32[]{:S(2)}, u32[]{:S(2)}) collective-permute-start(bf16[32,2048]{1,0:T(8,128)(2,1)S(1)} %get-tuple-element.30), channel_id=1, source_target_pairs={{0,1},{1,0},{2,3},{3,2},{4,5},{5,4},{6,7},{7,6},{8,9},{9,8},{10,11... | collective-permute-start | bytes 393224 | tf_op jit(solution)/shard_map/ppermute | solution.py:270
  117.2 13.2 %collective-permute-start.17 = (bf16[32,2048]{1,0:T(8,128)(2,1)S(1)}, bf16[32,2048]{1,0:T(8,128)(2,1)S(1)}, u32[]{:S(2)}, u32[]{:S(2)}) collective-permute-start(bf16[32,2048]{1,0:T(8,128)(2,1)S(1)} %get-tuple-element.29), channel_id=1, source_target_pairs={{0,1},{1,0},{2,3},{3,2},{4,5},{5,4},{6,7},{7,6},{8,9},{9,8},{10,11... | collective-permute-start | bytes 393224 | tf_op jit(solution)/shard_map/ppermute | solution.py:270
  126.8 6.1 %collective-permute-start.21 = (bf16[32,2048]{1,0:T(8,128)(2,1)S(1)}, bf16[32,2048]{1,0:T(8,128)(2,1)S(1)}, u32[]{:S(2)}, u32[]{:S(2)}) collective-permute-start(bf16[32,2048]{1,0:T(8,128)(2,1)S(1)} %get-tuple-element.34), channel_id=1, source_target_pairs={{0,4},{1,5},{2,6},{3,7},{4,0},{5,1},{6,2},{7,3},{8,12},{9,13},{10,... | collective-permute-start | bytes 393224 | tf_op jit(solution)/shard_map/ppermute | solution.py:270
  126.9 7.0 %collective-permute-start.22 = (bf16[32,2048]{1,0:T(8,128)(2,1)S(1)}, bf16[32,2048]{1,0:T(8,128)(2,1)S(1)}, u32[]{:S(2)}, u32[]{:S(2)}) collective-permute-start(bf16[32,2048]{1,0:T(8,128)(2,1)S(1)} %get-tuple-element.35), channel_id=1, source_target_pairs={{0,2},{1,3},{2,0},{3,1},{4,6},{5,7},{6,4},{7,5},{8,10},{9,11},{10,... | collective-permute-start | bytes 393224 | tf_op jit(solution)/shard_map/ppermute | solution.py:270
  128.9 9.5 %collective-permute-start.19 = (bf16[32,2048]{1,0:T(8,128)(2,1)S(1)}, bf16[32,2048]{1,0:T(8,128)(2,1)S(1)}, u32[]{:S(2)}, u32[]{:S(2)}) collective-permute-start(bf16[32,2048]{1,0:T(8,128)(2,1)S(1)} %get-tuple-element.38), channel_id=1, source_target_pairs={{0,6},{1,7},{2,4},{3,5},{4,2},{5,3},{6,0},{7,1},{8,14},{9,15},{10,... | collective-permute-start | bytes 393224 | tf_op jit(solution)/shard_map/ppermute | solution.py:270
  138.5 7.6 %collective-permute-start.23 = (bf16[16,2048]{1,0:T(8,128)(2,1)S(1)}, bf16[16,2048]{1,0:T(8,128)(2,1)S(1)}, u32[]{:S(2)}, u32[]{:S(2)}) collective-permute-start(bf16[16,2048]{1,0:T(8,128)(2,1)S(1)} %slice.78), channel_id=1, source_target_pairs={{0,14},{1,15},{2,12},{3,13},{4,10},{5,11},{6,8},{7,9},{8,6},{9,7},... | collective-permute-start | bytes 196616 | tf_op jit(solution)/shard_map/ppermute | solution.py:270
  146.3 7.4 %collective-permute-start.24 = (bf16[16,2048]{1,0:T(8,128)(2,1)S(1)}, bf16[16,2048]{1,0:T(8,128)(2,1)S(1)}, u32[]{:S(2)}, u32[]{:S(2)}) collective-permute-start(bf16[16,2048]{1,0:T(8,128)(2,1)S(1)} %shard_map.101), channel_id=1, source_target_pairs={{0,14},{1,15},{2,12},{3,13},{4,10},{5,11},{6,8},{7,9},{8,6},{9,7},... | collective-permute-start | bytes 196616 | tf_op jit(solution)/shard_map/ppermute | solution.py:270
  153.7 7.4 %collective-permute-start.27 = (bf16[32,2048]{1,0:T(8,128)(2,1)S(1)}, bf16[32,2048]{1,0:T(8,128)(2,1)S(1)}, u32[]{:S(2)}, u32[]{:S(2)}) collective-permute-start(bf16[32,2048]{1,0:T(8,128)(2,1)S(1)} %pad_maximum_fusion.refs_0_), channel_id=1, source_target_pairs={{0,6},{1,7},{2,4},{3,5},{4,2},{5,3},{6,0},{7,1},{8,14},{9,15},{10,... | collective-permute-start | bytes 393224 | tf_op jit(solution)/shard_map/ppermute | solution.py:270
  153.8 8.7 %collective-permute-start.26 = (bf16[32,2048]{1,0:T(8,128)(2,1)S(1)}, bf16[32,2048]{1,0:T(8,128)(2,1)S(1)}, u32[]{:S(2)}, u32[]{:S(2)}) collective-permute-start(bf16[32,2048]{1,0:T(8,128)(2,1)S(1)} %pad_maximum_fusion.refs_0_), channel_id=1, source_target_pairs={{0,4},{1,5},{2,6},{3,7},{4,0},{5,1},{6,2},{7,3},{8,12},{9,13},{10,... | collective-permute-start | bytes 393224 | tf_op jit(solution)/shard_map/ppermute | solution.py:270
  153.9 9.3 %collective-permute-start.25 = (bf16[32,2048]{1,0:T(8,128)(2,1)S(1)}, bf16[32,2048]{1,0:T(8,128)(2,1)S(1)}, u32[]{:S(2)}, u32[]{:S(2)}) collective-permute-start(bf16[32,2048]{1,0:T(8,128)(2,1)S(1)} %pad_maximum_fusion.refs_0_), channel_id=1, source_target_pairs={{0,2},{1,3},{2,0},{3,1},{4,6},{5,7},{6,4},{7,5},{8,10},{9,11},{10,... | collective-permute-start | bytes 393224 | tf_op jit(solution)/shard_map/ppermute | solution.py:270
  157.2 7.9 %collective-permute-start.28 = (bf16[32,2048]{1,0:T(8,128)(2,1)S(1)}, bf16[32,2048]{1,0:T(8,128)(2,1)S(1)}, u32[]{:S(2)}, u32[]{:S(2)}) collective-permute-start(bf16[32,2048]{1,0:T(8,128)(2,1)S(1)} %pad_maximum_fusion.refs_0_), channel_id=1, source_target_pairs={{0,1},{1,0},{2,3},{3,2},{4,5},{5,4},{6,7},{7,6},{8,9},{9,8},{10,11... | collective-permute-start | bytes 393224 | tf_op jit(solution)/shard_map/ppermute | solution.py:270
  161.1 5.0 %collective-permute-start.31 = (bf16[32,2048]{1,0:T(8,128)(2,1)S(1)}, bf16[32,2048]{1,0:T(8,128)(2,1)S(1)}, u32[]{:S(2)}, u32[]{:S(2)}) collective-permute-start(bf16[32,2048]{1,0:T(8,128)(2,1)S(1)} %collective-permute-done.27.refs_3_), channel_id=1, source_target_pairs={{0,1},{1,0},{2,3},{3,2},{4,5},{5,4},{6,7},{7,6},{8,9},{9,8},{10,11... | collective-permute-start | bytes 393224 | tf_op jit(solution)/shard_map/ppermute | solution.py:270
  162.4 5.0 %collective-permute-start.30 = (bf16[32,2048]{1,0:T(8,128)(2,1)S(1)}, bf16[32,2048]{1,0:T(8,128)(2,1)S(1)}, u32[]{:S(2)}, u32[]{:S(2)}) collective-permute-start(bf16[32,2048]{1,0:T(8,128)(2,1)S(1)} %collective-permute-done.26.refs_2_), channel_id=1, source_target_pairs={{0,1},{1,0},{2,3},{3,2},{4,5},{5,4},{6,7},{7,6},{8,9},{9,8},{10,11... | collective-permute-start | bytes 393224 | tf_op jit(solution)/shard_map/ppermute | solution.py:270
  163.1 5.7 %collective-permute-start.29 = (bf16[32,2048]{1,0:T(8,128)(2,1)S(1)}, bf16[32,2048]{1,0:T(8,128)(2,1)S(1)}, u32[]{:S(2)}, u32[]{:S(2)}) collective-permute-start(bf16[32,2048]{1,0:T(8,128)(2,1)S(1)} %collective-permute-done.25.refs_1_), channel_id=1, source_target_pairs={{0,1},{1,0},{2,3},{3,2},{4,5},{5,4},{6,7},{7,6},{8,9},{9,8},{10,11... | collective-permute-start | bytes 393224 | tf_op jit(solution)/shard_map/ppermute | solution.py:270

commit v4 on v3

--- a/solution.py
+++ b/solution.py
@@ -271,24 +271,29 @@
 
 
 def sum_to_owner(keep, gives):
-    part = {}
+    part, waiting = {}, []
     for hops, give in zip(GIVE, gives):
+        give, *ready = lax.optimization_barrier((give, *[part[hop] for hop in waiting]))
+        part.update(zip(waiting, ready))
         got = swap(give, SIDE)
         for n, hop in enumerate(hops):
             at = NEAR.index(hop) * 2 * OWN
-            part[hop] = keep[at : at + 2 * OWN] + got[2 * n * OWN : 2 * (n + 1) * OWN]
+            total = keep[at : at + 2 * OWN] + got[2 * n * OWN : 2 * (n + 1) * OWN]
+            part[hop] = total.astype(jnp.bfloat16) if hop else total
+        waiting = hops
     total = part[0]
     for hop in (6, 4, 2):
-        total = total + swap(part[hop].astype(jnp.bfloat16), hop)
+        total = total + swap(part[hop], hop)
     return total, swap(total[OWN:].astype(jnp.bfloat16), MIRROR)
 
 
 def gather_rows(own):
     pair = jnp.concatenate([own, swap(own, MIRROR)], axis=0)
-    got = {0: pair}
-    for hop in (2, 6, 4):
-        got[hop] = swap(pair, hop)
-    return [got[hop] for hop in NEAR] + [swap(got[hop], SIDE) for hop in NEAR]
+    got = {0: pair, 2: swap(pair, 2), 6: swap(pair, 6)}
+    beside = swap(pair, SIDE)
+    pair, *_ = lax.optimization_barrier((pair, got[6], beside))
+    got[4] = swap(pair, 4)
+    return [got[hop] for hop in NEAR] + [beside] + [swap(got[hop], SIDE) for hop in NEAR[1:]]
 
 
 def on_device(

time: 172 us -> 176 us (1.023)
  waiting for transfers between devices: 91.1 us -> 92.9 us
    ppermute x30, waiting for transfers between devices: 60 us -> 61.8 us  [swap(): return lax.ppermute(block, 'people', [(i, i ^ hop) for i in range(count)])]
  transfers between devices with their start and end apart: 32 -> 32, of which waited for: 22 -> 26; matrix products, arithmetic and copies ran while one was open for 0% -> 0% of each run, Pallas kernels for 3% -> 3%
where the time goes in v4:
time: 176 us; the launch traced here: 173 us
  waiting for transfers between devices  92.9 us (53%)
  starting transfers between devices  55.8 us (32%)
  Pallas kernels  22.1 us (13%)
    ppermute x30, waiting for transfers between devices, swap(): return lax.ppermute(block, 'people', [(i, i ^ hop) for i in range(count)])  61.8 us
    ppermute x30, starting transfers between devices, swap(): return lax.ppermute(block, 'people', [(i, i ^ hop) for i in range(count)])  53 us
    ppermute x1, waiting for transfers between devices, on_device(): slow = lax.ppermute(away, 'genome', beyond)  30.3 us
    pallas_call x2, Pallas kernels, local_grad(): pl.pallas_call(functools.partial(turn_kernel, len(pieces)), out_shape=out...  11.7 us
  transfers between devices with their start and end apart: 32, of which 26 were waited for; matrix products, arithmetic and copies ran while one was open for 0% of the time, Pallas kernels for 3%

profile of v4, /device:TPU:56, one launch (start us, length us, event | category | flops | bytes accessed | tf_op | source)
XLA Modules:
  0.0 172.7 jit_solution(14941405961669701720)
XLA Ops:
  0.7 3.0 %shard_map.96 = (bf16[3072,512]{1,0:T(8,128)(2,1)S(1)}, bf16[3072,512]{1,0:T(8,128)(2,1)S(1)}) custom-call(s32[1]{0:T(128)} %bitcast.where.refs_0_, bf16[3072,1024]{1,0:T(8,128)(2,1)} %whole.1), custom_call_target="tpu_custom_call" | custom-call | tf_op jit(solution)/shard_map/pallas_call | solution.py:208
  3.8 2.7 %collective-permute-start = (bf16[3072,512]{1,0:T(8,128)(2,1)S(1)}, bf16[3072,512]{1,0:T(8,128)(2,1)S(1)}, u32[]{:S(2)}, u32[]{:S(2)}) collective-permute-start(bf16[3072,512]{1,0:T(8,128)(2,1)S(1)} %get-tuple-element.31.second.refs_2_), channel_id=1, source_target_pairs={{16,32},{32,16},{48,64},{64,48},{80,96},{96,80},{112,128},{128,112... | collective-permute-start | bytes 9437192 | tf_op jit(solution)/shard_map/ppermute | solution.py:321
  6.6 2.1 %shard_map.95 = (f32[256,128]{1,0:T(8,128)S(1)}, bf16[256,2048]{1,0:T(8,128)(2,1)S(1)}, f32[16,2048]{1,0:T(8,128)S(1)}) custom-call(s32[1]{0:T(128)} %bitcast.where.refs_0_, s32[16,256]{1,0:T(8,128)S(1)} %bitcast.8, s32[1,256]{1,0:T(1,128)S(1)} %bitcast.9, s32[1,256]{1,0:T(1,128)S(1)} %bitcast.10, f32[1,256]{1,0:T(1,128)S(1)} %bitcast.11, ...), custom_call_target="tpu_custom_call" | custom-call | tf_op jit(solution)/shard_map/pallas_call | solution.py:258
  8.7 0.8 collective-permute-done.1.fourth.refs_4_
  9.5 2.6 %shard_map.97.refs_5_ = f32[3072,256]{1,0:T(8,128)S(1)} custom-call(s32[1]{0:T(128)} %bitcast.where.refs_0_, bf16[3072,512]{1,0:T(8,128)(2,1)S(1)} %get-tuple-element.31.second.refs_2_, bf16[3072,512]{1,0:T(8,128)(2,1)S(1)} %get-tuple-element.32.third.refs_3_, bf16[3072,512]{1,0:T(8,128)(2,1)S(1)} %collective-permute-done.1.fourth.refs_4_, ...), custom_call_target="tpu_custom_call" | custom-call | tf_op jit(solution)/shard_map/pallas_call | solution.py:225
  12.1 30.3 %collective-permute-done.refs_1_ = bf16[3072,512]{1,0:T(8,128)(2,1)S(1)} collective-permute-done((bf16[3072,512]{1,0:T(8,128)(2,1)S(1)}, bf16[3072,512]{1,0:T(8,128)(2,1)S(1)}, u32[]{:S(2)}, u32[]{:S(2)}) %collective-permute-start) | collective-permute-done | bytes 3145760 | tf_op jit(solution)/shard_map/ppermute | solution.py:321
  42.4 4.6 %shard_map.98 = (f32[128,2048]{1,0:T(8,128)S(1)}, bf16[32,2048]{1,0:T(8,128)(2,1)S(1)}, bf16[64,2048]{1,0:T(8,128)(2,1)S(1)}, bf16[32,2048]{1,0:T(8,128)(2,1)S(1)}) custom-call(s32[1]{0:T(128)} %bitcast.where.refs_0_, bf16[3072,512]{1,0:T(8,128)(2,1)S(1)} %collective-permute-done.refs_1_, bf16[3072,512]{1,0:T(8,128)(2,1)S(1)} %get-tuple-element.31.second.refs_2_, ...), custom_call_target="tpu_custom_call" | custom-call | flops 6442450944 | tf_op jit(solution)/shard_map/pallas_call | solution.py:246
  47.0 1.6 collective-permute-start.2
  48.6 3.5 %collective-permute-done.2 = bf16[32,2048]{1,0:T(8,128)(2,1)S(1)} collective-permute-done((bf16[32,2048]{1,0:T(8,128)(2,1)S(1)}, bf16[32,2048]{1,0:T(8,128)(2,1)S(1)}, u32[]{:S(2)}, u32[]{:S(2)}) %collective-permute-start.2) | collective-permute-done | bytes 131104 | tf_op jit(solution)/shard_map/ppermute | solution.py:270
  52.1 1.6 collective-permute-start.3
  53.7 1.9 %collective-permute-start.5 = (bf16[32,2048]{1,0:T(8,128)(2,1)S(1)}, bf16[32,2048]{1,0:T(8,128)(2,1)S(1)}, u32[]{:S(2)}, u32[]{:S(2)}) collective-permute-start(bf16[32,2048]{1,0:T(8,128)(2,1)S(1)} %add_convert_fusion.5), channel_id=1, source_target_pairs={{0,6},{1,7},{2,4},{3,5},{4,2},{5,3},{6,0},{7,1},{8,14},{9,15},{10,... | collective-permute-start | bytes 393224 | tf_op jit(solution)/shard_map/ppermute | solution.py:270
  55.6 3.7 %collective-permute-done.3 = bf16[64,2048]{1,0:T(8,128)(2,1)S(1)} collective-permute-done((bf16[64,2048]{1,0:T(8,128)(2,1)S(1)}, bf16[64,2048]{1,0:T(8,128)(2,1)S(1)}, u32[]{:S(2)}, u32[]{:S(2)}) %collective-permute-start.3) | collective-permute-done | bytes 262176 | tf_op jit(solution)/shard_map/ppermute | solution.py:270
  59.4 1.6 collective-permute-start.4
  61.0 3.3 %collective-permute-start.6 = (bf16[32,2048]{1,0:T(8,128)(2,1)S(1)}, bf16[32,2048]{1,0:T(8,128)(2,1)S(1)}, u32[]{:S(2)}, u32[]{:S(2)}) collective-permute-start(bf16[32,2048]{1,0:T(8,128)(2,1)S(1)} %get-tuple-element.41), channel_id=1, source_target_pairs={{0,4},{1,5},{2,6},{3,7},{4,0},{5,1},{6,2},{7,3},{8,12},{9,13},{10,... | collective-permute-start | bytes 393224 | tf_op jit(solution)/shard_map/ppermute | solution.py:270
  64.2 0.1 collective-permute-start.7
  64.4 0.6 collective-permute-done.4
  65.0 5.5 %collective-permute-done.6 = bf16[32,2048]{1,0:T(8,128)(2,1)S(1)} collective-permute-done((bf16[32,2048]{1,0:T(8,128)(2,1)S(1)}, bf16[32,2048]{1,0:T(8,128)(2,1)S(1)}, u32[]{:S(2)}, u32[]{:S(2)}) %collective-permute-start.6) | collective-permute-done | bytes 131104 | tf_op jit(solution)/shard_map/ppermute | solution.py:270
  70.4 0.6 collective-permute-done.7
  71.1 5.0 %collective-permute-start.8 = (bf16[16,2048]{1,0:T(8,128)(2,1)S(1)}, bf16[16,2048]{1,0:T(8,128)(2,1)S(1)}, u32[]{:S(2)}, u32[]{:S(2)}) collective-permute-start(bf16[16,2048]{1,0:T(8,128)(2,1)S(1)} %slice.79), channel_id=1, source_target_pairs={{0,14},{1,15},{2,12},{3,13},{4,10},{5,11},{6,8},{7,9},{8,6},{9,7},... | collective-permute-start | bytes 196616 | tf_op jit(solution)/shard_map/ppermute | solution.py:270
  76.1 2.7 %collective-permute-done.8.far = bf16[16,2048]{1,0:T(8,128)(2,1)S(1)} collective-permute-done((bf16[16,2048]{1,0:T(8,128)(2,1)S(1)}, bf16[16,2048]{1,0:T(8,128)(2,1)S(1)}, u32[]{:S(2)}, u32[]{:S(2)}) %collective-permute-start.8) | collective-permute-done | bytes 65568 | tf_op jit(solution)/shard_map/ppermute | solution.py:270
  78.8 1.0 shard_map.99
  79.8 5.0 %collective-permute-start.9 = (bf16[16,2176]{1,0:T(8,128)(2,1)S(1)}, bf16[16,2176]{1,0:T(8,128)(2,1)S(1)}, u32[]{:S(2)}, u32[]{:S(2)}) collective-permute-start(bf16[16,2176]{1,0:T(8,128)(2,1)S(1)} %get-tuple-element.44.base), channel_id=1, source_target_pairs={{0,14},{1,15},{2,12},{3,13},{4,10},{5,11},{6,8},{7,9},{8,6},{9,7},... | collective-permute-start | bytes 208904 | tf_op jit(solution)/shard_map/ppermute | solution.py:270
  84.8 2.6 %collective-permute-done.9 = bf16[16,2176]{1,0:T(8,128)(2,1)S(1)} collective-permute-done((bf16[16,2176]{1,0:T(8,128)(2,1)S(1)}, bf16[16,2176]{1,0:T(8,128)(2,1)S(1)}, u32[]{:S(2)}, u32[]{:S(2)}) %collective-permute-start.9) | collective-permute-done | bytes 69664 | tf_op jit(solution)/shard_map/ppermute | solution.py:270
  87.5 0.6 collective-permute-start.12
  88.1 1.0 collective-permute-start.11
  89.1 2.1 %collective-permute-start.10 = (bf16[32,2176]{1,0:T(8,128)(2,1)S(1)}, bf16[32,2176]{1,0:T(8,128)(2,1)S(1)}, u32[]{:S(2)}, u32[]{:S(2)}) collective-permute-start(bf16[32,2176]{1,0:T(8,128)(2,1)S(1)} %constant_dynamic-update-slice_fusion.refs_6_), channel_id=1, source_target_pairs={{0,2},{1,3},{2,0},{3,1},{4,6},{5,7},{6,4},{7,5},{8,10},{9,11},{10,... | collective-permute-start | bytes 417800 | tf_op jit(solution)/shard_map/ppermute | solution.py:270
  91.2 1.4 collective-permute-done.12.refs_10_
  92.6 3.4 %collective-permute-done.11.refs_9_ = bf16[32,2176]{1,0:T(8,128)(2,1)S(1)} collective-permute-done((bf16[32,2176]{1,0:T(8,128)(2,1)S(1)}, bf16[32,2176]{1,0:T(8,128)(2,1)S(1)}, u32[]{:S(2)}, u32[]{:S(2)}) %collective-permute-start.11) | collective-permute-done | bytes 139296 | tf_op jit(solution)/shard_map/ppermute | solution.py:270
  96.0 2.2 %collective-permute-start.13 = (bf16[32,2176]{1,0:T(8,128)(2,1)S(1)}, bf16[32,2176]{1,0:T(8,128)(2,1)S(1)}, u32[]{:S(2)}, u32[]{:S(2)}) collective-permute-start(bf16[32,2176]{1,0:T(8,128)(2,1)S(1)} %constant_dynamic-update-slice_fusion.refs_6_), channel_id=1, source_target_pairs={{0,4},{1,5},{2,6},{3,7},{4,0},{5,1},{6,2},{7,3},{8,12},{9,13},{10,... | collective-permute-start | bytes 417800 | tf_op jit(solution)/shard_map/ppermute | solution.py:270
  98.1 1.6 collective-permute-start.16
  99.7 0.6 collective-permute-start.14
  100.3 1.8 %collective-permute-done.13.refs_8_ = bf16[32,2176]{1,0:T(8,128)(2,1)S(1)} collective-permute-done((bf16[32,2176]{1,0:T(8,128)(2,1)S(1)}, bf16[32,2176]{1,0:T(8,128)(2,1)S(1)}, u32[]{:S(2)}, u32[]{:S(2)}) %collective-permute-start.13) | collective-permute-done | bytes 139296 | tf_op jit(solution)/shard_map/ppermute | solution.py:270
  102.0 1.5 collective-permute-start.15
  103.5 0.9 collective-permute-done.16.refs_13_
  104.4 1.5 collective-permute-done.14.refs_11_
  105.9 1.5 collective-permute-done.15.refs_12_
  107.4 7.1 %shard_map.100 = (f32[128,2048]{1,0:T(8,128)S(1)}, bf16[32,2048]{1,0:T(8,128)(2,1)S(1)}, bf16[64,2048]{1,0:T(8,128)(2,1)S(1)}, bf16[32,2048]{1,0:T(8,128)(2,1)S(1)}, f32[16,256]{1,0:T(8,128)S(1)}) custom-call(s32[1]{0:T(128)} %bitcast.where.refs_0_, bf16[3072,512]{1,0:T(8,128)(2,1)S(1)} %collective-permute-done.refs_1_, ...), custom_call_target="tpu_custom_call" | custom-call | flops 6442450944 | tf_op jit(solution)/shard_map/pallas_call | solution.py:246
  114.5 1.8 %collective-permute-start.17 = (bf16[32,2048]{1,0:T(8,128)(2,1)S(1)}, bf16[32,2048]{1,0:T(8,128)(2,1)S(1)}, u32[]{:S(2)}, u32[]{:S(2)}) collective-permute-start(bf16[32,2048]{1,0:T(8,128)(2,1)S(1)} %get-tuple-element.49), channel_id=1, source_target_pairs={{0,1},{1,0},{2,3},{3,2},{4,5},{5,4},{6,7},{7,6},{8,9},{9,8},{10,11... | collective-permute-start | bytes 393224 | tf_op jit(solution)/shard_map/ppermute | solution.py:270
  116.4 4.6 %collective-permute-done.17 = bf16[32,2048]{1,0:T(8,128)(2,1)S(1)} collective-permute-done((bf16[32,2048]{1,0:T(8,128)(2,1)S(1)}, bf16[32,2048]{1,0:T(8,128)(2,1)S(1)}, u32[]{:S(2)}, u32[]{:S(2)}) %collective-permute-start.17) | collective-permute-done | bytes 131104 | tf_op jit(solution)/shard_map/ppermute | solution.py:270
  121.0 1.8 %collective-permute-start.18 = (bf16[64,2048]{1,0:T(8,128)(2,1)S(1)}, bf16[64,2048]{1,0:T(8,128)(2,1)S(1)}, u32[]{:S(2)}, u32[]{:S(2)}) collective-permute-start(bf16[64,2048]{1,0:T(8,128)(2,1)S(1)} %get-tuple-element.50), channel_id=1, source_target_pairs={{0,1},{1,0},{2,3},{3,2},{4,5},{5,4},{6,7},{7,6},{8,9},{9,8},{10,11... | collective-permute-start | bytes 786440 | tf_op jit(solution)/shard_map/ppermute | solution.py:270
  122.8 0.9 collective-permute-start.20
  123.8 5.1 %collective-permute-done.18 = bf16[64,2048]{1,0:T(8,128)(2,1)S(1)} collective-permute-done((bf16[64,2048]{1,0:T(8,128)(2,1)S(1)}, bf16[64,2048]{1,0:T(8,128)(2,1)S(1)}, u32[]{:S(2)}, u32[]{:S(2)}) %collective-permute-start.18) | collective-permute-done | bytes 262176 | tf_op jit(solution)/shard_map/ppermute | solution.py:270
  128.9 1.8 %collective-permute-start.19 = (bf16[32,2048]{1,0:T(8,128)(2,1)S(1)}, bf16[32,2048]{1,0:T(8,128)(2,1)S(1)}, u32[]{:S(2)}, u32[]{:S(2)}) collective-permute-start(bf16[32,2048]{1,0:T(8,128)(2,1)S(1)} %get-tuple-element.51), channel_id=1, source_target_pairs={{0,1},{1,0},{2,3},{3,2},{4,5},{5,4},{6,7},{7,6},{8,9},{9,8},{10,11... | collective-permute-start | bytes 393224 | tf_op jit(solution)/shard_map/ppermute | solution.py:270
  130.8 1.8 %collective-permute-start.21 = (bf16[32,2048]{1,0:T(8,128)(2,1)S(1)}, bf16[32,2048]{1,0:T(8,128)(2,1)S(1)}, u32[]{:S(2)}, u32[]{:S(2)}) collective-permute-start(bf16[32,2048]{1,0:T(8,128)(2,1)S(1)} %get-tuple-element.53), channel_id=1, source_target_pairs={{0,4},{1,5},{2,6},{3,7},{4,0},{5,1},{6,2},{7,3},{8,12},{9,13},{10,... | collective-permute-start | bytes 393224 | tf_op jit(solution)/shard_map/ppermute | solution.py:270
  132.5 0.6 collective-permute-start.22
  133.2 0.8 collective-permute-done.19
  134.0 2.7 %collective-permute-done.21 = bf16[32,2048]{1,0:T(8,128)(2,1)S(1)} collective-permute-done((bf16[32,2048]{1,0:T(8,128)(2,1)S(1)}, bf16[32,2048]{1,0:T(8,128)(2,1)S(1)}, u32[]{:S(2)}, u32[]{:S(2)}) %collective-permute-start.21) | collective-permute-done | bytes 131104 | tf_op jit(solution)/shard_map/ppermute | solution.py:270
  136.7 0.9 collective-permute-done.22
  137.7 4.6 %collective-permute-start.23 = (bf16[16,2048]{1,0:T(8,128)(2,1)S(1)}, bf16[16,2048]{1,0:T(8,128)(2,1)S(1)}, u32[]{:S(2)}, u32[]{:S(2)}) collective-permute-start(bf16[16,2048]{1,0:T(8,128)(2,1)S(1)} %slice.78), channel_id=1, source_target_pairs={{0,14},{1,15},{2,12},{3,13},{4,10},{5,11},{6,8},{7,9},{8,6},{9,7},... | collective-permute-start | bytes 196616 | tf_op jit(solution)/shard_map/ppermute | solution.py:270
  142.3 3.5 %collective-permute-done.23.far = bf16[16,2048]{1,0:T(8,128)(2,1)S(1)} collective-permute-done((bf16[16,2048]{1,0:T(8,128)(2,1)S(1)}, bf16[16,2048]{1,0:T(8,128)(2,1)S(1)}, u32[]{:S(2)}, u32[]{:S(2)}) %collective-permute-start.23) | collective-permute-done | bytes 65568 | tf_op jit(solution)/shard_map/ppermute | solution.py:270
  145.8 0.2 shard_map.101
  146.0 3.9 %collective-permute-start.24 = (bf16[16,2048]{1,0:T(8,128)(2,1)S(1)}, bf16[16,2048]{1,0:T(8,128)(2,1)S(1)}, u32[]{:S(2)}, u32[]{:S(2)}) collective-permute-start(bf16[16,2048]{1,0:T(8,128)(2,1)S(1)} %shard_map.101), channel_id=1, source_target_pairs={{0,14},{1,15},{2,12},{3,13},{4,10},{5,11},{6,8},{7,9},{8,6},{9,7},... | collective-permute-start | bytes 196616 | tf_op jit(solution)/shard_map/ppermute | solution.py:270
  149.9 3.6 %collective-permute-done.24 = bf16[16,2048]{1,0:T(8,128)(2,1)S(1)} collective-permute-done((bf16[16,2048]{1,0:T(8,128)(2,1)S(1)}, bf16[16,2048]{1,0:T(8,128)(2,1)S(1)}, u32[]{:S(2)}, u32[]{:S(2)}) %collective-permute-start.24) | collective-permute-done | bytes 65568 | tf_op jit(solution)/shard_map/ppermute | solution.py:270
  153.6 1.8 %collective-permute-start.27 = (bf16[32,2048]{1,0:T(8,128)(2,1)S(1)}, bf16[32,2048]{1,0:T(8,128)(2,1)S(1)}, u32[]{:S(2)}, u32[]{:S(2)}) collective-permute-start(bf16[32,2048]{1,0:T(8,128)(2,1)S(1)} %pad_maximum_fusion.refs_0_), channel_id=1, source_target_pairs={{0,1},{1,0},{2,3},{3,2},{4,5},{5,4},{6,7},{7,6},{8,9},{9,8},{10,11... | collective-permute-start | bytes 393224 | tf_op jit(solution)/shard_map/ppermute | solution.py:270
  155.4 1.0 collective-permute-start.26
  156.4 2.8 %collective-permute-done.27.refs_4_ = bf16[32,2048]{1,0:T(8,128)(2,1)S(1)} collective-permute-done((bf16[32,2048]{1,0:T(8,128)(2,1)S(1)}, bf16[32,2048]{1,0:T(8,128)(2,1)S(1)}, u32[]{:S(2)}, u32[]{:S(2)}) %collective-permute-start.27) | collective-permute-done | bytes 131104 | tf_op jit(solution)/shard_map/ppermute | solution.py:270
  159.2 1.2 collective-permute-done.26.refs_3_
  160.4 1.5 collective-permute-start.31
  161.9 0.5 collective-permute-start.29
  162.4 3.8 %collective-permute-done.28.refs_2_ = bf16[32,2048]{1,0:T(8,128)(2,1)S(1)} collective-permute-done((bf16[32,2048]{1,0:T(8,128)(2,1)S(1)}, bf16[32,2048]{1,0:T(8,128)(2,1)S(1)}, u32[]{:S(2)}, u32[]{:S(2)}) %collective-permute-start.28) | collective-permute-done | bytes 131104 | tf_op jit(solution)/shard_map/ppermute | solution.py:270
  166.2 1.2 collective-permute-start.30
  167.4 0.6 copy.11
  168.0 3.2 %collective-permute-done.30.refs_6_ = bf16[32,2048]{1,0:T(8,128)(2,1)S(1)} collective-permute-done((bf16[32,2048]{1,0:T(8,128)(2,1)S(1)}, bf16[32,2048]{1,0:T(8,128)(2,1)S(1)}, u32[]{:S(2)}, u32[]{:S(2)}) %collective-permute-start.30) | collective-permute-done | bytes 131104 | tf_op jit(solution)/shard_map/ppermute | solution.py:270
  171.2 1.5 shard_map.102
  (34 shorter events, 0.5 us)
Async XLA Ops:
  0.6 5.9 %copy-start = (f32[256,2048]{1,0:T(8,128)S(1)}, f32[256,2048]{1,0:T(8,128)}, u32[]{:S(2)}) copy-start(f32[256,2048]{1,0:T(8,128)} %refs_4_.1) | copy-start | bytes 6291460
  0.6 5.9 %copy-start.2 = (s32[256,16]{0,1:T(8,128)S(1)}, s32[256,16]{0,1:T(8,128)}, u32[]{:S(2)}) copy-start(s32[256,16]{0,1:T(8,128)} %param.15) | copy-start | bytes 49156
  0.7 5.9 %copy-start.3 = (s32[256]{0:T(256)S(1)}, s32[256]{0:T(256)}, u32[]{:S(2)}) copy-start(s32[256]{0:T(256)} %param.13) | copy-start | bytes 3076
  0.7 5.9 %copy-start.4 = (s32[256]{0:T(256)S(1)}, s32[256]{0:T(256)}, u32[]{:S(2)}) copy-start(s32[256]{0:T(256)} %param.14) | copy-start | bytes 3076
  0.7 5.9 %copy-start.5 = (f32[256]{0:T(256)S(1)}, f32[256]{0:T(256)}, u32[]{:S(2)}) copy-start(f32[256]{0:T(256)} %param.11) | copy-start | bytes 3076
  0.7 5.9 %copy-start.6 = (f32[256]{0:T(256)S(1)}, f32[256]{0:T(256)}, u32[]{:S(2)}) copy-start(f32[256]{0:T(256)} %param.12) | copy-start | bytes 3076
  0.7 8.8 %copy-start.1 = (bf16[3072,256]{1,0:T(8,128)(2,1)S(1)}, bf16[3072,256]{1,0:T(8,128)(2,1)}, u32[]{:S(2)}) copy-start(bf16[3072,256]{1,0:T(8,128)(2,1)} %refs_5_.1) | copy-start | bytes 4718596
  3.7 5.7 %collective-permute-start.1 = (bf16[3072,512]{1,0:T(8,128)(2,1)S(1)}, bf16[3072,512]{1,0:T(8,128)(2,1)S(1)}, u32[]{:S(2)}, u32[]{:S(2)}) collective-permute-start(bf16[3072,512]{1,0:T(8,128)(2,1)S(1)} %get-tuple-element.32.third.refs_3_), channel_id=1, source_target_pairs={{0,16},{16,0},{32,48},{48,32},{64,80},{80,64},{96,112},{112,96},{1... | collective-permute-start | bytes 9437192 | tf_op jit(solution)/shard_map/ppermute | solution.py:322
  3.8 38.6 %collective-permute-start = (bf16[3072,512]{1,0:T(8,128)(2,1)S(1)}, bf16[3072,512]{1,0:T(8,128)(2,1)S(1)}, u32[]{:S(2)}, u32[]{:S(2)}) collective-permute-start(bf16[3072,512]{1,0:T(8,128)(2,1)S(1)} %get-tuple-element.31.second.refs_2_), channel_id=1, source_target_pairs={{16,32},{32,16},{48,64},{64,48},{80,96},{96,80},{112,128},{128,112... | collective-permute-start | bytes 9437192 | tf_op jit(solution)/shard_map/ppermute | solution.py:321
  47.0 5.1 %collective-permute-start.2 = (bf16[32,2048]{1,0:T(8,128)(2,1)S(1)}, bf16[32,2048]{1,0:T(8,128)(2,1)S(1)}, u32[]{:S(2)}, u32[]{:S(2)}) collective-permute-start(bf16[32,2048]{1,0:T(8,128)(2,1)S(1)} %get-tuple-element.37), channel_id=1, source_target_pairs={{0,1},{1,0},{2,3},{3,2},{4,5},{5,4},{6,7},{7,6},{8,9},{9,8},{10,11... | collective-permute-start | bytes 393224 | tf_op jit(solution)/shard_map/ppermute | solution.py:270
  52.1 7.2 %collective-permute-start.3 = (bf16[64,2048]{1,0:T(8,128)(2,1)S(1)}, bf16[64,2048]{1,0:T(8,128)(2,1)S(1)}, u32[]{:S(2)}, u32[]{:S(2)}) collective-permute-start(bf16[64,2048]{1,0:T(8,128)(2,1)S(1)} %get-tuple-element.38), channel_id=1, source_target_pairs={{0,1},{1,0},{2,3},{3,2},{4,5},{5,4},{6,7},{7,6},{8,9},{9,8},{10,11... | collective-permute-start | bytes 786440 | tf_op jit(solution)/shard_map/ppermute | solution.py:270
  53.7 10.7 %collective-permute-start.5 = (bf16[32,2048]{1,0:T(8,128)(2,1)S(1)}, bf16[32,2048]{1,0:T(8,128)(2,1)S(1)}, u32[]{:S(2)}, u32[]{:S(2)}) collective-permute-start(bf16[32,2048]{1,0:T(8,128)(2,1)S(1)} %add_convert_fusion.5), channel_id=1, source_target_pairs={{0,6},{1,7},{2,4},{3,5},{4,2},{5,3},{6,0},{7,1},{8,14},{9,15},{10,... | collective-permute-start | bytes 393224 | tf_op jit(solution)/shard_map/ppermute | solution.py:270
  59.4 5.6 %collective-permute-start.4 = (bf16[32,2048]{1,0:T(8,128)(2,1)S(1)}, bf16[32,2048]{1,0:T(8,128)(2,1)S(1)}, u32[]{:S(2)}, u32[]{:S(2)}) collective-permute-start(bf16[32,2048]{1,0:T(8,128)(2,1)S(1)} %get-tuple-element.39), channel_id=1, source_target_pairs={{0,1},{1,0},{2,3},{3,2},{4,5},{5,4},{6,7},{7,6},{8,9},{9,8},{10,11... | collective-permute-start | bytes 393224 | tf_op jit(solution)/shard_map/ppermute | solution.py:270
  61.0 9.5 %collective-permute-start.6 = (bf16[32,2048]{1,0:T(8,128)(2,1)S(1)}, bf16[32,2048]{1,0:T(8,128)(2,1)S(1)}, u32[]{:S(2)}, u32[]{:S(2)}) collective-permute-start(bf16[32,2048]{1,0:T(8,128)(2,1)S(1)} %get-tuple-element.41), channel_id=1, source_target_pairs={{0,4},{1,5},{2,6},{3,7},{4,0},{5,1},{6,2},{7,3},{8,12},{9,13},{10,... | collective-permute-start | bytes 393224 | tf_op jit(solution)/shard_map/ppermute | solution.py:270
  64.2 6.8 %collective-permute-start.7 = (bf16[32,2048]{1,0:T(8,128)(2,1)S(1)}, bf16[32,2048]{1,0:T(8,128)(2,1)S(1)}, u32[]{:S(2)}, u32[]{:S(2)}) collective-permute-start(bf16[32,2048]{1,0:T(8,128)(2,1)S(1)} %get-tuple-element.42), channel_id=1, source_target_pairs={{0,2},{1,3},{2,0},{3,1},{4,6},{5,7},{6,4},{7,5},{8,10},{9,11},{10,... | collective-permute-start | bytes 393224 | tf_op jit(solution)/shard_map/ppermute | solution.py:270
  71.1 7.8 %collective-permute-start.8 = (bf16[16,2048]{1,0:T(8,128)(2,1)S(1)}, bf16[16,2048]{1,0:T(8,128)(2,1)S(1)}, u32[]{:S(2)}, u32[]{:S(2)}) collective-permute-start(bf16[16,2048]{1,0:T(8,128)(2,1)S(1)} %slice.79), channel_id=1, source_target_pairs={{0,14},{1,15},{2,12},{3,13},{4,10},{5,11},{6,8},{7,9},{8,6},{9,7},... | collective-permute-start | bytes 196616 | tf_op jit(solution)/shard_map/ppermute | solution.py:270
  79.8 7.6 %collective-permute-start.9 = (bf16[16,2176]{1,0:T(8,128)(2,1)S(1)}, bf16[16,2176]{1,0:T(8,128)(2,1)S(1)}, u32[]{:S(2)}, u32[]{:S(2)}) collective-permute-start(bf16[16,2176]{1,0:T(8,128)(2,1)S(1)} %get-tuple-element.44.base), channel_id=1, source_target_pairs={{0,14},{1,15},{2,12},{3,13},{4,10},{5,11},{6,8},{7,9},{8,6},{9,7},... | collective-permute-start | bytes 208904 | tf_op jit(solution)/shard_map/ppermute | solution.py:270
  87.5 5.1 %collective-permute-start.12 = (bf16[32,2176]{1,0:T(8,128)(2,1)S(1)}, bf16[32,2176]{1,0:T(8,128)(2,1)S(1)}, u32[]{:S(2)}, u32[]{:S(2)}) collective-permute-start(bf16[32,2176]{1,0:T(8,128)(2,1)S(1)} %constant_dynamic-update-slice_fusion.refs_6_), channel_id=1, source_target_pairs={{0,1},{1,0},{2,3},{3,2},{4,5},{5,4},{6,7},{7,6},{8,9},{9,8},{10,11... | collective-permute-start | bytes 417800 | tf_op jit(solution)/shard_map/ppermute | solution.py:270
  88.1 7.9 %collective-permute-start.11 = (bf16[32,2176]{1,0:T(8,128)(2,1)S(1)}, bf16[32,2176]{1,0:T(8,128)(2,1)S(1)}, u32[]{:S(2)}, u32[]{:S(2)}) collective-permute-start(bf16[32,2176]{1,0:T(8,128)(2,1)S(1)} %constant_dynamic-update-slice_fusion.refs_6_), channel_id=1, source_target_pairs={{0,6},{1,7},{2,4},{3,5},{4,2},{5,3},{6,0},{7,1},{8,14},{9,15},{10,... | collective-permute-start | bytes 417800 | tf_op jit(solution)/shard_map/ppermute | solution.py:270
  89.1 10.6 %collective-permute-start.10 = (bf16[32,2176]{1,0:T(8,128)(2,1)S(1)}, bf16[32,2176]{1,0:T(8,128)(2,1)S(1)}, u32[]{:S(2)}, u32[]{:S(2)}) collective-permute-start(bf16[32,2176]{1,0:T(8,128)(2,1)S(1)} %constant_dynamic-update-slice_fusion.refs_6_), channel_id=1, source_target_pairs={{0,2},{1,3},{2,0},{3,1},{4,6},{5,7},{6,4},{7,5},{8,10},{9,11},{10,... | collective-permute-start | bytes 417800 | tf_op jit(solution)/shard_map/ppermute | solution.py:270
  96.0 6.1 %collective-permute-start.13 = (bf16[32,2176]{1,0:T(8,128)(2,1)S(1)}, bf16[32,2176]{1,0:T(8,128)(2,1)S(1)}, u32[]{:S(2)}, u32[]{:S(2)}) collective-permute-start(bf16[32,2176]{1,0:T(8,128)(2,1)S(1)} %constant_dynamic-update-slice_fusion.refs_6_), channel_id=1, source_target_pairs={{0,4},{1,5},{2,6},{3,7},{4,0},{5,1},{6,2},{7,3},{8,12},{9,13},{10,... | collective-permute-start | bytes 417800 | tf_op jit(solution)/shard_map/ppermute | solution.py:270
  98.1 6.3 %collective-permute-start.16 = (bf16[32,2176]{1,0:T(8,128)(2,1)S(1)}, bf16[32,2176]{1,0:T(8,128)(2,1)S(1)}, u32[]{:S(2)}, u32[]{:S(2)}) collective-permute-start(bf16[32,2176]{1,0:T(8,128)(2,1)S(1)} %collective-permute-done.11.refs_9_), channel_id=1, source_target_pairs={{0,1},{1,0},{2,3},{3,2},{4,5},{5,4},{6,7},{7,6},{8,9},{9,8},{10,11... | collective-permute-start | bytes 417800 | tf_op jit(solution)/shard_map/ppermute | solution.py:270
  99.7 6.2 %collective-permute-start.14 = (bf16[32,2176]{1,0:T(8,128)(2,1)S(1)}, bf16[32,2176]{1,0:T(8,128)(2,1)S(1)}, u32[]{:S(2)}, u32[]{:S(2)}) collective-permute-start(bf16[32,2176]{1,0:T(8,128)(2,1)S(1)} %collective-permute-done.10.refs_7_), channel_id=1, source_target_pairs={{0,1},{1,0},{2,3},{3,2},{4,5},{5,4},{6,7},{7,6},{8,9},{9,8},{10,11... | collective-permute-start | bytes 417800 | tf_op jit(solution)/shard_map/ppermute | solution.py:270
  102.0 5.4 %collective-permute-start.15 = (bf16[32,2176]{1,0:T(8,128)(2,1)S(1)}, bf16[32,2176]{1,0:T(8,128)(2,1)S(1)}, u32[]{:S(2)}, u32[]{:S(2)}) collective-permute-start(bf16[32,2176]{1,0:T(8,128)(2,1)S(1)} %collective-permute-done.13.refs_8_), channel_id=1, source_target_pairs={{0,1},{1,0},{2,3},{3,2},{4,5},{5,4},{6,7},{7,6},{8,9},{9,8},{10,11... | collective-permute-start | bytes 417800 | tf_op jit(solution)/shard_map/ppermute | solution.py:270
  114.5 6.5 %collective-permute-start.17 = (bf16[32,2048]{1,0:T(8,128)(2,1)S(1)}, bf16[32,2048]{1,0:T(8,128)(2,1)S(1)}, u32[]{:S(2)}, u32[]{:S(2)}) collective-permute-start(bf16[32,2048]{1,0:T(8,128)(2,1)S(1)} %get-tuple-element.49), channel_id=1, source_target_pairs={{0,1},{1,0},{2,3},{3,2},{4,5},{5,4},{6,7},{7,6},{8,9},{9,8},{10,11... | collective-permute-start | bytes 393224 | tf_op jit(solution)/shard_map/ppermute | solution.py:270
  121.0 7.9 %collective-permute-start.18 = (bf16[64,2048]{1,0:T(8,128)(2,1)S(1)}, bf16[64,2048]{1,0:T(8,128)(2,1)S(1)}, u32[]{:S(2)}, u32[]{:S(2)}) collective-permute-start(bf16[64,2048]{1,0:T(8,128)(2,1)S(1)} %get-tuple-element.50), channel_id=1, source_target_pairs={{0,1},{1,0},{2,3},{3,2},{4,5},{5,4},{6,7},{7,6},{8,9},{9,8},{10,11... | collective-permute-start | bytes 786440 | tf_op jit(solution)/shard_map/ppermute | solution.py:270
  122.8 10.3 %collective-permute-start.20 = (bf16[32,2048]{1,0:T(8,128)(2,1)S(1)}, bf16[32,2048]{1,0:T(8,128)(2,1)S(1)}, u32[]{:S(2)}, u32[]{:S(2)}) collective-permute-start(bf16[32,2048]{1,0:T(8,128)(2,1)S(1)} %add_convert_fusion.2), channel_id=1, source_target_pairs={{0,6},{1,7},{2,4},{3,5},{4,2},{5,3},{6,0},{7,1},{8,14},{9,15},{10,... | collective-permute-start | bytes 393224 | tf_op jit(solution)/shard_map/ppermute | solution.py:270
  128.9 5.1 %collective-permute-start.19 = (bf16[32,2048]{1,0:T(8,128)(2,1)S(1)}, bf16[32,2048]{1,0:T(8,128)(2,1)S(1)}, u32[]{:S(2)}, u32[]{:S(2)}) collective-permute-start(bf16[32,2048]{1,0:T(8,128)(2,1)S(1)} %get-tuple-element.51), channel_id=1, source_target_pairs={{0,1},{1,0},{2,3},{3,2},{4,5},{5,4},{6,7},{7,6},{8,9},{9,8},{10,11... | collective-permute-start | bytes 393224 | tf_op jit(solution)/shard_map/ppermute | solution.py:270
  130.8 6.0 %collective-permute-start.21 = (bf16[32,2048]{1,0:T(8,128)(2,1)S(1)}, bf16[32,2048]{1,0:T(8,128)(2,1)S(1)}, u32[]{:S(2)}, u32[]{:S(2)}) collective-permute-start(bf16[32,2048]{1,0:T(8,128)(2,1)S(1)} %get-tuple-element.53), channel_id=1, source_target_pairs={{0,4},{1,5},{2,6},{3,7},{4,0},{5,1},{6,2},{7,3},{8,12},{9,13},{10,... | collective-permute-start | bytes 393224 | tf_op jit(solution)/shard_map/ppermute | solution.py:270
  132.5 5.1 %collective-permute-start.22 = (bf16[32,2048]{1,0:T(8,128)(2,1)S(1)}, bf16[32,2048]{1,0:T(8,128)(2,1)S(1)}, u32[]{:S(2)}, u32[]{:S(2)}) collective-permute-start(bf16[32,2048]{1,0:T(8,128)(2,1)S(1)} %get-tuple-element.54), channel_id=1, source_target_pairs={{0,2},{1,3},{2,0},{3,1},{4,6},{5,7},{6,4},{7,5},{8,10},{9,11},{10,... | collective-permute-start | bytes 393224 | tf_op jit(solution)/shard_map/ppermute | solution.py:270
  137.7 8.1 %collective-permute-start.23 = (bf16[16,2048]{1,0:T(8,128)(2,1)S(1)}, bf16[16,2048]{1,0:T(8,128)(2,1)S(1)}, u32[]{:S(2)}, u32[]{:S(2)}) collective-permute-start(bf16[16,2048]{1,0:T(8,128)(2,1)S(1)} %slice.78), channel_id=1, source_target_pairs={{0,14},{1,15},{2,12},{3,13},{4,10},{5,11},{6,8},{7,9},{8,6},{9,7},... | collective-permute-start | bytes 196616 | tf_op jit(solution)/shard_map/ppermute | solution.py:270
  146.0 7.5 %collective-permute-start.24 = (bf16[16,2048]{1,0:T(8,128)(2,1)S(1)}, bf16[16,2048]{1,0:T(8,128)(2,1)S(1)}, u32[]{:S(2)}, u32[]{:S(2)}) collective-permute-start(bf16[16,2048]{1,0:T(8,128)(2,1)S(1)} %shard_map.101), channel_id=1, source_target_pairs={{0,14},{1,15},{2,12},{3,13},{4,10},{5,11},{6,8},{7,9},{8,6},{9,7},... | collective-permute-start | bytes 196616 | tf_op jit(solution)/shard_map/ppermute | solution.py:270
  153.6 5.6 %collective-permute-start.27 = (bf16[32,2048]{1,0:T(8,128)(2,1)S(1)}, bf16[32,2048]{1,0:T(8,128)(2,1)S(1)}, u32[]{:S(2)}, u32[]{:S(2)}) collective-permute-start(bf16[32,2048]{1,0:T(8,128)(2,1)S(1)} %pad_maximum_fusion.refs_0_), channel_id=1, source_target_pairs={{0,1},{1,0},{2,3},{3,2},{4,5},{5,4},{6,7},{7,6},{8,9},{9,8},{10,11... | collective-permute-start | bytes 393224 | tf_op jit(solution)/shard_map/ppermute | solution.py:270
  155.4 5.0 %collective-permute-start.26 = (bf16[32,2048]{1,0:T(8,128)(2,1)S(1)}, bf16[32,2048]{1,0:T(8,128)(2,1)S(1)}, u32[]{:S(2)}, u32[]{:S(2)}) collective-permute-start(bf16[32,2048]{1,0:T(8,128)(2,1)S(1)} %pad_maximum_fusion.refs_0_), channel_id=1, source_target_pairs={{0,6},{1,7},{2,4},{3,5},{4,2},{5,3},{6,0},{7,1},{8,14},{9,15},{10,... | collective-permute-start | bytes 393224 | tf_op jit(solution)/shard_map/ppermute | solution.py:270
  156.4 5.5 %collective-permute-start.25 = (bf16[32,2048]{1,0:T(8,128)(2,1)S(1)}, bf16[32,2048]{1,0:T(8,128)(2,1)S(1)}, u32[]{:S(2)}, u32[]{:S(2)}) collective-permute-start(bf16[32,2048]{1,0:T(8,128)(2,1)S(1)} %pad_maximum_fusion.refs_0_), channel_id=1, source_target_pairs={{0,2},{1,3},{2,0},{3,1},{4,6},{5,7},{6,4},{7,5},{8,10},{9,11},{10,... | collective-permute-start | bytes 393224 | tf_op jit(solution)/shard_map/ppermute | solution.py:270
  160.4 5.9 %collective-permute-start.28 = (bf16[32,2048]{1,0:T(8,128)(2,1)S(1)}, bf16[32,2048]{1,0:T(8,128)(2,1)S(1)}, u32[]{:S(2)}, u32[]{:S(2)}) collective-permute-start(bf16[32,2048]{1,0:T(8,128)(2,1)S(1)} %pad_maximum_fusion.refs_0_), channel_id=1, source_target_pairs={{0,4},{1,5},{2,6},{3,7},{4,0},{5,1},{6,2},{7,3},{8,12},{9,13},{10,... | collective-permute-start | bytes 393224 | tf_op jit(solution)/shard_map/ppermute | solution.py:270
  160.4 7.6 %collective-permute-start.31 = (bf16[32,2048]{1,0:T(8,128)(2,1)S(1)}, bf16[32,2048]{1,0:T(8,128)(2,1)S(1)}, u32[]{:S(2)}, u32[]{:S(2)}) collective-permute-start(bf16[32,2048]{1,0:T(8,128)(2,1)S(1)} %collective-permute-done.26.refs_3_), channel_id=1, source_target_pairs={{0,1},{1,0},{2,3},{3,2},{4,5},{5,4},{6,7},{7,6},{8,9},{9,8},{10,11... | collective-permute-start | bytes 393224 | tf_op jit(solution)/shard_map/ppermute | solution.py:270
  161.9 6.1 %collective-permute-start.29 = (bf16[32,2048]{1,0:T(8,128)(2,1)S(1)}, bf16[32,2048]{1,0:T(8,128)(2,1)S(1)}, u32[]{:S(2)}, u32[]{:S(2)}) collective-permute-start(bf16[32,2048]{1,0:T(8,128)(2,1)S(1)} %collective-permute-done.25.refs_1_), channel_id=1, source_target_pairs={{0,1},{1,0},{2,3},{3,2},{4,5},{5,4},{6,7},{7,6},{8,9},{9,8},{10,11... | collective-permute-start | bytes 393224 | tf_op jit(solution)/shard_map/ppermute | solution.py:270
  166.2 5.0 %collective-permute-start.30 = (bf16[32,2048]{1,0:T(8,128)(2,1)S(1)}, bf16[32,2048]{1,0:T(8,128)(2,1)S(1)}, u32[]{:S(2)}, u32[]{:S(2)}) collective-permute-start(bf16[32,2048]{1,0:T(8,128)(2,1)S(1)} %collective-permute-done.28.refs_2_), channel_id=1, source_target_pairs={{0,1},{1,0},{2,3},{3,2},{4,5},{5,4},{6,7},{7,6},{8,9},{9,8},{10,11... | collective-permute-start | bytes 393224 | tf_op jit(solution)/shard_map/ppermute | solution.py:270

commit v5 on v3

--- a/solution.py
+++ b/solution.py
@@ -285,10 +285,11 @@
 
 def gather_rows(own):
     pair = jnp.concatenate([own, swap(own, MIRROR)], axis=0)
-    got = {0: pair}
-    for hop in (2, 6, 4):
-        got[hop] = swap(pair, hop)
-    return [got[hop] for hop in NEAR] + [swap(got[hop], SIDE) for hop in NEAR]
+    got = {0: pair, 2: swap(pair, 2), 6: swap(pair, 6)}
+    beside = swap(pair, SIDE)
+    pair, *_ = lax.optimization_barrier((pair, got[6], beside))
+    got[4] = swap(pair, 4)
+    return [got[hop] for hop in NEAR] + [beside] + [swap(got[hop], SIDE) for hop in NEAR[1:]]
 
 
 def on_device(

time: 172 us -> 172 us (level)
  waiting for transfers between devices: 91.1 us -> 95.9 us
  starting transfers between devices: 55.3 us -> 50.8 us
    ppermute x30, waiting for transfers between devices: 60 us -> 64.8 us  [swap(): return lax.ppermute(block, 'people', [(i, i ^ hop) for i in range(count)])]
    ppermute x30, starting transfers between devices: 52.4 us -> 48 us  [swap(): return lax.ppermute(block, 'people', [(i, i ^ hop) for i in range(count)])]
  transfers between devices with their start and end apart: 32 -> 32, of which waited for: 22 -> 23; matrix products, arithmetic and copies ran while one was open for 0% -> 0% of each run, Pallas kernels for 3% -> 3%
where the time goes in v5:
time: 172 us; the launch traced here: 171 us
  waiting for transfers between devices  95.9 us (56%)
  starting transfers between devices  50.8 us (30%)
  Pallas kernels  22.1 us (13%)
    ppermute x30, waiting for transfers between devices, swap(): return lax.ppermute(block, 'people', [(i, i ^ hop) for i in range(count)])  64.8 us
    ppermute x30, starting transfers between devices, swap(): return lax.ppermute(block, 'people', [(i, i ^ hop) for i in range(count)])  48 us
    ppermute x1, waiting for transfers between devices, on_device(): slow = lax.ppermute(away, 'genome', beyond)  30.3 us
    pallas_call x2, Pallas kernels, local_grad(): pl.pallas_call(functools.partial(turn_kernel, len(pieces)), out_shape=out...  11.7 us
  transfers between devices with their start and end apart: 32, of which 23 were waited for; matrix products, arithmetic and copies ran while one was open for 0% of the time, Pallas kernels for 3%

profile of v5, /device:TPU:56, one launch (start us, length us, event | category | flops | bytes accessed | tf_op | source)
XLA Modules:
  0.0 170.7 jit_solution(3389947745473883992)
XLA Ops:
  0.7 3.0 %shard_map.96 = (bf16[3072,512]{1,0:T(8,128)(2,1)S(1)}, bf16[3072,512]{1,0:T(8,128)(2,1)S(1)}) custom-call(s32[1]{0:T(128)} %bitcast.where.refs_0_, bf16[3072,1024]{1,0:T(8,128)(2,1)} %whole.1), custom_call_target="tpu_custom_call" | custom-call | tf_op jit(solution)/shard_map/pallas_call | solution.py:208
  3.7 0.1 collective-permute-start.1
  3.8 2.7 %collective-permute-start = (bf16[3072,512]{1,0:T(8,128)(2,1)S(1)}, bf16[3072,512]{1,0:T(8,128)(2,1)S(1)}, u32[]{:S(2)}, u32[]{:S(2)}) collective-permute-start(bf16[3072,512]{1,0:T(8,128)(2,1)S(1)} %get-tuple-element.21.second.refs_2_), channel_id=1, source_target_pairs={{16,32},{32,16},{48,64},{64,48},{80,96},{96,80},{112,128},{128,112... | collective-permute-start | bytes 9437192 | tf_op jit(solution)/shard_map/ppermute | solution.py:317
  6.6 2.1 %shard_map.95 = (f32[256,128]{1,0:T(8,128)S(1)}, bf16[256,2048]{1,0:T(8,128)(2,1)S(1)}, f32[16,2048]{1,0:T(8,128)S(1)}) custom-call(s32[1]{0:T(128)} %bitcast.where.refs_0_, s32[16,256]{1,0:T(8,128)S(1)} %bitcast.8, s32[1,256]{1,0:T(1,128)S(1)} %bitcast.9, s32[1,256]{1,0:T(1,128)S(1)} %bitcast.10, f32[1,256]{1,0:T(1,128)S(1)} %bitcast.11, ...), custom_call_target="tpu_custom_call" | custom-call | tf_op jit(solution)/shard_map/pallas_call | solution.py:258
  8.7 0.8 collective-permute-done.1.fourth.refs_4_
  9.5 2.6 %shard_map.97.refs_5_ = f32[3072,256]{1,0:T(8,128)S(1)} custom-call(s32[1]{0:T(128)} %bitcast.where.refs_0_, bf16[3072,512]{1,0:T(8,128)(2,1)S(1)} %get-tuple-element.21.second.refs_2_, bf16[3072,512]{1,0:T(8,128)(2,1)S(1)} %get-tuple-element.22.third.refs_3_, bf16[3072,512]{1,0:T(8,128)(2,1)S(1)} %collective-permute-done.1.fourth.refs_4_, ...), custom_call_target="tpu_custom_call" | custom-call | tf_op jit(solution)/shard_map/pallas_call | solution.py:225
  12.1 30.3 %collective-permute-done.refs_1_ = bf16[3072,512]{1,0:T(8,128)(2,1)S(1)} collective-permute-done((bf16[3072,512]{1,0:T(8,128)(2,1)S(1)}, bf16[3072,512]{1,0:T(8,128)(2,1)S(1)}, u32[]{:S(2)}, u32[]{:S(2)}) %collective-permute-start) | collective-permute-done | bytes 3145760 | tf_op jit(solution)/shard_map/ppermute | solution.py:317
  42.4 4.6 %shard_map.98 = (f32[128,2048]{1,0:T(8,128)S(1)}, bf16[32,2048]{1,0:T(8,128)(2,1)S(1)}, bf16[64,2048]{1,0:T(8,128)(2,1)S(1)}, bf16[32,2048]{1,0:T(8,128)(2,1)S(1)}) custom-call(s32[1]{0:T(128)} %bitcast.where.refs_0_, bf16[3072,512]{1,0:T(8,128)(2,1)S(1)} %collective-permute-done.refs_1_, bf16[3072,512]{1,0:T(8,128)(2,1)S(1)} %get-tuple-element.21.second.refs_2_, ...), custom_call_target="tpu_custom_call" | custom-call | flops 6442450944 | tf_op jit(solution)/shard_map/pallas_call | solution.py:246
  47.0 1.6 collective-permute-start.5
  48.6 0.5 collective-permute-start.3
  49.1 1.5 collective-permute-start.2
  50.6 5.3 %collective-permute-done.3 = bf16[32,2048]{1,0:T(8,128)(2,1)S(1)} collective-permute-done((bf16[32,2048]{1,0:T(8,128)(2,1)S(1)}, bf16[32,2048]{1,0:T(8,128)(2,1)S(1)}, u32[]{:S(2)}, u32[]{:S(2)}) %collective-permute-start.3) | collective-permute-done | bytes 131104 | tf_op jit(solution)/shard_map/ppermute | solution.py:270
  55.9 0.1 add_convert_fusion.4
  56.0 3.4 %collective-permute-start.6 = (bf16[32,2048]{1,0:T(8,128)(2,1)S(1)}, bf16[32,2048]{1,0:T(8,128)(2,1)S(1)}, u32[]{:S(2)}, u32[]{:S(2)}) collective-permute-start(bf16[32,2048]{1,0:T(8,128)(2,1)S(1)} %get-tuple-element.40), channel_id=1, source_target_pairs={{0,4},{1,5},{2,6},{3,7},{4,0},{5,1},{6,2},{7,3},{8,12},{9,13},{10,... | collective-permute-start | bytes 393224 | tf_op jit(solution)/shard_map/ppermute | solution.py:270
  59.4 0.1 collective-permute-start.7
  59.5 0.6 collective-permute-start.4
  60.0 0.0 collective-permute-done.2
  60.0 2.7 %collective-permute-done.6 = bf16[32,2048]{1,0:T(8,128)(2,1)S(1)} collective-permute-done((bf16[32,2048]{1,0:T(8,128)(2,1)S(1)}, bf16[32,2048]{1,0:T(8,128)(2,1)S(1)}, u32[]{:S(2)}, u32[]{:S(2)}) %collective-permute-start.6) | collective-permute-done | bytes 131104 | tf_op jit(solution)/shard_map/ppermute | solution.py:270
  62.8 1.6 collective-permute-done.7
  64.3 4.0 %collective-permute-done.4 = bf16[32,2048]{1,0:T(8,128)(2,1)S(1)} collective-permute-done((bf16[32,2048]{1,0:T(8,128)(2,1)S(1)}, bf16[32,2048]{1,0:T(8,128)(2,1)S(1)}, u32[]{:S(2)}, u32[]{:S(2)}) %collective-permute-start.4) | collective-permute-done | bytes 131104 | tf_op jit(solution)/shard_map/ppermute | solution.py:270
  68.4 0.1 convert_add_fusion.1.near
  68.5 5.4 %collective-permute-start.8 = (bf16[16,2048]{1,0:T(8,128)(2,1)S(1)}, bf16[16,2048]{1,0:T(8,128)(2,1)S(1)}, u32[]{:S(2)}, u32[]{:S(2)}) collective-permute-start(bf16[16,2048]{1,0:T(8,128)(2,1)S(1)} %slice.79), channel_id=1, source_target_pairs={{0,14},{1,15},{2,12},{3,13},{4,10},{5,11},{6,8},{7,9},{8,6},{9,7},... | collective-permute-start | bytes 196616 | tf_op jit(solution)/shard_map/ppermute | solution.py:270
  73.8 2.2 %collective-permute-done.8.far = bf16[16,2048]{1,0:T(8,128)(2,1)S(1)} collective-permute-done((bf16[16,2048]{1,0:T(8,128)(2,1)S(1)}, bf16[16,2048]{1,0:T(8,128)(2,1)S(1)}, u32[]{:S(2)}, u32[]{:S(2)}) %collective-permute-start.8) | collective-permute-done | bytes 65568 | tf_op jit(solution)/shard_map/ppermute | solution.py:270
  76.1 1.0 shard_map.99
  77.1 5.3 %collective-permute-start.9 = (bf16[16,2176]{1,0:T(8,128)(2,1)S(1)}, bf16[16,2176]{1,0:T(8,128)(2,1)S(1)}, u32[]{:S(2)}, u32[]{:S(2)}) collective-permute-start(bf16[16,2176]{1,0:T(8,128)(2,1)S(1)} %get-tuple-element.29.base), channel_id=1, source_target_pairs={{0,14},{1,15},{2,12},{3,13},{4,10},{5,11},{6,8},{7,9},{8,6},{9,7},... | collective-permute-start | bytes 208904 | tf_op jit(solution)/shard_map/ppermute | solution.py:270
  82.4 2.3 %collective-permute-done.9 = bf16[16,2176]{1,0:T(8,128)(2,1)S(1)} collective-permute-done((bf16[16,2176]{1,0:T(8,128)(2,1)S(1)}, bf16[16,2176]{1,0:T(8,128)(2,1)S(1)}, u32[]{:S(2)}, u32[]{:S(2)}) %collective-permute-start.9) | collective-permute-done | bytes 69664 | tf_op jit(solution)/shard_map/ppermute | solution.py:270
  84.7 1.6 collective-permute-start.12
  86.3 3.6 %collective-permute-start.11 = (bf16[32,2176]{1,0:T(8,128)(2,1)S(1)}, bf16[32,2176]{1,0:T(8,128)(2,1)S(1)}, u32[]{:S(2)}, u32[]{:S(2)}) collective-permute-start(bf16[32,2176]{1,0:T(8,128)(2,1)S(1)} %constant_dynamic-update-slice_fusion.refs_6_), channel_id=1, source_target_pairs={{0,6},{1,7},{2,4},{3,5},{4,2},{5,3},{6,0},{7,1},{8,14},{9,15},{10,... | collective-permute-start | bytes 417800 | tf_op jit(solution)/shard_map/ppermute | solution.py:270
  89.8 1.2 collective-permute-done.12.refs_10_
  91.1 2.5 %collective-permute-done.11.refs_9_ = bf16[32,2176]{1,0:T(8,128)(2,1)S(1)} collective-permute-done((bf16[32,2176]{1,0:T(8,128)(2,1)S(1)}, bf16[32,2176]{1,0:T(8,128)(2,1)S(1)}, u32[]{:S(2)}, u32[]{:S(2)}) %collective-permute-start.11) | collective-permute-done | bytes 139296 | tf_op jit(solution)/shard_map/ppermute | solution.py:270
  93.6 1.5 collective-permute-start.16
  95.1 0.5 collective-permute-start.14
  95.6 3.9 %collective-permute-done.13.refs_8_ = bf16[32,2176]{1,0:T(8,128)(2,1)S(1)} collective-permute-done((bf16[32,2176]{1,0:T(8,128)(2,1)S(1)}, bf16[32,2176]{1,0:T(8,128)(2,1)S(1)}, u32[]{:S(2)}, u32[]{:S(2)}) %collective-permute-start.13) | collective-permute-done | bytes 139296 | tf_op jit(solution)/shard_map/ppermute | solution.py:270
  99.5 2.1 %collective-permute-start.15 = (bf16[32,2176]{1,0:T(8,128)(2,1)S(1)}, bf16[32,2176]{1,0:T(8,128)(2,1)S(1)}, u32[]{:S(2)}, u32[]{:S(2)}) collective-permute-start(bf16[32,2176]{1,0:T(8,128)(2,1)S(1)} %collective-permute-done.13.refs_8_), channel_id=1, source_target_pairs={{0,1},{1,0},{2,3},{3,2},{4,5},{5,4},{6,7},{7,6},{8,9},{9,8},{10,11... | collective-permute-start | bytes 417800 | tf_op jit(solution)/shard_map/ppermute | solution.py:270
  101.6 0.3 collective-permute-done.14.refs_11_
  101.9 3.2 %collective-permute-done.15.refs_12_ = bf16[32,2176]{1,0:T(8,128)(2,1)S(1)} collective-permute-done((bf16[32,2176]{1,0:T(8,128)(2,1)S(1)}, bf16[32,2176]{1,0:T(8,128)(2,1)S(1)}, u32[]{:S(2)}, u32[]{:S(2)}) %collective-permute-start.15) | collective-permute-done | bytes 139296 | tf_op jit(solution)/shard_map/ppermute | solution.py:270
  105.1 7.1 %shard_map.100 = (f32[128,2048]{1,0:T(8,128)S(1)}, bf16[32,2048]{1,0:T(8,128)(2,1)S(1)}, bf16[64,2048]{1,0:T(8,128)(2,1)S(1)}, bf16[32,2048]{1,0:T(8,128)(2,1)S(1)}, f32[16,256]{1,0:T(8,128)S(1)}) custom-call(s32[1]{0:T(128)} %bitcast.where.refs_0_, bf16[3072,512]{1,0:T(8,128)(2,1)S(1)} %collective-permute-done.refs_1_, ...), custom_call_target="tpu_custom_call" | custom-call | flops 6442450944 | tf_op jit(solution)/shard_map/pallas_call | solution.py:246
  112.3 1.8 %collective-permute-start.20 = (bf16[64,2048]{1,0:T(8,128)(2,1)S(1)}, bf16[64,2048]{1,0:T(8,128)(2,1)S(1)}, u32[]{:S(2)}, u32[]{:S(2)}) collective-permute-start(bf16[64,2048]{1,0:T(8,128)(2,1)S(1)} %get-tuple-element.34), channel_id=1, source_target_pairs={{0,1},{1,0},{2,3},{3,2},{4,5},{5,4},{6,7},{7,6},{8,9},{9,8},{10,11... | collective-permute-start | bytes 786440 | tf_op jit(solution)/shard_map/ppermute | solution.py:270
  114.1 0.3 collective-permute-start.18
  114.4 1.7 %collective-permute-start.17 = (bf16[32,2048]{1,0:T(8,128)(2,1)S(1)}, bf16[32,2048]{1,0:T(8,128)(2,1)S(1)}, u32[]{:S(2)}, u32[]{:S(2)}) collective-permute-start(bf16[32,2048]{1,0:T(8,128)(2,1)S(1)} %get-tuple-element.32), channel_id=1, source_target_pairs={{0,1},{1,0},{2,3},{3,2},{4,5},{5,4},{6,7},{7,6},{8,9},{9,8},{10,11... | collective-permute-start | bytes 393224 | tf_op jit(solution)/shard_map/ppermute | solution.py:270
  116.1 7.8 %collective-permute-done.18 = bf16[32,2048]{1,0:T(8,128)(2,1)S(1)} collective-permute-done((bf16[32,2048]{1,0:T(8,128)(2,1)S(1)}, bf16[32,2048]{1,0:T(8,128)(2,1)S(1)}, u32[]{:S(2)}, u32[]{:S(2)}) %collective-permute-start.18) | collective-permute-done | bytes 131104 | tf_op jit(solution)/shard_map/ppermute | solution.py:270
  123.9 0.1 add_convert_fusion.1
  124.0 3.6 %collective-permute-start.21 = (bf16[32,2048]{1,0:T(8,128)(2,1)S(1)}, bf16[32,2048]{1,0:T(8,128)(2,1)S(1)}, u32[]{:S(2)}, u32[]{:S(2)}) collective-permute-start(bf16[32,2048]{1,0:T(8,128)(2,1)S(1)} %get-tuple-element.38), channel_id=1, source_target_pairs={{0,4},{1,5},{2,6},{3,7},{4,0},{5,1},{6,2},{7,3},{8,12},{9,13},{10,... | collective-permute-start | bytes 393224 | tf_op jit(solution)/shard_map/ppermute | solution.py:270
  127.7 0.7 collective-permute-start.19
  128.3 3.6 %collective-permute-done.21 = bf16[32,2048]{1,0:T(8,128)(2,1)S(1)} collective-permute-done((bf16[32,2048]{1,0:T(8,128)(2,1)S(1)}, bf16[32,2048]{1,0:T(8,128)(2,1)S(1)}, u32[]{:S(2)}, u32[]{:S(2)}) %collective-permute-start.21) | collective-permute-done | bytes 131104 | tf_op jit(solution)/shard_map/ppermute | solution.py:270
  131.9 0.7 collective-permute-done.22
  132.6 2.7 %collective-permute-done.19 = bf16[32,2048]{1,0:T(8,128)(2,1)S(1)} collective-permute-done((bf16[32,2048]{1,0:T(8,128)(2,1)S(1)}, bf16[32,2048]{1,0:T(8,128)(2,1)S(1)}, u32[]{:S(2)}, u32[]{:S(2)}) %collective-permute-start.19) | collective-permute-done | bytes 131104 | tf_op jit(solution)/shard_map/ppermute | solution.py:270
  135.3 0.1 convert_add_fusion.near
  135.4 3.1 %collective-permute-start.23 = (bf16[16,2048]{1,0:T(8,128)(2,1)S(1)}, bf16[16,2048]{1,0:T(8,128)(2,1)S(1)}, u32[]{:S(2)}, u32[]{:S(2)}) collective-permute-start(bf16[16,2048]{1,0:T(8,128)(2,1)S(1)} %slice.78), channel_id=1, source_target_pairs={{0,14},{1,15},{2,12},{3,13},{4,10},{5,11},{6,8},{7,9},{8,6},{9,7},... | collective-permute-start | bytes 196616 | tf_op jit(solution)/shard_map/ppermute | solution.py:270
  138.5 4.6 %collective-permute-done.23.far = bf16[16,2048]{1,0:T(8,128)(2,1)S(1)} collective-permute-done((bf16[16,2048]{1,0:T(8,128)(2,1)S(1)}, bf16[16,2048]{1,0:T(8,128)(2,1)S(1)}, u32[]{:S(2)}, u32[]{:S(2)}) %collective-permute-start.23) | collective-permute-done | bytes 65568 | tf_op jit(solution)/shard_map/ppermute | solution.py:270
  143.1 0.2 shard_map.101
  143.3 2.8 %collective-permute-start.24 = (bf16[16,2048]{1,0:T(8,128)(2,1)S(1)}, bf16[16,2048]{1,0:T(8,128)(2,1)S(1)}, u32[]{:S(2)}, u32[]{:S(2)}) collective-permute-start(bf16[16,2048]{1,0:T(8,128)(2,1)S(1)} %shard_map.101), channel_id=1, source_target_pairs={{0,14},{1,15},{2,12},{3,13},{4,10},{5,11},{6,8},{7,9},{8,6},{9,7},... | collective-permute-start | bytes 196616 | tf_op jit(solution)/shard_map/ppermute | solution.py:270
  146.1 4.7 %collective-permute-done.24 = bf16[16,2048]{1,0:T(8,128)(2,1)S(1)} collective-permute-done((bf16[16,2048]{1,0:T(8,128)(2,1)S(1)}, bf16[16,2048]{1,0:T(8,128)(2,1)S(1)}, u32[]{:S(2)}, u32[]{:S(2)}) %collective-permute-start.24) | collective-permute-done | bytes 65568 | tf_op jit(solution)/shard_map/ppermute | solution.py:270
  150.8 0.9 collective-permute-start.27
  151.7 2.5 %collective-permute-start.26 = (bf16[32,2048]{1,0:T(8,128)(2,1)S(1)}, bf16[32,2048]{1,0:T(8,128)(2,1)S(1)}, u32[]{:S(2)}, u32[]{:S(2)}) collective-permute-start(bf16[32,2048]{1,0:T(8,128)(2,1)S(1)} %pad_maximum_fusion.refs_0_), channel_id=1, source_target_pairs={{0,6},{1,7},{2,4},{3,5},{4,2},{5,3},{6,0},{7,1},{8,14},{9,15},{10,... | collective-permute-start | bytes 393224 | tf_op jit(solution)/shard_map/ppermute | solution.py:270
  154.2 3.1 %collective-permute-done.27.refs_4_ = bf16[32,2048]{1,0:T(8,128)(2,1)S(1)} collective-permute-done((bf16[32,2048]{1,0:T(8,128)(2,1)S(1)}, bf16[32,2048]{1,0:T(8,128)(2,1)S(1)}, u32[]{:S(2)}, u32[]{:S(2)}) %collective-permute-start.27) | collective-permute-done | bytes 131104 | tf_op jit(solution)/shard_map/ppermute | solution.py:270
  157.3 1.0 collective-permute-done.26.refs_3_
  158.3 1.0 collective-permute-start.31
  159.3 1.1 collective-permute-start.29
  160.3 3.9 %collective-permute-done.28.refs_2_ = bf16[32,2048]{1,0:T(8,128)(2,1)S(1)} collective-permute-done((bf16[32,2048]{1,0:T(8,128)(2,1)S(1)}, bf16[32,2048]{1,0:T(8,128)(2,1)S(1)}, u32[]{:S(2)}, u32[]{:S(2)}) %collective-permute-start.28) | collective-permute-done | bytes 131104 | tf_op jit(solution)/shard_map/ppermute | solution.py:270
  164.3 1.0 collective-permute-start.30
  165.2 0.6 copy.11
  165.9 3.4 %collective-permute-done.30.refs_6_ = bf16[32,2048]{1,0:T(8,128)(2,1)S(1)} collective-permute-done((bf16[32,2048]{1,0:T(8,128)(2,1)S(1)}, bf16[32,2048]{1,0:T(8,128)(2,1)S(1)}, u32[]{:S(2)}, u32[]{:S(2)}) %collective-permute-start.30) | collective-permute-done | bytes 131104 | tf_op jit(solution)/shard_map/ppermute | solution.py:270
  169.2 1.5 shard_map.102
  (32 shorter events, 0.1 us)
Async XLA Ops:
  0.6 5.9 %copy-start = (f32[256,2048]{1,0:T(8,128)S(1)}, f32[256,2048]{1,0:T(8,128)}, u32[]{:S(2)}) copy-start(f32[256,2048]{1,0:T(8,128)} %refs_4_.1) | copy-start | bytes 6291460
  0.6 5.9 %copy-start.2 = (s32[256,16]{0,1:T(8,128)S(1)}, s32[256,16]{0,1:T(8,128)}, u32[]{:S(2)}) copy-start(s32[256,16]{0,1:T(8,128)} %param.15) | copy-start | bytes 49156
  0.7 5.9 %copy-start.3 = (s32[256]{0:T(256)S(1)}, s32[256]{0:T(256)}, u32[]{:S(2)}) copy-start(s32[256]{0:T(256)} %param.13) | copy-start | bytes 3076
  0.7 5.9 %copy-start.4 = (s32[256]{0:T(256)S(1)}, s32[256]{0:T(256)}, u32[]{:S(2)}) copy-start(s32[256]{0:T(256)} %param.14) | copy-start | bytes 3076
  0.7 5.9 %copy-start.5 = (f32[256]{0:T(256)S(1)}, f32[256]{0:T(256)}, u32[]{:S(2)}) copy-start(f32[256]{0:T(256)} %param.11) | copy-start | bytes 3076
  0.7 5.9 %copy-start.6 = (f32[256]{0:T(256)S(1)}, f32[256]{0:T(256)}, u32[]{:S(2)}) copy-start(f32[256]{0:T(256)} %param.12) | copy-start | bytes 3076
  0.7 8.8 %copy-start.1 = (bf16[3072,256]{1,0:T(8,128)(2,1)S(1)}, bf16[3072,256]{1,0:T(8,128)(2,1)}, u32[]{:S(2)}) copy-start(bf16[3072,256]{1,0:T(8,128)(2,1)} %refs_5_.1) | copy-start | bytes 4718596
  3.7 5.7 %collective-permute-start.1 = (bf16[3072,512]{1,0:T(8,128)(2,1)S(1)}, bf16[3072,512]{1,0:T(8,128)(2,1)S(1)}, u32[]{:S(2)}, u32[]{:S(2)}) collective-permute-start(bf16[3072,512]{1,0:T(8,128)(2,1)S(1)} %get-tuple-element.22.third.refs_3_), channel_id=1, source_target_pairs={{0,16},{16,0},{32,48},{48,32},{64,80},{80,64},{96,112},{112,96},{1... | collective-permute-start | bytes 9437192 | tf_op jit(solution)/shard_map/ppermute | solution.py:318
  3.8 38.6 %collective-permute-start = (bf16[3072,512]{1,0:T(8,128)(2,1)S(1)}, bf16[3072,512]{1,0:T(8,128)(2,1)S(1)}, u32[]{:S(2)}, u32[]{:S(2)}) collective-permute-start(bf16[3072,512]{1,0:T(8,128)(2,1)S(1)} %get-tuple-element.21.second.refs_2_), channel_id=1, source_target_pairs={{16,32},{32,16},{48,64},{64,48},{80,96},{96,80},{112,128},{128,112... | collective-permute-start | bytes 9437192 | tf_op jit(solution)/shard_map/ppermute | solution.py:317
  47.0 8.9 %collective-permute-start.5 = (bf16[64,2048]{1,0:T(8,128)(2,1)S(1)}, bf16[64,2048]{1,0:T(8,128)(2,1)S(1)}, u32[]{:S(2)}, u32[]{:S(2)}) collective-permute-start(bf16[64,2048]{1,0:T(8,128)(2,1)S(1)} %get-tuple-element.27), channel_id=1, source_target_pairs={{0,1},{1,0},{2,3},{3,2},{4,5},{5,4},{6,7},{7,6},{8,9},{9,8},{10,11... | collective-permute-start | bytes 786440 | tf_op jit(solution)/shard_map/ppermute | solution.py:270
  48.6 7.3 %collective-permute-start.3 = (bf16[32,2048]{1,0:T(8,128)(2,1)S(1)}, bf16[32,2048]{1,0:T(8,128)(2,1)S(1)}, u32[]{:S(2)}, u32[]{:S(2)}) collective-permute-start(bf16[32,2048]{1,0:T(8,128)(2,1)S(1)} %get-tuple-element.26), channel_id=1, source_target_pairs={{0,1},{1,0},{2,3},{3,2},{4,5},{5,4},{6,7},{7,6},{8,9},{9,8},{10,11... | collective-permute-start | bytes 393224 | tf_op jit(solution)/shard_map/ppermute | solution.py:270
  49.1 10.9 %collective-permute-start.2 = (bf16[32,2048]{1,0:T(8,128)(2,1)S(1)}, bf16[32,2048]{1,0:T(8,128)(2,1)S(1)}, u32[]{:S(2)}, u32[]{:S(2)}) collective-permute-start(bf16[32,2048]{1,0:T(8,128)(2,1)S(1)} %get-tuple-element.25), channel_id=1, source_target_pairs={{0,1},{1,0},{2,3},{3,2},{4,5},{5,4},{6,7},{7,6},{8,9},{9,8},{10,11... | collective-permute-start | bytes 393224 | tf_op jit(solution)/shard_map/ppermute | solution.py:270
  56.0 6.8 %collective-permute-start.6 = (bf16[32,2048]{1,0:T(8,128)(2,1)S(1)}, bf16[32,2048]{1,0:T(8,128)(2,1)S(1)}, u32[]{:S(2)}, u32[]{:S(2)}) collective-permute-start(bf16[32,2048]{1,0:T(8,128)(2,1)S(1)} %get-tuple-element.40), channel_id=1, source_target_pairs={{0,4},{1,5},{2,6},{3,7},{4,0},{5,1},{6,2},{7,3},{8,12},{9,13},{10,... | collective-permute-start | bytes 393224 | tf_op jit(solution)/shard_map/ppermute | solution.py:270
  59.4 5.0 %collective-permute-start.7 = (bf16[32,2048]{1,0:T(8,128)(2,1)S(1)}, bf16[32,2048]{1,0:T(8,128)(2,1)S(1)}, u32[]{:S(2)}, u32[]{:S(2)}) collective-permute-start(bf16[32,2048]{1,0:T(8,128)(2,1)S(1)} %get-tuple-element.41), channel_id=1, source_target_pairs={{0,2},{1,3},{2,0},{3,1},{4,6},{5,7},{6,4},{7,5},{8,10},{9,11},{10,... | collective-permute-start | bytes 393224 | tf_op jit(solution)/shard_map/ppermute | solution.py:270
  59.5 8.9 %collective-permute-start.4 = (bf16[32,2048]{1,0:T(8,128)(2,1)S(1)}, bf16[32,2048]{1,0:T(8,128)(2,1)S(1)}, u32[]{:S(2)}, u32[]{:S(2)}) collective-permute-start(bf16[32,2048]{1,0:T(8,128)(2,1)S(1)} %get-tuple-element.43), channel_id=1, source_target_pairs={{0,6},{1,7},{2,4},{3,5},{4,2},{5,3},{6,0},{7,1},{8,14},{9,15},{10,... | collective-permute-start | bytes 393224 | tf_op jit(solution)/shard_map/ppermute | solution.py:270
  68.5 7.6 %collective-permute-start.8 = (bf16[16,2048]{1,0:T(8,128)(2,1)S(1)}, bf16[16,2048]{1,0:T(8,128)(2,1)S(1)}, u32[]{:S(2)}, u32[]{:S(2)}) collective-permute-start(bf16[16,2048]{1,0:T(8,128)(2,1)S(1)} %slice.79), channel_id=1, source_target_pairs={{0,14},{1,15},{2,12},{3,13},{4,10},{5,11},{6,8},{7,9},{8,6},{9,7},... | collective-permute-start | bytes 196616 | tf_op jit(solution)/shard_map/ppermute | solution.py:270
  77.1 7.6 %collective-permute-start.9 = (bf16[16,2176]{1,0:T(8,128)(2,1)S(1)}, bf16[16,2176]{1,0:T(8,128)(2,1)S(1)}, u32[]{:S(2)}, u32[]{:S(2)}) collective-permute-start(bf16[16,2176]{1,0:T(8,128)(2,1)S(1)} %get-tuple-element.29.base), channel_id=1, source_target_pairs={{0,14},{1,15},{2,12},{3,13},{4,10},{5,11},{6,8},{7,9},{8,6},{9,7},... | collective-permute-start | bytes 208904 | tf_op jit(solution)/shard_map/ppermute | solution.py:270
  84.7 6.4 %collective-permute-start.12 = (bf16[32,2176]{1,0:T(8,128)(2,1)S(1)}, bf16[32,2176]{1,0:T(8,128)(2,1)S(1)}, u32[]{:S(2)}, u32[]{:S(2)}) collective-permute-start(bf16[32,2176]{1,0:T(8,128)(2,1)S(1)} %constant_dynamic-update-slice_fusion.refs_6_), channel_id=1, source_target_pairs={{0,1},{1,0},{2,3},{3,2},{4,5},{5,4},{6,7},{7,6},{8,9},{9,8},{10,11... | collective-permute-start | bytes 417800 | tf_op jit(solution)/shard_map/ppermute | solution.py:270
  86.3 7.3 %collective-permute-start.11 = (bf16[32,2176]{1,0:T(8,128)(2,1)S(1)}, bf16[32,2176]{1,0:T(8,128)(2,1)S(1)}, u32[]{:S(2)}, u32[]{:S(2)}) collective-permute-start(bf16[32,2176]{1,0:T(8,128)(2,1)S(1)} %constant_dynamic-update-slice_fusion.refs_6_), channel_id=1, source_target_pairs={{0,6},{1,7},{2,4},{3,5},{4,2},{5,3},{6,0},{7,1},{8,14},{9,15},{10,... | collective-permute-start | bytes 417800 | tf_op jit(solution)/shard_map/ppermute | solution.py:270
  89.8 5.2 %collective-permute-start.10 = (bf16[32,2176]{1,0:T(8,128)(2,1)S(1)}, bf16[32,2176]{1,0:T(8,128)(2,1)S(1)}, u32[]{:S(2)}, u32[]{:S(2)}) collective-permute-start(bf16[32,2176]{1,0:T(8,128)(2,1)S(1)} %constant_dynamic-update-slice_fusion.refs_6_), channel_id=1, source_target_pairs={{0,2},{1,3},{2,0},{3,1},{4,6},{5,7},{6,4},{7,5},{8,10},{9,11},{10,... | collective-permute-start | bytes 417800 | tf_op jit(solution)/shard_map/ppermute | solution.py:270
  93.6 6.0 %collective-permute-start.13 = (bf16[32,2176]{1,0:T(8,128)(2,1)S(1)}, bf16[32,2176]{1,0:T(8,128)(2,1)S(1)}, u32[]{:S(2)}, u32[]{:S(2)}) collective-permute-start(bf16[32,2176]{1,0:T(8,128)(2,1)S(1)} %constant_dynamic-update-slice_fusion.refs_6_), channel_id=1, source_target_pairs={{0,4},{1,5},{2,6},{3,7},{4,0},{5,1},{6,2},{7,3},{8,12},{9,13},{10,... | collective-permute-start | bytes 417800 | tf_op jit(solution)/shard_map/ppermute | solution.py:270
  93.6 8.0 %collective-permute-start.16 = (bf16[32,2176]{1,0:T(8,128)(2,1)S(1)}, bf16[32,2176]{1,0:T(8,128)(2,1)S(1)}, u32[]{:S(2)}, u32[]{:S(2)}) collective-permute-start(bf16[32,2176]{1,0:T(8,128)(2,1)S(1)} %collective-permute-done.11.refs_9_), channel_id=1, source_target_pairs={{0,1},{1,0},{2,3},{3,2},{4,5},{5,4},{6,7},{7,6},{8,9},{9,8},{10,11... | collective-permute-start | bytes 417800 | tf_op jit(solution)/shard_map/ppermute | solution.py:270
  95.1 6.8 %collective-permute-start.14 = (bf16[32,2176]{1,0:T(8,128)(2,1)S(1)}, bf16[32,2176]{1,0:T(8,128)(2,1)S(1)}, u32[]{:S(2)}, u32[]{:S(2)}) collective-permute-start(bf16[32,2176]{1,0:T(8,128)(2,1)S(1)} %collective-permute-done.10.refs_7_), channel_id=1, source_target_pairs={{0,1},{1,0},{2,3},{3,2},{4,5},{5,4},{6,7},{7,6},{8,9},{9,8},{10,11... | collective-permute-start | bytes 417800 | tf_op jit(solution)/shard_map/ppermute | solution.py:270
  99.5 5.6 %collective-permute-start.15 = (bf16[32,2176]{1,0:T(8,128)(2,1)S(1)}, bf16[32,2176]{1,0:T(8,128)(2,1)S(1)}, u32[]{:S(2)}, u32[]{:S(2)}) collective-permute-start(bf16[32,2176]{1,0:T(8,128)(2,1)S(1)} %collective-permute-done.13.refs_8_), channel_id=1, source_target_pairs={{0,1},{1,0},{2,3},{3,2},{4,5},{5,4},{6,7},{7,6},{8,9},{9,8},{10,11... | collective-permute-start | bytes 417800 | tf_op jit(solution)/shard_map/ppermute | solution.py:270
  112.3 11.6 %collective-permute-start.20 = (bf16[64,2048]{1,0:T(8,128)(2,1)S(1)}, bf16[64,2048]{1,0:T(8,128)(2,1)S(1)}, u32[]{:S(2)}, u32[]{:S(2)}) collective-permute-start(bf16[64,2048]{1,0:T(8,128)(2,1)S(1)} %get-tuple-element.34), channel_id=1, source_target_pairs={{0,1},{1,0},{2,3},{3,2},{4,5},{5,4},{6,7},{7,6},{8,9},{9,8},{10,11... | collective-permute-start | bytes 786440 | tf_op jit(solution)/shard_map/ppermute | solution.py:270
  114.1 9.8 %collective-permute-start.18 = (bf16[32,2048]{1,0:T(8,128)(2,1)S(1)}, bf16[32,2048]{1,0:T(8,128)(2,1)S(1)}, u32[]{:S(2)}, u32[]{:S(2)}) collective-permute-start(bf16[32,2048]{1,0:T(8,128)(2,1)S(1)} %get-tuple-element.33), channel_id=1, source_target_pairs={{0,1},{1,0},{2,3},{3,2},{4,5},{5,4},{6,7},{7,6},{8,9},{9,8},{10,11... | collective-permute-start | bytes 393224 | tf_op jit(solution)/shard_map/ppermute | solution.py:270
  114.4 13.9 %collective-permute-start.17 = (bf16[32,2048]{1,0:T(8,128)(2,1)S(1)}, bf16[32,2048]{1,0:T(8,128)(2,1)S(1)}, u32[]{:S(2)}, u32[]{:S(2)}) collective-permute-start(bf16[32,2048]{1,0:T(8,128)(2,1)S(1)} %get-tuple-element.32), channel_id=1, source_target_pairs={{0,1},{1,0},{2,3},{3,2},{4,5},{5,4},{6,7},{7,6},{8,9},{9,8},{10,11... | collective-permute-start | bytes 393224 | tf_op jit(solution)/shard_map/ppermute | solution.py:270
  124.0 7.9 %collective-permute-start.21 = (bf16[32,2048]{1,0:T(8,128)(2,1)S(1)}, bf16[32,2048]{1,0:T(8,128)(2,1)S(1)}, u32[]{:S(2)}, u32[]{:S(2)}) collective-permute-start(bf16[32,2048]{1,0:T(8,128)(2,1)S(1)} %get-tuple-element.38), channel_id=1, source_target_pairs={{0,4},{1,5},{2,6},{3,7},{4,0},{5,1},{6,2},{7,3},{8,12},{9,13},{10,... | collective-permute-start | bytes 393224 | tf_op jit(solution)/shard_map/ppermute | solution.py:270
  127.7 5.0 %collective-permute-start.22 = (bf16[32,2048]{1,0:T(8,128)(2,1)S(1)}, bf16[32,2048]{1,0:T(8,128)(2,1)S(1)}, u32[]{:S(2)}, u32[]{:S(2)}) collective-permute-start(bf16[32,2048]{1,0:T(8,128)(2,1)S(1)} %get-tuple-element.39), channel_id=1, source_target_pairs={{0,2},{1,3},{2,0},{3,1},{4,6},{5,7},{6,4},{7,5},{8,10},{9,11},{10,... | collective-permute-start | bytes 393224 | tf_op jit(solution)/shard_map/ppermute | solution.py:270
  127.7 7.7 %collective-permute-start.19 = (bf16[32,2048]{1,0:T(8,128)(2,1)S(1)}, bf16[32,2048]{1,0:T(8,128)(2,1)S(1)}, u32[]{:S(2)}, u32[]{:S(2)}) collective-permute-start(bf16[32,2048]{1,0:T(8,128)(2,1)S(1)} %get-tuple-element.42), channel_id=1, source_target_pairs={{0,6},{1,7},{2,4},{3,5},{4,2},{5,3},{6,0},{7,1},{8,14},{9,15},{10,... | collective-permute-start | bytes 393224 | tf_op jit(solution)/shard_map/ppermute | solution.py:270
  135.4 7.7 %collective-permute-start.23 = (bf16[16,2048]{1,0:T(8,128)(2,1)S(1)}, bf16[16,2048]{1,0:T(8,128)(2,1)S(1)}, u32[]{:S(2)}, u32[]{:S(2)}) collective-permute-start(bf16[16,2048]{1,0:T(8,128)(2,1)S(1)} %slice.78), channel_id=1, source_target_pairs={{0,14},{1,15},{2,12},{3,13},{4,10},{5,11},{6,8},{7,9},{8,6},{9,7},... | collective-permute-start | bytes 196616 | tf_op jit(solution)/shard_map/ppermute | solution.py:270
  143.3 7.5 %collective-permute-start.24 = (bf16[16,2048]{1,0:T(8,128)(2,1)S(1)}, bf16[16,2048]{1,0:T(8,128)(2,1)S(1)}, u32[]{:S(2)}, u32[]{:S(2)}) collective-permute-start(bf16[16,2048]{1,0:T(8,128)(2,1)S(1)} %shard_map.101), channel_id=1, source_target_pairs={{0,14},{1,15},{2,12},{3,13},{4,10},{5,11},{6,8},{7,9},{8,6},{9,7},... | collective-permute-start | bytes 196616 | tf_op jit(solution)/shard_map/ppermute | solution.py:270
  150.8 6.5 %collective-permute-start.27 = (bf16[32,2048]{1,0:T(8,128)(2,1)S(1)}, bf16[32,2048]{1,0:T(8,128)(2,1)S(1)}, u32[]{:S(2)}, u32[]{:S(2)}) collective-permute-start(bf16[32,2048]{1,0:T(8,128)(2,1)S(1)} %pad_maximum_fusion.refs_0_), channel_id=1, source_target_pairs={{0,1},{1,0},{2,3},{3,2},{4,5},{5,4},{6,7},{7,6},{8,9},{9,8},{10,11... | collective-permute-start | bytes 393224 | tf_op jit(solution)/shard_map/ppermute | solution.py:270
  151.7 6.6 %collective-permute-start.26 = (bf16[32,2048]{1,0:T(8,128)(2,1)S(1)}, bf16[32,2048]{1,0:T(8,128)(2,1)S(1)}, u32[]{:S(2)}, u32[]{:S(2)}) collective-permute-start(bf16[32,2048]{1,0:T(8,128)(2,1)S(1)} %pad_maximum_fusion.refs_0_), channel_id=1, source_target_pairs={{0,6},{1,7},{2,4},{3,5},{4,2},{5,3},{6,0},{7,1},{8,14},{9,15},{10,... | collective-permute-start | bytes 393224 | tf_op jit(solution)/shard_map/ppermute | solution.py:270
  154.2 5.1 %collective-permute-start.25 = (bf16[32,2048]{1,0:T(8,128)(2,1)S(1)}, bf16[32,2048]{1,0:T(8,128)(2,1)S(1)}, u32[]{:S(2)}, u32[]{:S(2)}) collective-permute-start(bf16[32,2048]{1,0:T(8,128)(2,1)S(1)} %pad_maximum_fusion.refs_0_), channel_id=1, source_target_pairs={{0,2},{1,3},{2,0},{3,1},{4,6},{5,7},{6,4},{7,5},{8,10},{9,11},{10,... | collective-permute-start | bytes 393224 | tf_op jit(solution)/shard_map/ppermute | solution.py:270
  158.3 6.0 %collective-permute-start.28 = (bf16[32,2048]{1,0:T(8,128)(2,1)S(1)}, bf16[32,2048]{1,0:T(8,128)(2,1)S(1)}, u32[]{:S(2)}, u32[]{:S(2)}) collective-permute-start(bf16[32,2048]{1,0:T(8,128)(2,1)S(1)} %pad_maximum_fusion.refs_0_), channel_id=1, source_target_pairs={{0,4},{1,5},{2,6},{3,7},{4,0},{5,1},{6,2},{7,3},{8,12},{9,13},{10,... | collective-permute-start | bytes 393224 | tf_op jit(solution)/shard_map/ppermute | solution.py:270
  158.3 7.5 %collective-permute-start.31 = (bf16[32,2048]{1,0:T(8,128)(2,1)S(1)}, bf16[32,2048]{1,0:T(8,128)(2,1)S(1)}, u32[]{:S(2)}, u32[]{:S(2)}) collective-permute-start(bf16[32,2048]{1,0:T(8,128)(2,1)S(1)} %collective-permute-done.26.refs_3_), channel_id=1, source_target_pairs={{0,1},{1,0},{2,3},{3,2},{4,5},{5,4},{6,7},{7,6},{8,9},{9,8},{10,11... | collective-permute-start | bytes 393224 | tf_op jit(solution)/shard_map/ppermute | solution.py:270
  159.3 6.6 %collective-permute-start.29 = (bf16[32,2048]{1,0:T(8,128)(2,1)S(1)}, bf16[32,2048]{1,0:T(8,128)(2,1)S(1)}, u32[]{:S(2)}, u32[]{:S(2)}) collective-permute-start(bf16[32,2048]{1,0:T(8,128)(2,1)S(1)} %collective-permute-done.25.refs_1_), channel_id=1, source_target_pairs={{0,1},{1,0},{2,3},{3,2},{4,5},{5,4},{6,7},{7,6},{8,9},{9,8},{10,11... | collective-permute-start | bytes 393224 | tf_op jit(solution)/shard_map/ppermute | solution.py:270
  164.3 5.0 %collective-permute-start.30 = (bf16[32,2048]{1,0:T(8,128)(2,1)S(1)}, bf16[32,2048]{1,0:T(8,128)(2,1)S(1)}, u32[]{:S(2)}, u32[]{:S(2)}) collective-permute-start(bf16[32,2048]{1,0:T(8,128)(2,1)S(1)} %collective-permute-done.28.refs_2_), channel_id=1, source_target_pairs={{0,1},{1,0},{2,3},{3,2},{4,5},{5,4},{6,7},{7,6},{8,9},{9,8},{10,11... | collective-permute-start | bytes 393224 | tf_op jit(solution)/shard_map/ppermute | solution.py:270

commit v6 on v5

--- a/solution.py
+++ b/solution.py
@@ -148,41 +148,46 @@
     for row, vector in zip((START, END, PENALTY, STEP), vectors):
         table[row : row + 1, :] = vector[...].astype(jnp.float32)
     by_gene[...] = table[...].T
-    own = rows_of(person(where), 0)
+    low, high = slice(0, OWN), slice(OWN, 2 * OWN)
     width = coef.shape[1]
     for block in range(width // LANES):
         cols = slice(block * LANES, (block + 1) * LANES)
         mask = block_mask(where, by_gene[...], block, width // 4)
         coef[:, cols] = (mask * coef_start[:, cols]).astype(jnp.bfloat16)
-        mask = block_mask(where, by_gene[own, :], block, width // 4)
-        coef_own[:, cols] = mask * coef_start[own, cols]
+        for part, hop in ((low, 0), (high, MIRROR)):
+            rows = rows_of(person(where), hop)
+            mask = block_mask(where, by_gene[rows, :], block, width // 4)
+            coef_own[part, cols] = mask * coef_start[rows, cols]
 
 
 def update_kernel(total, first, where, by_gene, near, far, coef_own, base, *refs):
-    own = rows_of(person(where), 0)
-    table = by_gene[own, :]
     width = coef_own.shape[1]
-    penalty, step = table[:, PENALTY : PENALTY + 1], table[:, STEP : STEP + 1]
-    cut = step * penalty
     lane = lax.broadcasted_iota(jnp.int32, (OWN, LANES), 1)
-    high = low = jnp.zeros((OWN, LANES), jnp.float32)
-    for block in range(width // LANES):
-        cols = slice(block * LANES, (block + 1) * LANES)
-        mask = block_mask(where, table, block, width // 4)
-        used = base[own, cols] if first else base[:, cols]
-        grad = (near[:OWN, cols] + far[:, cols].astype(jnp.float32)) / total - used.astype(jnp.float32)
-        moved = coef_own[:, cols] + step * grad
-        size = jnp.maximum(jnp.abs(moved) - cut * l1_share, 0.0)
-        kept = mask * jnp.where(moved < 0, -size, size) / (1.0 + cut * (1.0 - l1_share))
+    for half, hop in enumerate((0, MIRROR)):
+        rows = rows_of(person(where), hop)
+        part, other = slice(half * OWN, (half + 1) * OWN), slice((1 - half) * OWN, (2 - half) * OWN)
+        table = by_gene[rows, :]
+        penalty, step = table[:, PENALTY : PENALTY + 1], table[:, STEP : STEP + 1]
+        cut = step * penalty
+        high = low = jnp.zeros((OWN, LANES), jnp.float32)
+        for block in range(width // LANES):
+            cols = slice(block * LANES, (block + 1) * LANES)
+            mask = block_mask(where, table, block, width // 4)
+            used = base[rows, cols] if first else base[part, cols]
+            sums = near[part, cols].astype(jnp.float32) + far[other, cols].astype(jnp.float32)
+            grad = sums / total - used.astype(jnp.float32)
+            moved = coef_own[part, cols] + step * grad
+            size = jnp.maximum(jnp.abs(moved) - cut * l1_share, 0.0)
+            kept = mask * jnp.where(moved < 0, -size, size) / (1.0 + cut * (1.0 - l1_share))
+            if first:
+                refs[0][part, cols] = kept
+                peak = jnp.max(mask * jnp.abs(grad) / penalty, axis=1, keepdims=True)
+                rounded = peak.astype(jnp.bfloat16).astype(jnp.float32)
+                high = jnp.where(lane == block, rounded, high)
+                low = jnp.where(lane == block + width // LANES, peak - rounded, low)
+            refs[-1][part, cols] = kept.astype(jnp.bfloat16)
         if first:
-            refs[0][:, cols] = kept
-            peak = jnp.max(mask * jnp.abs(grad) / penalty, axis=1, keepdims=True)
-            rounded = peak.astype(jnp.bfloat16).astype(jnp.float32)
-            high = jnp.where(lane == block, rounded, high)
-            low = jnp.where(lane == block + width // LANES, peak - rounded, low)
-        refs[-1][:, cols] = kept.astype(jnp.bfloat16)
-    if first:
-        refs[-1][:, width:] = (high + low).astype(jnp.bfloat16)
+            refs[-1][part, width:] = (high + low).astype(jnp.bfloat16)
 
 
 def output_kernel(where, *refs):
@@ -280,11 +285,11 @@
     total = part[0]
     for hop in (6, 4, 2):
         total = total + swap(part[hop].astype(jnp.bfloat16), hop)
-    return total, swap(total[OWN:].astype(jnp.bfloat16), MIRROR)
-
-
-def gather_rows(own):
-    pair = jnp.concatenate([own, swap(own, MIRROR)], axis=0)
+    near = total.astype(jnp.bfloat16)
+    return near, swap(near, MIRROR)
+
+
+def gather_rows(pair):
     got = {0: pair, 2: swap(pair, 2), 6: swap(pair, 6)}
     beside = swap(pair, SIDE)
     pair, *_ = lax.optimization_barrier((pair, got[6], beside))
@@ -309,7 +314,7 @@
         start_kernel,
         where,
         [active_blocks.T, *vectors, coef_start],
-        [((genes, LANES), jnp.float32), ((genes, width), jnp.bfloat16), ((OWN, width), jnp.float32)],
+        [((genes, LANES), jnp.float32), ((genes, width), jnp.bfloat16), ((2 * OWN, width), jnp.float32)],
         [pltpu.VMEM((LANES, genes), jnp.float32)],
     )
 
@@ -324,7 +329,7 @@
         functools.partial(update_kernel, total, True),
         where,
         [by_gene, near, far, coef_own, coef],
-        [((OWN, width), jnp.float32), ((OWN, width + LANES), jnp.bfloat16)],
+        [((2 * OWN, width), jnp.float32), ((2 * OWN, width + LANES), jnp.bfloat16)],
     )
     pieces = gather_rows(sent)
 
@@ -334,7 +339,7 @@
         functools.partial(update_kernel, total, False),
         where,
         [by_gene, near, far, coef_own, sent],
-        [((OWN, width), jnp.bfloat16)],
+        [((2 * OWN, width), jnp.bfloat16)],
     )
     pieces = gather_rows(last)
     coef = pl.pallas_call(

time: 172 us -> 165 us (0.959)
  starting transfers between devices: 50.8 us -> 38.2 us
  waiting for transfers between devices: 95.9 us -> 101 us
    ppermute x30 -> x28, starting transfers between devices: 48 us -> 35.4 us  [swap(): return lax.ppermute(block, 'people', [(i, i ^ hop) for i in range(count)])]
    ppermute x30 -> x28, waiting for transfers between devices: 64.8 us -> 70 us  [swap(): return lax.ppermute(block, 'people', [(i, i ^ hop) for i in range(count)])]
  transfers between devices with their start and end apart: 32 -> 30, of which waited for: 23 -> 21; matrix products, arithmetic and copies ran while one was open for 0% -> 0% of each run, Pallas kernels for 3% -> 3%
where the time goes in v6:
time: 165 us
  waiting for transfers between devices  101 us (61%)
  starting transfers between devices  38.2 us (23%)
  Pallas kernels  23.7 us (14%)
    ppermute x28, waiting for transfers between devices, swap(): return lax.ppermute(block, 'people', [(i, i ^ hop) for i in range(count)])  70 us
    ppermute x28, starting transfers between devices, swap(): return lax.ppermute(block, 'people', [(i, i ^ hop) for i in range(count)])  35.4 us
    ppermute x1, waiting for transfers between devices, on_device(): slow = lax.ppermute(away, 'genome', beyond)  30.3 us
    pallas_call x2, Pallas kernels, local_grad(): pl.pallas_call(functools.partial(turn_kernel, len(pieces)), out_shape=out...  11.7 us
    pallas_call x3, Pallas kernels, small_call(): pl.pallas_call(kernel, out_shape=[pltpu.VMEM(shape, dtype) for shape, dty...  4.84 us
  transfers between devices with their start and end apart: 30, of which 21 were waited for; matrix products, arithmetic and copies ran while one was open for 0% of the time, Pallas kernels for 3%

profile of v6, /device:TPU:56, one launch (start us, length us, event | category | flops | bytes accessed | tf_op | source)
XLA Modules:
  0.0 164.6 jit_solution(3609600221695379372)
XLA Ops:
  0.7 3.0 %shard_map.96 = (bf16[3072,512]{1,0:T(8,128)(2,1)S(1)}, bf16[3072,512]{1,0:T(8,128)(2,1)S(1)}) custom-call(s32[1]{0:T(128)} %bitcast.where.refs_0_, bf16[3072,1024]{1,0:T(8,128)(2,1)} %whole.1), custom_call_target="tpu_custom_call" | custom-call | tf_op jit(solution)/shard_map/pallas_call | solution.py:213
  3.7 0.1 collective-permute-start.1
  3.8 2.7 %collective-permute-start = (bf16[3072,512]{1,0:T(8,128)(2,1)S(1)}, bf16[3072,512]{1,0:T(8,128)(2,1)S(1)}, u32[]{:S(2)}, u32[]{:S(2)}) collective-permute-start(bf16[3072,512]{1,0:T(8,128)(2,1)S(1)} %get-tuple-element.21.second.refs_2_), channel_id=1, source_target_pairs={{16,32},{32,16},{48,64},{64,48},{80,96},{96,80},{112,128},{128,112... | collective-permute-start | bytes 9437192 | tf_op jit(solution)/shard_map/ppermute | solution.py:322
  6.6 2.2 %shard_map.95 = (f32[256,128]{1,0:T(8,128)S(1)}, bf16[256,2048]{1,0:T(8,128)(2,1)S(1)}, f32[32,2048]{1,0:T(8,128)S(1)}) custom-call(s32[1]{0:T(128)} %bitcast.where.refs_0_, s32[16,256]{1,0:T(8,128)S(1)} %bitcast.8, s32[1,256]{1,0:T(1,128)S(1)} %bitcast.9, s32[1,256]{1,0:T(1,128)S(1)} %bitcast.10, f32[1,256]{1,0:T(1,128)S(1)} %bitcast.11, ...), custom_call_target="tpu_custom_call" | custom-call | tf_op jit(solution)/shard_map/pallas_call | solution.py:263
  8.9 0.6 collective-permute-done.1.fourth.refs_4_
  9.5 2.6 %shard_map.97.refs_5_ = f32[3072,256]{1,0:T(8,128)S(1)} custom-call(s32[1]{0:T(128)} %bitcast.where.refs_0_, bf16[3072,512]{1,0:T(8,128)(2,1)S(1)} %get-tuple-element.21.second.refs_2_, bf16[3072,512]{1,0:T(8,128)(2,1)S(1)} %get-tuple-element.22.third.refs_3_, bf16[3072,512]{1,0:T(8,128)(2,1)S(1)} %collective-permute-done.1.fourth.refs_4_, ...), custom_call_target="tpu_custom_call" | custom-call | tf_op jit(solution)/shard_map/pallas_call | solution.py:230
  12.1 30.3 %collective-permute-done.refs_1_ = bf16[3072,512]{1,0:T(8,128)(2,1)S(1)} collective-permute-done((bf16[3072,512]{1,0:T(8,128)(2,1)S(1)}, bf16[3072,512]{1,0:T(8,128)(2,1)S(1)}, u32[]{:S(2)}, u32[]{:S(2)}) %collective-permute-start) | collective-permute-done | bytes 3145760 | tf_op jit(solution)/shard_map/ppermute | solution.py:322
  42.4 4.6 %shard_map.98 = (f32[128,2048]{1,0:T(8,128)S(1)}, bf16[32,2048]{1,0:T(8,128)(2,1)S(1)}, bf16[64,2048]{1,0:T(8,128)(2,1)S(1)}, bf16[32,2048]{1,0:T(8,128)(2,1)S(1)}) custom-call(s32[1]{0:T(128)} %bitcast.where.refs_0_, bf16[3072,512]{1,0:T(8,128)(2,1)S(1)} %collective-permute-done.refs_1_, bf16[3072,512]{1,0:T(8,128)(2,1)S(1)} %get-tuple-element.21.second.refs_2_, ...), custom_call_target="tpu_custom_call" | custom-call | flops 6442450944 | tf_op jit(solution)/shard_map/pallas_call | solution.py:251
  47.0 1.6 collective-permute-start.5
  48.6 0.5 collective-permute-start.3
  49.1 1.5 collective-permute-start.2
  50.6 5.3 %collective-permute-done.3 = bf16[32,2048]{1,0:T(8,128)(2,1)S(1)} collective-permute-done((bf16[32,2048]{1,0:T(8,128)(2,1)S(1)}, bf16[32,2048]{1,0:T(8,128)(2,1)S(1)}, u32[]{:S(2)}, u32[]{:S(2)}) %collective-permute-start.3) | collective-permute-done | bytes 131104 | tf_op jit(solution)/shard_map/ppermute | solution.py:275
  55.9 0.1 add_convert_fusion.6
  56.0 3.4 %collective-permute-start.6 = (bf16[32,2048]{1,0:T(8,128)(2,1)S(1)}, bf16[32,2048]{1,0:T(8,128)(2,1)S(1)}, u32[]{:S(2)}, u32[]{:S(2)}) collective-permute-start(bf16[32,2048]{1,0:T(8,128)(2,1)S(1)} %get-tuple-element.40), channel_id=1, source_target_pairs={{0,4},{1,5},{2,6},{3,7},{4,0},{5,1},{6,2},{7,3},{8,12},{9,13},{10,... | collective-permute-start | bytes 393224 | tf_op jit(solution)/shard_map/ppermute | solution.py:275
  59.4 0.1 collective-permute-start.7
  59.5 0.6 collective-permute-start.4
  60.1 2.7 %collective-permute-done.6 = bf16[32,2048]{1,0:T(8,128)(2,1)S(1)} collective-permute-done((bf16[32,2048]{1,0:T(8,128)(2,1)S(1)}, bf16[32,2048]{1,0:T(8,128)(2,1)S(1)}, u32[]{:S(2)}, u32[]{:S(2)}) %collective-permute-start.6) | collective-permute-done | bytes 131104 | tf_op jit(solution)/shard_map/ppermute | solution.py:275
  62.8 1.6 collective-permute-done.7
  64.4 4.0 %collective-permute-done.4 = bf16[32,2048]{1,0:T(8,128)(2,1)S(1)} collective-permute-done((bf16[32,2048]{1,0:T(8,128)(2,1)S(1)}, bf16[32,2048]{1,0:T(8,128)(2,1)S(1)}, u32[]{:S(2)}, u32[]{:S(2)}) %collective-permute-start.4) | collective-permute-done | bytes 131104 | tf_op jit(solution)/shard_map/ppermute | solution.py:275
  68.4 0.1 add_convert_fusion.4.near
  68.5 5.5 %collective-permute-start.8 = (bf16[32,2048]{1,0:T(8,128)(2,1)S(1)}, bf16[32,2048]{1,0:T(8,128)(2,1)S(1)}, u32[]{:S(2)}, u32[]{:S(2)}) collective-permute-start(bf16[32,2048]{1,0:T(8,128)(2,1)S(1)} %add_convert_fusion.4.near), channel_id=1, source_target_pairs={{0,14},{1,15},{2,12},{3,13},{4,10},{5,11},{6,8},{7,9},{8,6},{9,7},... | collective-permute-start | bytes 393224 | tf_op jit(solution)/shard_map/ppermute | solution.py:275
  74.0 3.0 %collective-permute-done.8.far = bf16[32,2048]{1,0:T(8,128)(2,1)S(1)} collective-permute-done((bf16[32,2048]{1,0:T(8,128)(2,1)S(1)}, bf16[32,2048]{1,0:T(8,128)(2,1)S(1)}, u32[]{:S(2)}, u32[]{:S(2)}) %collective-permute-start.8) | collective-permute-done | bytes 131104 | tf_op jit(solution)/shard_map/ppermute | solution.py:275
  77.0 2.3 %shard_map.99 = (f32[32,2048]{1,0:T(8,128)S(1)}, bf16[32,2176]{1,0:T(8,128)(2,1)S(1)}) custom-call(s32[1]{0:T(128)} %bitcast.where.refs_0_, f32[256,128]{1,0:T(8,128)S(1)} %get-tuple-element.20.by_gene, bf16[32,2048]{1,0:T(8,128)(2,1)S(1)} %add_convert_fusion.4.near, bf16[32,2048]{1,0:T(8,128)(2,1)S(1)} %collective-permute-done.8.far, ...), custom_call_target="tpu_custom_call" | custom-call | tf_op jit(solution)/shard_map/pallas_call | solution.py:263
  79.3 1.6 collective-permute-start.11
  80.9 3.6 %collective-permute-start.10 = (bf16[32,2176]{1,0:T(8,128)(2,1)S(1)}, bf16[32,2176]{1,0:T(8,128)(2,1)S(1)}, u32[]{:S(2)}, u32[]{:S(2)}) collective-permute-start(bf16[32,2176]{1,0:T(8,128)(2,1)S(1)} %get-tuple-element.30.refs_6_.base), channel_id=1, source_target_pairs={{0,6},{1,7},{2,4},{3,5},{4,2},{5,3},{6,0},{7,1},{8,14},{9,15},{10,... | collective-permute-start | bytes 417800 | tf_op jit(solution)/shard_map/ppermute | solution.py:275
  84.4 5.6 %collective-permute-done.10.refs_9_ = bf16[32,2176]{1,0:T(8,128)(2,1)S(1)} collective-permute-done((bf16[32,2176]{1,0:T(8,128)(2,1)S(1)}, bf16[32,2176]{1,0:T(8,128)(2,1)S(1)}, u32[]{:S(2)}, u32[]{:S(2)}) %collective-permute-start.10) | collective-permute-done | bytes 139296 | tf_op jit(solution)/shard_map/ppermute | solution.py:275
  90.1 0.4 collective-permute-start.15
  90.5 0.4 collective-permute-done.9.refs_7_
  90.9 1.2 collective-permute-start.13
  92.1 4.2 %collective-permute-done.12.refs_8_ = bf16[32,2176]{1,0:T(8,128)(2,1)S(1)} collective-permute-done((bf16[32,2176]{1,0:T(8,128)(2,1)S(1)}, bf16[32,2176]{1,0:T(8,128)(2,1)S(1)}, u32[]{:S(2)}, u32[]{:S(2)}) %collective-permute-start.12) | collective-permute-done | bytes 139296 | tf_op jit(solution)/shard_map/ppermute | solution.py:275
  96.3 0.6 collective-permute-start.14
  96.9 1.9 %collective-permute-done.13.refs_11_ = bf16[32,2176]{1,0:T(8,128)(2,1)S(1)} collective-permute-done((bf16[32,2176]{1,0:T(8,128)(2,1)S(1)}, bf16[32,2176]{1,0:T(8,128)(2,1)S(1)}, u32[]{:S(2)}, u32[]{:S(2)}) %collective-permute-start.13) | collective-permute-done | bytes 139296 | tf_op jit(solution)/shard_map/ppermute | solution.py:275
  98.8 4.0 %collective-permute-done.14.refs_12_ = bf16[32,2176]{1,0:T(8,128)(2,1)S(1)} collective-permute-done((bf16[32,2176]{1,0:T(8,128)(2,1)S(1)}, bf16[32,2176]{1,0:T(8,128)(2,1)S(1)}, u32[]{:S(2)}, u32[]{:S(2)}) %collective-permute-start.14) | collective-permute-done | bytes 139296 | tf_op jit(solution)/shard_map/ppermute | solution.py:275
  102.8 7.1 %shard_map.100 = (f32[128,2048]{1,0:T(8,128)S(1)}, bf16[32,2048]{1,0:T(8,128)(2,1)S(1)}, bf16[64,2048]{1,0:T(8,128)(2,1)S(1)}, bf16[32,2048]{1,0:T(8,128)(2,1)S(1)}, f32[16,256]{1,0:T(8,128)S(1)}) custom-call(s32[1]{0:T(128)} %bitcast.where.refs_0_, bf16[3072,512]{1,0:T(8,128)(2,1)S(1)} %collective-permute-done.refs_1_, ...), custom_call_target="tpu_custom_call" | custom-call | flops 6442450944 | tf_op jit(solution)/shard_map/pallas_call | solution.py:251
  110.0 0.5 collective-permute-start.19
  110.5 1.6 collective-permute-start.17
  112.1 0.4 collective-permute-start.16
  112.5 9.5 %collective-permute-done.17 = bf16[32,2048]{1,0:T(8,128)(2,1)S(1)} collective-permute-done((bf16[32,2048]{1,0:T(8,128)(2,1)S(1)}, bf16[32,2048]{1,0:T(8,128)(2,1)S(1)}, u32[]{:S(2)}, u32[]{:S(2)}) %collective-permute-start.17) | collective-permute-done | bytes 131104 | tf_op jit(solution)/shard_map/ppermute | solution.py:275
  122.0 0.1 add_convert_fusion.2
  122.1 3.2 %collective-permute-start.20 = (bf16[32,2048]{1,0:T(8,128)(2,1)S(1)}, bf16[32,2048]{1,0:T(8,128)(2,1)S(1)}, u32[]{:S(2)}, u32[]{:S(2)}) collective-permute-start(bf16[32,2048]{1,0:T(8,128)(2,1)S(1)} %get-tuple-element.38), channel_id=1, source_target_pairs={{0,4},{1,5},{2,6},{3,7},{4,0},{5,1},{6,2},{7,3},{8,12},{9,13},{10,... | collective-permute-start | bytes 393224 | tf_op jit(solution)/shard_map/ppermute | solution.py:275
  125.3 0.3 collective-permute-start.21
  125.5 1.4 collective-permute-start.18
  126.9 4.1 %collective-permute-done.20 = bf16[32,2048]{1,0:T(8,128)(2,1)S(1)} collective-permute-done((bf16[32,2048]{1,0:T(8,128)(2,1)S(1)}, bf16[32,2048]{1,0:T(8,128)(2,1)S(1)}, u32[]{:S(2)}, u32[]{:S(2)}) %collective-permute-start.20) | collective-permute-done | bytes 131104 | tf_op jit(solution)/shard_map/ppermute | solution.py:275
  131.0 0.7 collective-permute-done.21
  131.7 4.0 %collective-permute-done.18 = bf16[32,2048]{1,0:T(8,128)(2,1)S(1)} collective-permute-done((bf16[32,2048]{1,0:T(8,128)(2,1)S(1)}, bf16[32,2048]{1,0:T(8,128)(2,1)S(1)}, u32[]{:S(2)}, u32[]{:S(2)}) %collective-permute-start.18) | collective-permute-done | bytes 131104 | tf_op jit(solution)/shard_map/ppermute | solution.py:275
  135.7 0.1 add_convert_fusion.near
  135.7 2.0 %collective-permute-start.22 = (bf16[32,2048]{1,0:T(8,128)(2,1)S(1)}, bf16[32,2048]{1,0:T(8,128)(2,1)S(1)}, u32[]{:S(2)}, u32[]{:S(2)}) collective-permute-start(bf16[32,2048]{1,0:T(8,128)(2,1)S(1)} %add_convert_fusion.near), channel_id=1, source_target_pairs={{0,14},{1,15},{2,12},{3,13},{4,10},{5,11},{6,8},{7,9},{8,6},{9,7},... | collective-permute-start | bytes 393224 | tf_op jit(solution)/shard_map/ppermute | solution.py:275
  137.7 6.4 %collective-permute-done.22.far = bf16[32,2048]{1,0:T(8,128)(2,1)S(1)} collective-permute-done((bf16[32,2048]{1,0:T(8,128)(2,1)S(1)}, bf16[32,2048]{1,0:T(8,128)(2,1)S(1)}, u32[]{:S(2)}, u32[]{:S(2)}) %collective-permute-start.22) | collective-permute-done | bytes 131104 | tf_op jit(solution)/shard_map/ppermute | solution.py:275
  144.2 0.3 shard_map.101.refs_0_
  144.5 0.6 collective-permute-start.25
  145.1 0.6 collective-permute-start.24
  145.7 0.0 collective-permute-start.23
  145.7 5.1 %collective-permute-done.25.refs_4_ = bf16[32,2048]{1,0:T(8,128)(2,1)S(1)} collective-permute-done((bf16[32,2048]{1,0:T(8,128)(2,1)S(1)}, bf16[32,2048]{1,0:T(8,128)(2,1)S(1)}, u32[]{:S(2)}, u32[]{:S(2)}) %collective-permute-start.25) | collective-permute-done | bytes 131104 | tf_op jit(solution)/shard_map/ppermute | solution.py:275
  150.8 1.5 collective-permute-done.24.refs_3_
  152.3 0.0 collective-permute-start.26
  152.3 2.1 %collective-permute-start.29 = (bf16[32,2048]{1,0:T(8,128)(2,1)S(1)}, bf16[32,2048]{1,0:T(8,128)(2,1)S(1)}, u32[]{:S(2)}, u32[]{:S(2)}) collective-permute-start(bf16[32,2048]{1,0:T(8,128)(2,1)S(1)} %collective-permute-done.24.refs_3_), channel_id=1, source_target_pairs={{0,1},{1,0},{2,3},{3,2},{4,5},{5,4},{6,7},{7,6},{8,9},{9,8},{10,11... | collective-permute-start | bytes 393224 | tf_op jit(solution)/shard_map/ppermute | solution.py:275
  154.4 0.1 collective-permute-start.27
  154.5 3.7 %collective-permute-done.26.refs_2_ = bf16[32,2048]{1,0:T(8,128)(2,1)S(1)} collective-permute-done((bf16[32,2048]{1,0:T(8,128)(2,1)S(1)}, bf16[32,2048]{1,0:T(8,128)(2,1)S(1)}, u32[]{:S(2)}, u32[]{:S(2)}) %collective-permute-start.26) | collective-permute-done | bytes 131104 | tf_op jit(solution)/shard_map/ppermute | solution.py:275
  158.1 2.1 %collective-permute-start.28 = (bf16[32,2048]{1,0:T(8,128)(2,1)S(1)}, bf16[32,2048]{1,0:T(8,128)(2,1)S(1)}, u32[]{:S(2)}, u32[]{:S(2)}) collective-permute-start(bf16[32,2048]{1,0:T(8,128)(2,1)S(1)} %collective-permute-done.26.refs_2_), channel_id=1, source_target_pairs={{0,1},{1,0},{2,3},{3,2},{4,5},{5,4},{6,7},{7,6},{8,9},{9,8},{10,11... | collective-permute-start | bytes 393224 | tf_op jit(solution)/shard_map/ppermute | solution.py:275
  160.2 0.6 copy.10
  160.8 0.0 collective-permute-done.29.refs_7_
  160.8 0.0 collective-permute-done.27.refs_5_
  160.8 2.3 %collective-permute-done.28.refs_6_ = bf16[32,2048]{1,0:T(8,128)(2,1)S(1)} collective-permute-done((bf16[32,2048]{1,0:T(8,128)(2,1)S(1)}, bf16[32,2048]{1,0:T(8,128)(2,1)S(1)}, u32[]{:S(2)}, u32[]{:S(2)}) %collective-permute-start.28) | collective-permute-done | bytes 131104 | tf_op jit(solution)/shard_map/ppermute | solution.py:275
  163.2 1.5 shard_map.102
  (23 shorter events, 0.1 us)
Async XLA Ops:
  0.6 5.9 %copy-start = (f32[256,2048]{1,0:T(8,128)S(1)}, f32[256,2048]{1,0:T(8,128)}, u32[]{:S(2)}) copy-start(f32[256,2048]{1,0:T(8,128)} %refs_4_.1) | copy-start | bytes 6291460
  0.6 5.9 %copy-start.2 = (s32[256,16]{0,1:T(8,128)S(1)}, s32[256,16]{0,1:T(8,128)}, u32[]{:S(2)}) copy-start(s32[256,16]{0,1:T(8,128)} %param.15) | copy-start | bytes 49156
  0.7 5.9 %copy-start.3 = (s32[256]{0:T(256)S(1)}, s32[256]{0:T(256)}, u32[]{:S(2)}) copy-start(s32[256]{0:T(256)} %param.13) | copy-start | bytes 3076
  0.7 5.9 %copy-start.4 = (s32[256]{0:T(256)S(1)}, s32[256]{0:T(256)}, u32[]{:S(2)}) copy-start(s32[256]{0:T(256)} %param.14) | copy-start | bytes 3076
  0.7 5.9 %copy-start.5 = (f32[256]{0:T(256)S(1)}, f32[256]{0:T(256)}, u32[]{:S(2)}) copy-start(f32[256]{0:T(256)} %param.11) | copy-start | bytes 3076
  0.7 5.9 %copy-start.6 = (f32[256]{0:T(256)S(1)}, f32[256]{0:T(256)}, u32[]{:S(2)}) copy-start(f32[256]{0:T(256)} %param.12) | copy-start | bytes 3076
  0.7 8.8 %copy-start.1 = (bf16[3072,256]{1,0:T(8,128)(2,1)S(1)}, bf16[3072,256]{1,0:T(8,128)(2,1)}, u32[]{:S(2)}) copy-start(bf16[3072,256]{1,0:T(8,128)(2,1)} %refs_5_.1) | copy-start | bytes 4718596
  3.7 5.7 %collective-permute-start.1 = (bf16[3072,512]{1,0:T(8,128)(2,1)S(1)}, bf16[3072,512]{1,0:T(8,128)(2,1)S(1)}, u32[]{:S(2)}, u32[]{:S(2)}) collective-permute-start(bf16[3072,512]{1,0:T(8,128)(2,1)S(1)} %get-tuple-element.22.third.refs_3_), channel_id=1, source_target_pairs={{0,16},{16,0},{32,48},{48,32},{64,80},{80,64},{96,112},{112,96},{1... | collective-permute-start | bytes 9437192 | tf_op jit(solution)/shard_map/ppermute | solution.py:323
  3.8 38.6 %collective-permute-start = (bf16[3072,512]{1,0:T(8,128)(2,1)S(1)}, bf16[3072,512]{1,0:T(8,128)(2,1)S(1)}, u32[]{:S(2)}, u32[]{:S(2)}) collective-permute-start(bf16[3072,512]{1,0:T(8,128)(2,1)S(1)} %get-tuple-element.21.second.refs_2_), channel_id=1, source_target_pairs={{16,32},{32,16},{48,64},{64,48},{80,96},{96,80},{112,128},{128,112... | collective-permute-start | bytes 9437192 | tf_op jit(solution)/shard_map/ppermute | solution.py:322
  47.0 8.9 %collective-permute-start.5 = (bf16[64,2048]{1,0:T(8,128)(2,1)S(1)}, bf16[64,2048]{1,0:T(8,128)(2,1)S(1)}, u32[]{:S(2)}, u32[]{:S(2)}) collective-permute-start(bf16[64,2048]{1,0:T(8,128)(2,1)S(1)} %get-tuple-element.27), channel_id=1, source_target_pairs={{0,1},{1,0},{2,3},{3,2},{4,5},{5,4},{6,7},{7,6},{8,9},{9,8},{10,11... | collective-permute-start | bytes 786440 | tf_op jit(solution)/shard_map/ppermute | solution.py:275
  48.6 7.3 %collective-permute-start.3 = (bf16[32,2048]{1,0:T(8,128)(2,1)S(1)}, bf16[32,2048]{1,0:T(8,128)(2,1)S(1)}, u32[]{:S(2)}, u32[]{:S(2)}) collective-permute-start(bf16[32,2048]{1,0:T(8,128)(2,1)S(1)} %get-tuple-element.26), channel_id=1, source_target_pairs={{0,1},{1,0},{2,3},{3,2},{4,5},{5,4},{6,7},{7,6},{8,9},{9,8},{10,11... | collective-permute-start | bytes 393224 | tf_op jit(solution)/shard_map/ppermute | solution.py:275
  49.1 10.9 %collective-permute-start.2 = (bf16[32,2048]{1,0:T(8,128)(2,1)S(1)}, bf16[32,2048]{1,0:T(8,128)(2,1)S(1)}, u32[]{:S(2)}, u32[]{:S(2)}) collective-permute-start(bf16[32,2048]{1,0:T(8,128)(2,1)S(1)} %get-tuple-element.25), channel_id=1, source_target_pairs={{0,1},{1,0},{2,3},{3,2},{4,5},{5,4},{6,7},{7,6},{8,9},{9,8},{10,11... | collective-permute-start | bytes 393224 | tf_op jit(solution)/shard_map/ppermute | solution.py:275
  56.0 6.8 %collective-permute-start.6 = (bf16[32,2048]{1,0:T(8,128)(2,1)S(1)}, bf16[32,2048]{1,0:T(8,128)(2,1)S(1)}, u32[]{:S(2)}, u32[]{:S(2)}) collective-permute-start(bf16[32,2048]{1,0:T(8,128)(2,1)S(1)} %get-tuple-element.40), channel_id=1, source_target_pairs={{0,4},{1,5},{2,6},{3,7},{4,0},{5,1},{6,2},{7,3},{8,12},{9,13},{10,... | collective-permute-start | bytes 393224 | tf_op jit(solution)/shard_map/ppermute | solution.py:275
  59.4 5.0 %collective-permute-start.7 = (bf16[32,2048]{1,0:T(8,128)(2,1)S(1)}, bf16[32,2048]{1,0:T(8,128)(2,1)S(1)}, u32[]{:S(2)}, u32[]{:S(2)}) collective-permute-start(bf16[32,2048]{1,0:T(8,128)(2,1)S(1)} %get-tuple-element.41), channel_id=1, source_target_pairs={{0,2},{1,3},{2,0},{3,1},{4,6},{5,7},{6,4},{7,5},{8,10},{9,11},{10,... | collective-permute-start | bytes 393224 | tf_op jit(solution)/shard_map/ppermute | solution.py:275
  59.5 8.9 %collective-permute-start.4 = (bf16[32,2048]{1,0:T(8,128)(2,1)S(1)}, bf16[32,2048]{1,0:T(8,128)(2,1)S(1)}, u32[]{:S(2)}, u32[]{:S(2)}) collective-permute-start(bf16[32,2048]{1,0:T(8,128)(2,1)S(1)} %get-tuple-element.43), channel_id=1, source_target_pairs={{0,6},{1,7},{2,4},{3,5},{4,2},{5,3},{6,0},{7,1},{8,14},{9,15},{10,... | collective-permute-start | bytes 393224 | tf_op jit(solution)/shard_map/ppermute | solution.py:275
  68.5 8.5 %collective-permute-start.8 = (bf16[32,2048]{1,0:T(8,128)(2,1)S(1)}, bf16[32,2048]{1,0:T(8,128)(2,1)S(1)}, u32[]{:S(2)}, u32[]{:S(2)}) collective-permute-start(bf16[32,2048]{1,0:T(8,128)(2,1)S(1)} %add_convert_fusion.4.near), channel_id=1, source_target_pairs={{0,14},{1,15},{2,12},{3,13},{4,10},{5,11},{6,8},{7,9},{8,6},{9,7},... | collective-permute-start | bytes 393224 | tf_op jit(solution)/shard_map/ppermute | solution.py:275
  79.3 5.1 %collective-permute-start.11 = (bf16[32,2176]{1,0:T(8,128)(2,1)S(1)}, bf16[32,2176]{1,0:T(8,128)(2,1)S(1)}, u32[]{:S(2)}, u32[]{:S(2)}) collective-permute-start(bf16[32,2176]{1,0:T(8,128)(2,1)S(1)} %get-tuple-element.30.refs_6_.base), channel_id=1, source_target_pairs={{0,1},{1,0},{2,3},{3,2},{4,5},{5,4},{6,7},{7,6},{8,9},{9,8},{10,11... | collective-permute-start | bytes 417800 | tf_op jit(solution)/shard_map/ppermute | solution.py:275
  80.9 9.2 %collective-permute-start.10 = (bf16[32,2176]{1,0:T(8,128)(2,1)S(1)}, bf16[32,2176]{1,0:T(8,128)(2,1)S(1)}, u32[]{:S(2)}, u32[]{:S(2)}) collective-permute-start(bf16[32,2176]{1,0:T(8,128)(2,1)S(1)} %get-tuple-element.30.refs_6_.base), channel_id=1, source_target_pairs={{0,6},{1,7},{2,4},{3,5},{4,2},{5,3},{6,0},{7,1},{8,14},{9,15},{10,... | collective-permute-start | bytes 417800 | tf_op jit(solution)/shard_map/ppermute | solution.py:275
  84.4 6.5 %collective-permute-start.9 = (bf16[32,2176]{1,0:T(8,128)(2,1)S(1)}, bf16[32,2176]{1,0:T(8,128)(2,1)S(1)}, u32[]{:S(2)}, u32[]{:S(2)}) collective-permute-start(bf16[32,2176]{1,0:T(8,128)(2,1)S(1)} %get-tuple-element.30.refs_6_.base), channel_id=1, source_target_pairs={{0,2},{1,3},{2,0},{3,1},{4,6},{5,7},{6,4},{7,5},{8,10},{9,11},{10,... | collective-permute-start | bytes 417800 | tf_op jit(solution)/shard_map/ppermute | solution.py:275
  90.1 6.2 %collective-permute-start.12 = (bf16[32,2176]{1,0:T(8,128)(2,1)S(1)}, bf16[32,2176]{1,0:T(8,128)(2,1)S(1)}, u32[]{:S(2)}, u32[]{:S(2)}) collective-permute-start(bf16[32,2176]{1,0:T(8,128)(2,1)S(1)} %get-tuple-element.30.refs_6_.base), channel_id=1, source_target_pairs={{0,4},{1,5},{2,6},{3,7},{4,0},{5,1},{6,2},{7,3},{8,12},{9,13},{10,... | collective-permute-start | bytes 417800 | tf_op jit(solution)/shard_map/ppermute | solution.py:275
  90.1 6.8 %collective-permute-start.15 = (bf16[32,2176]{1,0:T(8,128)(2,1)S(1)}, bf16[32,2176]{1,0:T(8,128)(2,1)S(1)}, u32[]{:S(2)}, u32[]{:S(2)}) collective-permute-start(bf16[32,2176]{1,0:T(8,128)(2,1)S(1)} %collective-permute-done.10.refs_9_), channel_id=1, source_target_pairs={{0,1},{1,0},{2,3},{3,2},{4,5},{5,4},{6,7},{7,6},{8,9},{9,8},{10,11... | collective-permute-start | bytes 417800 | tf_op jit(solution)/shard_map/ppermute | solution.py:275
  90.9 7.9 %collective-permute-start.13 = (bf16[32,2176]{1,0:T(8,128)(2,1)S(1)}, bf16[32,2176]{1,0:T(8,128)(2,1)S(1)}, u32[]{:S(2)}, u32[]{:S(2)}) collective-permute-start(bf16[32,2176]{1,0:T(8,128)(2,1)S(1)} %collective-permute-done.9.refs_7_), channel_id=1, source_target_pairs={{0,1},{1,0},{2,3},{3,2},{4,5},{5,4},{6,7},{7,6},{8,9},{9,8},{10,11... | collective-permute-start | bytes 417800 | tf_op jit(solution)/shard_map/ppermute | solution.py:275
  96.3 6.5 %collective-permute-start.14 = (bf16[32,2176]{1,0:T(8,128)(2,1)S(1)}, bf16[32,2176]{1,0:T(8,128)(2,1)S(1)}, u32[]{:S(2)}, u32[]{:S(2)}) collective-permute-start(bf16[32,2176]{1,0:T(8,128)(2,1)S(1)} %collective-permute-done.12.refs_8_), channel_id=1, source_target_pairs={{0,1},{1,0},{2,3},{3,2},{4,5},{5,4},{6,7},{7,6},{8,9},{9,8},{10,11... | collective-permute-start | bytes 417800 | tf_op jit(solution)/shard_map/ppermute | solution.py:275
  110.0 12.1 %collective-permute-start.19 = (bf16[64,2048]{1,0:T(8,128)(2,1)S(1)}, bf16[64,2048]{1,0:T(8,128)(2,1)S(1)}, u32[]{:S(2)}, u32[]{:S(2)}) collective-permute-start(bf16[64,2048]{1,0:T(8,128)(2,1)S(1)} %get-tuple-element.34), channel_id=1, source_target_pairs={{0,1},{1,0},{2,3},{3,2},{4,5},{5,4},{6,7},{7,6},{8,9},{9,8},{10,11... | collective-permute-start | bytes 786440 | tf_op jit(solution)/shard_map/ppermute | solution.py:275
  110.5 11.5 %collective-permute-start.17 = (bf16[32,2048]{1,0:T(8,128)(2,1)S(1)}, bf16[32,2048]{1,0:T(8,128)(2,1)S(1)}, u32[]{:S(2)}, u32[]{:S(2)}) collective-permute-start(bf16[32,2048]{1,0:T(8,128)(2,1)S(1)} %get-tuple-element.33), channel_id=1, source_target_pairs={{0,1},{1,0},{2,3},{3,2},{4,5},{5,4},{6,7},{7,6},{8,9},{9,8},{10,11... | collective-permute-start | bytes 393224 | tf_op jit(solution)/shard_map/ppermute | solution.py:275
  112.1 14.8 %collective-permute-start.16 = (bf16[32,2048]{1,0:T(8,128)(2,1)S(1)}, bf16[32,2048]{1,0:T(8,128)(2,1)S(1)}, u32[]{:S(2)}, u32[]{:S(2)}) collective-permute-start(bf16[32,2048]{1,0:T(8,128)(2,1)S(1)} %get-tuple-element.32), channel_id=1, source_target_pairs={{0,1},{1,0},{2,3},{3,2},{4,5},{5,4},{6,7},{7,6},{8,9},{9,8},{10,11... | collective-permute-start | bytes 393224 | tf_op jit(solution)/shard_map/ppermute | solution.py:275
  122.1 8.8 %collective-permute-start.20 = (bf16[32,2048]{1,0:T(8,128)(2,1)S(1)}, bf16[32,2048]{1,0:T(8,128)(2,1)S(1)}, u32[]{:S(2)}, u32[]{:S(2)}) collective-permute-start(bf16[32,2048]{1,0:T(8,128)(2,1)S(1)} %get-tuple-element.38), channel_id=1, source_target_pairs={{0,4},{1,5},{2,6},{3,7},{4,0},{5,1},{6,2},{7,3},{8,12},{9,13},{10,... | collective-permute-start | bytes 393224 | tf_op jit(solution)/shard_map/ppermute | solution.py:275
  125.3 6.4 %collective-permute-start.21 = (bf16[32,2048]{1,0:T(8,128)(2,1)S(1)}, bf16[32,2048]{1,0:T(8,128)(2,1)S(1)}, u32[]{:S(2)}, u32[]{:S(2)}) collective-permute-start(bf16[32,2048]{1,0:T(8,128)(2,1)S(1)} %get-tuple-element.39), channel_id=1, source_target_pairs={{0,2},{1,3},{2,0},{3,1},{4,6},{5,7},{6,4},{7,5},{8,10},{9,11},{10,... | collective-permute-start | bytes 393224 | tf_op jit(solution)/shard_map/ppermute | solution.py:275
  125.5 10.1 %collective-permute-start.18 = (bf16[32,2048]{1,0:T(8,128)(2,1)S(1)}, bf16[32,2048]{1,0:T(8,128)(2,1)S(1)}, u32[]{:S(2)}, u32[]{:S(2)}) collective-permute-start(bf16[32,2048]{1,0:T(8,128)(2,1)S(1)} %get-tuple-element.42), channel_id=1, source_target_pairs={{0,6},{1,7},{2,4},{3,5},{4,2},{5,3},{6,0},{7,1},{8,14},{9,15},{10,... | collective-permute-start | bytes 393224 | tf_op jit(solution)/shard_map/ppermute | solution.py:275
  135.7 8.4 %collective-permute-start.22 = (bf16[32,2048]{1,0:T(8,128)(2,1)S(1)}, bf16[32,2048]{1,0:T(8,128)(2,1)S(1)}, u32[]{:S(2)}, u32[]{:S(2)}) collective-permute-start(bf16[32,2048]{1,0:T(8,128)(2,1)S(1)} %add_convert_fusion.near), channel_id=1, source_target_pairs={{0,14},{1,15},{2,12},{3,13},{4,10},{5,11},{6,8},{7,9},{8,6},{9,7},... | collective-permute-start | bytes 393224 | tf_op jit(solution)/shard_map/ppermute | solution.py:275
  144.5 6.3 %collective-permute-start.25 = (bf16[32,2048]{1,0:T(8,128)(2,1)S(1)}, bf16[32,2048]{1,0:T(8,128)(2,1)S(1)}, u32[]{:S(2)}, u32[]{:S(2)}) collective-permute-start(bf16[32,2048]{1,0:T(8,128)(2,1)S(1)} %shard_map.101.refs_0_), channel_id=1, source_target_pairs={{0,1},{1,0},{2,3},{3,2},{4,5},{5,4},{6,7},{7,6},{8,9},{9,8},{10,11... | collective-permute-start | bytes 393224 | tf_op jit(solution)/shard_map/ppermute | solution.py:275
  145.1 7.2 %collective-permute-start.24 = (bf16[32,2048]{1,0:T(8,128)(2,1)S(1)}, bf16[32,2048]{1,0:T(8,128)(2,1)S(1)}, u32[]{:S(2)}, u32[]{:S(2)}) collective-permute-start(bf16[32,2048]{1,0:T(8,128)(2,1)S(1)} %shard_map.101.refs_0_), channel_id=1, source_target_pairs={{0,6},{1,7},{2,4},{3,5},{4,2},{5,3},{6,0},{7,1},{8,14},{9,15},{10,... | collective-permute-start | bytes 393224 | tf_op jit(solution)/shard_map/ppermute | solution.py:275
  145.7 8.7 %collective-permute-start.23 = (bf16[32,2048]{1,0:T(8,128)(2,1)S(1)}, bf16[32,2048]{1,0:T(8,128)(2,1)S(1)}, u32[]{:S(2)}, u32[]{:S(2)}) collective-permute-start(bf16[32,2048]{1,0:T(8,128)(2,1)S(1)} %shard_map.101.refs_0_), channel_id=1, source_target_pairs={{0,2},{1,3},{2,0},{3,1},{4,6},{5,7},{6,4},{7,5},{8,10},{9,11},{10,... | collective-permute-start | bytes 393224 | tf_op jit(solution)/shard_map/ppermute | solution.py:275
  152.3 5.9 %collective-permute-start.26 = (bf16[32,2048]{1,0:T(8,128)(2,1)S(1)}, bf16[32,2048]{1,0:T(8,128)(2,1)S(1)}, u32[]{:S(2)}, u32[]{:S(2)}) collective-permute-start(bf16[32,2048]{1,0:T(8,128)(2,1)S(1)} %shard_map.101.refs_0_), channel_id=1, source_target_pairs={{0,4},{1,5},{2,6},{3,7},{4,0},{5,1},{6,2},{7,3},{8,12},{9,13},{10,... | collective-permute-start | bytes 393224 | tf_op jit(solution)/shard_map/ppermute | solution.py:275
  152.3 8.6 %collective-permute-start.29 = (bf16[32,2048]{1,0:T(8,128)(2,1)S(1)}, bf16[32,2048]{1,0:T(8,128)(2,1)S(1)}, u32[]{:S(2)}, u32[]{:S(2)}) collective-permute-start(bf16[32,2048]{1,0:T(8,128)(2,1)S(1)} %collective-permute-done.24.refs_3_), channel_id=1, source_target_pairs={{0,1},{1,0},{2,3},{3,2},{4,5},{5,4},{6,7},{7,6},{8,9},{9,8},{10,11... | collective-permute-start | bytes 393224 | tf_op jit(solution)/shard_map/ppermute | solution.py:275
  154.4 6.5 %collective-permute-start.27 = (bf16[32,2048]{1,0:T(8,128)(2,1)S(1)}, bf16[32,2048]{1,0:T(8,128)(2,1)S(1)}, u32[]{:S(2)}, u32[]{:S(2)}) collective-permute-start(bf16[32,2048]{1,0:T(8,128)(2,1)S(1)} %collective-permute-done.23.refs_1_), channel_id=1, source_target_pairs={{0,1},{1,0},{2,3},{3,2},{4,5},{5,4},{6,7},{7,6},{8,9},{9,8},{10,11... | collective-permute-start | bytes 393224 | tf_op jit(solution)/shard_map/ppermute | solution.py:275
  158.1 5.0 %collective-permute-start.28 = (bf16[32,2048]{1,0:T(8,128)(2,1)S(1)}, bf16[32,2048]{1,0:T(8,128)(2,1)S(1)}, u32[]{:S(2)}, u32[]{:S(2)}) collective-permute-start(bf16[32,2048]{1,0:T(8,128)(2,1)S(1)} %collective-permute-done.26.refs_2_), channel_id=1, source_target_pairs={{0,1},{1,0},{2,3},{3,2},{4,5},{5,4},{6,7},{7,6},{8,9},{9,8},{10,11... | collective-permute-start | bytes 393224 | tf_op jit(solution)/shard_map/ppermute | solution.py:275

commit v7 on v6

--- a/solution.py
+++ b/solution.py
@@ -92,16 +92,12 @@
     width = 4 * reach
     me = person(where)
     if n_pieces > 1:
-        peaks, grad, resid_t, coef, tail = refs
+        grad, resid_t, coef = refs
 
         def put(rows, piece):
-            coef[rows, :] = piece[:, :width]
-            tail[rows, :] = piece[:, width:]
+            coef[rows, :] = piece[...]
 
         place(me, pieces, put)
-        count = peaks.shape[0]
-        flat = tail[...].astype(jnp.float32).T
-        peaks[...] = flat[:count, :] + flat[count : 2 * count, :]
     else:
         (coef,) = pieces
         grad, resid_t = refs
@@ -160,43 +156,64 @@
             coef_own[part, cols] = mask * coef_start[rows, cols]
 
 
+def gradient(total, near, far, half, cols, used):
+    part, other = slice(half * OWN, (half + 1) * OWN), slice((1 - half) * OWN, (2 - half) * OWN)
+    sums = near[part, cols].astype(jnp.float32) + far[other, cols].astype(jnp.float32)
+    return sums / total - used.astype(jnp.float32)
+
+
 def update_kernel(total, first, where, by_gene, near, far, coef_own, base, *refs):
     width = coef_own.shape[1]
+    for half, hop in enumerate((0, MIRROR)):
+        rows, part = rows_of(person(where), hop), slice(half * OWN, (half + 1) * OWN)
+        table = by_gene[rows, :]
+        penalty, step = table[:, PENALTY : PENALTY + 1], table[:, STEP : STEP + 1]
+        cut = step * penalty
+        for block in range(width // LANES):
+            cols = slice(block * LANES, (block + 1) * LANES)
+            mask = block_mask(where, table, block, width // 4)
+            used = base[rows, cols] if first else base[part, cols]
+            moved = coef_own[part, cols] + step * gradient(total, near, far, half, cols, used)
+            size = jnp.maximum(jnp.abs(moved) - cut * l1_share, 0.0)
+            kept = mask * jnp.where(moved < 0, -size, size) / (1.0 + cut * (1.0 - l1_share))
+            if first:
+                refs[0][part, cols] = kept
+            refs[-1][part, cols] = kept.astype(jnp.bfloat16)
+    if not first:
+        refs[-1][:, width:] = refs[0][...]
+
+
+def peaks_kernel(total, where, by_gene, near, far, base, out):
+    width = near.shape[1]
     lane = lax.broadcasted_iota(jnp.int32, (OWN, LANES), 1)
     for half, hop in enumerate((0, MIRROR)):
         rows = rows_of(person(where), hop)
-        part, other = slice(half * OWN, (half + 1) * OWN), slice((1 - half) * OWN, (2 - half) * OWN)
         table = by_gene[rows, :]
-        penalty, step = table[:, PENALTY : PENALTY + 1], table[:, STEP : STEP + 1]
-        cut = step * penalty
         high = low = jnp.zeros((OWN, LANES), jnp.float32)
         for block in range(width // LANES):
             cols = slice(block * LANES, (block + 1) * LANES)
             mask = block_mask(where, table, block, width // 4)
-            used = base[rows, cols] if first else base[part, cols]
-            sums = near[part, cols].astype(jnp.float32) + far[other, cols].astype(jnp.float32)
-            grad = sums / total - used.astype(jnp.float32)
-            moved = coef_own[part, cols] + step * grad
-            size = jnp.maximum(jnp.abs(moved) - cut * l1_share, 0.0)
-            kept = mask * jnp.where(moved < 0, -size, size) / (1.0 + cut * (1.0 - l1_share))
-            if first:
-                refs[0][part, cols] = kept
-                peak = jnp.max(mask * jnp.abs(grad) / penalty, axis=1, keepdims=True)
-                rounded = peak.astype(jnp.bfloat16).astype(jnp.float32)
-                high = jnp.where(lane == block, rounded, high)
-                low = jnp.where(lane == block + width // LANES, peak - rounded, low)
-            refs[-1][part, cols] = kept.astype(jnp.bfloat16)
-        if first:
-            refs[-1][part, width:] = (high + low).astype(jnp.bfloat16)
+            grad = gradient(total, near, far, half, cols, base[rows, cols])
+            scaled = mask * jnp.abs(grad) / table[:, PENALTY : PENALTY + 1]
+            peak = jnp.max(scaled, axis=1, keepdims=True)
+            rounded = peak.astype(jnp.bfloat16).astype(jnp.float32)
+            high = jnp.where(lane == block, rounded, high)
+            low = jnp.where(lane == block + width // LANES, peak - rounded, low)
+        out[half * OWN : (half + 1) * OWN, :] = (high + low).astype(jnp.bfloat16)
 
 
 def output_kernel(where, *refs):
-    *pieces, out = refs
+    *pieces, out, peaks, tail = refs
+    width = out.shape[1]
 
     def put(rows, piece):
-        out[rows, :] = piece.astype(jnp.float32)
+        out[rows, :] = piece[:, :width].astype(jnp.float32)
+        tail[rows, :] = piece[:, width:].astype(jnp.float32)
 
     place(person(where), pieces, put)
+    count = peaks.shape[0]
+    flat = tail[...].T
+    peaks[...] = flat[:count, :] + flat[count : 2 * count, :]
 
 
 def in_vmem(array):
@@ -245,9 +262,7 @@
     outs += [pltpu.VMEM((2 * OWN * len(hops), width), jnp.bfloat16) for hops in GIVE]
     scratch = [pltpu.VMEM((genes, width), jnp.float32), pltpu.VMEM((genes, people), jnp.bfloat16)]
     if len(pieces) > 1:
-        outs.append(pltpu.VMEM((width // LANES, genes), jnp.float32))
         scratch.append(pltpu.VMEM((genes, width), jnp.bfloat16))
-        scratch.append(pltpu.VMEM((genes, LANES), jnp.bfloat16))
     return pl.pallas_call(
         functools.partial(turn_kernel, len(pieces)),
         out_shape=outs,
@@ -278,6 +293,8 @@
 def sum_to_owner(keep, gives):
     part = {}
     for hops, give in zip(GIVE, gives):
+        if hops == GIVE[-1]:
+            give, *_ = lax.optimization_barrier((give, got))
         got = swap(give, SIDE)
         for n, hop in enumerate(hops):
             at = NEAR.index(hop) * 2 * OWN
@@ -329,24 +346,34 @@
         functools.partial(update_kernel, total, True),
         where,
         [by_gene, near, far, coef_own, coef],
-        [((2 * OWN, width), jnp.float32), ((2 * OWN, width + LANES), jnp.bfloat16)],
+        [((2 * OWN, width), jnp.float32), ((2 * OWN, width), jnp.bfloat16)],
     )
     pieces = gather_rows(sent)
-
-    keep, *gives, peaks = local_grad(where, blocks, expression, pieces)
+    (tail,) = small_call(
+        functools.partial(peaks_kernel, total),
+        where,
+        [by_gene, near, far, coef],
+        [((2 * OWN, LANES), jnp.bfloat16)],
+    )
+
+    keep, *gives = local_grad(where, blocks, expression, pieces)
     near, far = sum_to_owner(keep, gives)
     (last,) = small_call(
         functools.partial(update_kernel, total, False),
         where,
-        [by_gene, near, far, coef_own, sent],
-        [((2 * OWN, width), jnp.bfloat16)],
+        [by_gene, near, far, coef_own, sent, tail],
+        [((2 * OWN, width + LANES), jnp.bfloat16)],
     )
     pieces = gather_rows(last)
-    coef = pl.pallas_call(
+    coef, peaks = pl.pallas_call(
         output_kernel,
-        out_shape=jax.ShapeDtypeStruct((genes, width), jnp.float32),
+        out_shape=[
+            jax.ShapeDtypeStruct((genes, width), jnp.float32),
+            jax.ShapeDtypeStruct((width // LANES, genes), jnp.float32),
+        ],
         in_specs=specs(len(pieces)),
-        out_specs=pl.BlockSpec(memory_space=pltpu.VMEM),
+        out_specs=[pl.BlockSpec(memory_space=pltpu.VMEM)] * 2,
+        scratch_shapes=[pltpu.VMEM((genes, LANES), jnp.float32)],
         compiler_params=pltpu.CompilerParams(vmem_limit_bytes=8 << 20),
     )(where, *[in_vmem(piece) for piece in pieces])
     return (coef, peaks.T)

time: 165 us -> 163 us (0.988)
  waiting for transfers between devices: 101 us -> 95.1 us
  starting transfers between devices: 38.2 us -> 42.9 us
    ppermute x28, waiting for transfers between devices: 70 us -> 64.2 us  [swap(): return lax.ppermute(block, 'people', [(i, i ^ hop) for i in range(count)])]
    ppermute x28, starting transfers between devices: 35.4 us -> 40.1 us  [swap(): return lax.ppermute(block, 'people', [(i, i ^ hop) for i in range(count)])]
    pallas_call x3 -> x4, Pallas kernels: 4.84 us -> 5.02 us  [small_call(): pl.pallas_call(kernel, out_shape=[pltpu.VMEM(shape, dtype) for shape, dty...]
  transfers between devices with their start and end apart: 30 -> 30, of which waited for: 21 -> 25; matrix products, arithmetic and copies ran while one was open for 0% -> 0% of each run, Pallas kernels for 3% -> 4%
where the time goes in v7:
time: 163 us
  waiting for transfers between devices  95.1 us (58%)
  starting transfers between devices  42.9 us (26%)
  Pallas kernels  23.9 us (15%)
    ppermute x28, waiting for transfers between devices, swap(): return lax.ppermute(block, 'people', [(i, i ^ hop) for i in range(count)])  64.2 us
    ppermute x28, starting transfers between devices, swap(): return lax.ppermute(block, 'people', [(i, i ^ hop) for i in range(count)])  40.1 us
    ppermute x1, waiting for transfers between devices, on_device(): slow = lax.ppermute(away, 'genome', beyond)  30.3 us
    pallas_call x2, Pallas kernels, local_grad(): pl.pallas_call(functools.partial(turn_kernel, len(pieces)), out_shape=out...  11.7 us
    pallas_call x4, Pallas kernels, small_call(): pl.pallas_call(kernel, out_shape=[pltpu.VMEM(shape, dtype) for shape, dty...  5.02 us
  transfers between devices with their start and end apart: 30, of which 25 were waited for; matrix products, arithmetic and copies ran while one was open for 0% of the time, Pallas kernels for 4%

profile of v7, /device:TPU:56, one launch (start us, length us, event | category | flops | bytes accessed | tf_op | source)
XLA Modules:
  0.0 163.1 jit_solution(5894595932550426718)
XLA Ops:
  0.7 3.0 %shard_map.96 = (bf16[3072,512]{1,0:T(8,128)(2,1)S(1)}, bf16[3072,512]{1,0:T(8,128)(2,1)S(1)}) custom-call(s32[1]{0:T(128)} %bitcast.where.refs_0_, bf16[3072,1024]{1,0:T(8,128)(2,1)} %whole.1), custom_call_target="tpu_custom_call" | custom-call | tf_op jit(solution)/shard_map/pallas_call | solution.py:230
  3.7 0.1 collective-permute-start.1
  3.8 2.7 %collective-permute-start = (bf16[3072,512]{1,0:T(8,128)(2,1)S(1)}, bf16[3072,512]{1,0:T(8,128)(2,1)S(1)}, u32[]{:S(2)}, u32[]{:S(2)}) collective-permute-start(bf16[3072,512]{1,0:T(8,128)(2,1)S(1)} %get-tuple-element.24.second.refs_2_), channel_id=1, source_target_pairs={{16,32},{32,16},{48,64},{64,48},{80,96},{96,80},{112,128},{128,112... | collective-permute-start | bytes 9437192 | tf_op jit(solution)/shard_map/ppermute | solution.py:339
  6.6 2.2 %shard_map.95 = (f32[256,128]{1,0:T(8,128)S(1)}, bf16[256,2048]{1,0:T(8,128)(2,1)S(1)}, f32[32,2048]{1,0:T(8,128)S(1)}) custom-call(s32[1]{0:T(128)} %bitcast.where.refs_0_, s32[16,256]{1,0:T(8,128)S(1)} %bitcast.7, s32[1,256]{1,0:T(1,128)S(1)} %bitcast.8, s32[1,256]{1,0:T(1,128)S(1)} %bitcast.9, f32[1,256]{1,0:T(1,128)S(1)} %bitcast.10, ...), custom_call_target="tpu_custom_call" | custom-call | tf_op jit(solution)/shard_map/pallas_call | solution.py:278
  8.9 0.6 collective-permute-done.1.fourth.refs_4_
  9.5 2.6 %shard_map.97.refs_5_ = f32[3072,256]{1,0:T(8,128)S(1)} custom-call(s32[1]{0:T(128)} %bitcast.where.refs_0_, bf16[3072,512]{1,0:T(8,128)(2,1)S(1)} %get-tuple-element.24.second.refs_2_, bf16[3072,512]{1,0:T(8,128)(2,1)S(1)} %get-tuple-element.25.third.refs_3_, bf16[3072,512]{1,0:T(8,128)(2,1)S(1)} %collective-permute-done.1.fourth.refs_4_, ...), custom_call_target="tpu_custom_call" | custom-call | tf_op jit(solution)/shard_map/pallas_call | solution.py:247
  12.1 30.3 %collective-permute-done.refs_1_ = bf16[3072,512]{1,0:T(8,128)(2,1)S(1)} collective-permute-done((bf16[3072,512]{1,0:T(8,128)(2,1)S(1)}, bf16[3072,512]{1,0:T(8,128)(2,1)S(1)}, u32[]{:S(2)}, u32[]{:S(2)}) %collective-permute-start) | collective-permute-done | bytes 3145760 | tf_op jit(solution)/shard_map/ppermute | solution.py:339
  42.4 4.6 %shard_map.98 = (f32[128,2048]{1,0:T(8,128)S(1)}, bf16[32,2048]{1,0:T(8,128)(2,1)S(1)}, bf16[64,2048]{1,0:T(8,128)(2,1)S(1)}, bf16[32,2048]{1,0:T(8,128)(2,1)S(1)}) custom-call(s32[1]{0:T(128)} %bitcast.where.refs_0_, bf16[3072,512]{1,0:T(8,128)(2,1)S(1)} %collective-permute-done.refs_1_, bf16[3072,512]{1,0:T(8,128)(2,1)S(1)} %get-tuple-element.24.second.refs_2_, ...), custom_call_target="tpu_custom_call" | custom-call | flops 6442450944 | tf_op jit(solution)/shard_map/pallas_call | solution.py:266
  47.0 1.6 collective-permute-start.2
  48.6 0.5 collective-permute-start.4
  49.1 4.3 %collective-permute-done.2 = bf16[64,2048]{1,0:T(8,128)(2,1)S(1)} collective-permute-done((bf16[64,2048]{1,0:T(8,128)(2,1)S(1)}, bf16[64,2048]{1,0:T(8,128)(2,1)S(1)}, u32[]{:S(2)}, u32[]{:S(2)}) %collective-permute-start.2) | collective-permute-done | bytes 262176 | tf_op jit(solution)/shard_map/ppermute | solution.py:290
  53.5 1.5 collective-permute-start.3
  55.0 0.9 collective-permute-done.4
  56.0 3.4 %collective-permute-start.6 = (bf16[32,2048]{1,0:T(8,128)(2,1)S(1)}, bf16[32,2048]{1,0:T(8,128)(2,1)S(1)}, u32[]{:S(2)}, u32[]{:S(2)}) collective-permute-start(bf16[32,2048]{1,0:T(8,128)(2,1)S(1)} %get-tuple-element.46), channel_id=1, source_target_pairs={{0,4},{1,5},{2,6},{3,7},{4,0},{5,1},{6,2},{7,3},{8,12},{9,13},{10,... | collective-permute-start | bytes 393224 | tf_op jit(solution)/shard_map/ppermute | solution.py:290
  59.4 0.1 collective-permute-start.7
  59.5 0.6 collective-permute-start.5
  60.0 2.8 %collective-permute-done.6 = bf16[32,2048]{1,0:T(8,128)(2,1)S(1)} collective-permute-done((bf16[32,2048]{1,0:T(8,128)(2,1)S(1)}, bf16[32,2048]{1,0:T(8,128)(2,1)S(1)}, u32[]{:S(2)}, u32[]{:S(2)}) %collective-permute-start.6) | collective-permute-done | bytes 131104 | tf_op jit(solution)/shard_map/ppermute | solution.py:290
  62.8 1.5 collective-permute-done.7
  64.3 4.1 %collective-permute-done.5 = bf16[32,2048]{1,0:T(8,128)(2,1)S(1)} collective-permute-done((bf16[32,2048]{1,0:T(8,128)(2,1)S(1)}, bf16[32,2048]{1,0:T(8,128)(2,1)S(1)}, u32[]{:S(2)}, u32[]{:S(2)}) %collective-permute-start.5) | collective-permute-done | bytes 131104 | tf_op jit(solution)/shard_map/ppermute | solution.py:290
  68.4 0.1 add_convert_fusion.4.near
  68.5 6.8 %collective-permute-start.8 = (bf16[32,2048]{1,0:T(8,128)(2,1)S(1)}, bf16[32,2048]{1,0:T(8,128)(2,1)S(1)}, u32[]{:S(2)}, u32[]{:S(2)}) collective-permute-start(bf16[32,2048]{1,0:T(8,128)(2,1)S(1)} %add_convert_fusion.4.near), channel_id=1, source_target_pairs={{0,14},{1,15},{2,12},{3,13},{4,10},{5,11},{6,8},{7,9},{8,6},{9,7},... | collective-permute-start | bytes 393224 | tf_op jit(solution)/shard_map/ppermute | solution.py:290
  75.2 3.2 %collective-permute-done.8.far = bf16[32,2048]{1,0:T(8,128)(2,1)S(1)} collective-permute-done((bf16[32,2048]{1,0:T(8,128)(2,1)S(1)}, bf16[32,2048]{1,0:T(8,128)(2,1)S(1)}, u32[]{:S(2)}, u32[]{:S(2)}) %collective-permute-start.8) | collective-permute-done | bytes 131104 | tf_op jit(solution)/shard_map/ppermute | solution.py:290
  78.5 0.3 shard_map.99
  78.8 0.3 collective-permute-start.11
  79.1 3.3 %collective-permute-start.10 = (bf16[32,2048]{1,0:T(8,128)(2,1)S(1)}, bf16[32,2048]{1,0:T(8,128)(2,1)S(1)}, u32[]{:S(2)}, u32[]{:S(2)}) collective-permute-start(bf16[32,2048]{1,0:T(8,128)(2,1)S(1)} %get-tuple-element.34.refs_6_.base), channel_id=1, source_target_pairs={{0,6},{1,7},{2,4},{3,5},{4,2},{5,3},{6,0},{7,1},{8,14},{9,15},{10,... | collective-permute-start | bytes 393224 | tf_op jit(solution)/shard_map/ppermute | solution.py:290
  82.4 2.9 %collective-permute-done.11.refs_10_ = bf16[32,2048]{1,0:T(8,128)(2,1)S(1)} collective-permute-done((bf16[32,2048]{1,0:T(8,128)(2,1)S(1)}, bf16[32,2048]{1,0:T(8,128)(2,1)S(1)}, u32[]{:S(2)}, u32[]{:S(2)}) %collective-permute-start.11) | collective-permute-done | bytes 131104 | tf_op jit(solution)/shard_map/ppermute | solution.py:290
  85.4 2.3 %collective-permute-done.10.refs_9_ = bf16[32,2048]{1,0:T(8,128)(2,1)S(1)} collective-permute-done((bf16[32,2048]{1,0:T(8,128)(2,1)S(1)}, bf16[32,2048]{1,0:T(8,128)(2,1)S(1)}, u32[]{:S(2)}, u32[]{:S(2)}) %collective-permute-start.10) | collective-permute-done | bytes 131104 | tf_op jit(solution)/shard_map/ppermute | solution.py:290
  87.6 0.5 collective-permute-start.15
  88.1 0.6 collective-permute-done.9.refs_7_
  88.7 1.0 collective-permute-start.13
  89.7 4.1 %collective-permute-done.12.refs_8_ = bf16[32,2048]{1,0:T(8,128)(2,1)S(1)} collective-permute-done((bf16[32,2048]{1,0:T(8,128)(2,1)S(1)}, bf16[32,2048]{1,0:T(8,128)(2,1)S(1)}, u32[]{:S(2)}, u32[]{:S(2)}) %collective-permute-start.12) | collective-permute-done | bytes 131104 | tf_op jit(solution)/shard_map/ppermute | solution.py:290
  93.8 0.6 collective-permute-start.14
  94.4 1.3 collective-permute-done.13.refs_11_
  95.7 4.2 %collective-permute-done.14.refs_12_ = bf16[32,2048]{1,0:T(8,128)(2,1)S(1)} collective-permute-done((bf16[32,2048]{1,0:T(8,128)(2,1)S(1)}, bf16[32,2048]{1,0:T(8,128)(2,1)S(1)}, u32[]{:S(2)}, u32[]{:S(2)}) %collective-permute-start.14) | collective-permute-done | bytes 131104 | tf_op jit(solution)/shard_map/ppermute | solution.py:290
  99.9 7.1 %shard_map.100 = (f32[128,2048]{1,0:T(8,128)S(1)}, bf16[32,2048]{1,0:T(8,128)(2,1)S(1)}, bf16[64,2048]{1,0:T(8,128)(2,1)S(1)}, bf16[32,2048]{1,0:T(8,128)(2,1)S(1)}) custom-call(s32[1]{0:T(128)} %bitcast.where.refs_0_, bf16[3072,512]{1,0:T(8,128)(2,1)S(1)} %collective-permute-done.refs_1_, bf16[3072,512]{1,0:T(8,128)(2,1)S(1)} %get-tuple-element.24.second.refs_2_, ...), custom_call_target="tpu_custom_call" | custom-call | flops 6442450944 | tf_op jit(solution)/shard_map/pallas_call | solution.py:266
  107.0 0.7 collective-permute-start.16
  107.7 1.4 collective-permute-start.18
  109.1 7.2 %collective-permute-done.16 = bf16[64,2048]{1,0:T(8,128)(2,1)S(1)} collective-permute-done((bf16[64,2048]{1,0:T(8,128)(2,1)S(1)}, bf16[64,2048]{1,0:T(8,128)(2,1)S(1)}, u32[]{:S(2)}, u32[]{:S(2)}) %collective-permute-start.16) | collective-permute-done | bytes 262176 | tf_op jit(solution)/shard_map/ppermute | solution.py:290
  116.3 0.6 collective-permute-start.17
  116.9 2.2 %collective-permute-done.18 = bf16[32,2048]{1,0:T(8,128)(2,1)S(1)} collective-permute-done((bf16[32,2048]{1,0:T(8,128)(2,1)S(1)}, bf16[32,2048]{1,0:T(8,128)(2,1)S(1)}, u32[]{:S(2)}, u32[]{:S(2)}) %collective-permute-start.18) | collective-permute-done | bytes 131104 | tf_op jit(solution)/shard_map/ppermute | solution.py:290
  119.2 0.1 collective-permute-start.20
  119.3 3.4 %collective-permute-start.21 = (bf16[32,2048]{1,0:T(8,128)(2,1)S(1)}, bf16[32,2048]{1,0:T(8,128)(2,1)S(1)}, u32[]{:S(2)}, u32[]{:S(2)}) collective-permute-start(bf16[32,2048]{1,0:T(8,128)(2,1)S(1)} %get-tuple-element.45), channel_id=1, source_target_pairs={{0,2},{1,3},{2,0},{3,1},{4,6},{5,7},{6,4},{7,5},{8,10},{9,11},{10,... | collective-permute-start | bytes 393224 | tf_op jit(solution)/shard_map/ppermute | solution.py:290
  122.6 1.4 collective-permute-start.19
  124.0 2.6 %collective-permute-done.20 = bf16[32,2048]{1,0:T(8,128)(2,1)S(1)} collective-permute-done((bf16[32,2048]{1,0:T(8,128)(2,1)S(1)}, bf16[32,2048]{1,0:T(8,128)(2,1)S(1)}, u32[]{:S(2)}, u32[]{:S(2)}) %collective-permute-start.20) | collective-permute-done | bytes 131104 | tf_op jit(solution)/shard_map/ppermute | solution.py:290
  126.6 1.5 collective-permute-done.21
  128.2 3.7 %collective-permute-done.19 = bf16[32,2048]{1,0:T(8,128)(2,1)S(1)} collective-permute-done((bf16[32,2048]{1,0:T(8,128)(2,1)S(1)}, bf16[32,2048]{1,0:T(8,128)(2,1)S(1)}, u32[]{:S(2)}, u32[]{:S(2)}) %collective-permute-start.19) | collective-permute-done | bytes 131104 | tf_op jit(solution)/shard_map/ppermute | solution.py:290
  131.8 0.1 add_convert_fusion.near
  131.9 4.7 %collective-permute-start.22 = (bf16[32,2048]{1,0:T(8,128)(2,1)S(1)}, bf16[32,2048]{1,0:T(8,128)(2,1)S(1)}, u32[]{:S(2)}, u32[]{:S(2)}) collective-permute-start(bf16[32,2048]{1,0:T(8,128)(2,1)S(1)} %add_convert_fusion.near), channel_id=1, source_target_pairs={{0,14},{1,15},{2,12},{3,13},{4,10},{5,11},{6,8},{7,9},{8,6},{9,7},... | collective-permute-start | bytes 393224 | tf_op jit(solution)/shard_map/ppermute | solution.py:290
  136.6 2.2 %shard_map.101.refs_0_ = bf16[32,128]{1,0:T(8,128)(2,1)S(1)} custom-call(s32[1]{0:T(128)} %bitcast.where.refs_0_, f32[256,128]{1,0:T(8,128)S(1)} %get-tuple-element.23.by_gene, bf16[32,2048]{1,0:T(8,128)(2,1)S(1)} %add_convert_fusion.4.near, bf16[32,2048]{1,0:T(8,128)(2,1)S(1)} %collective-permute-done.8.far, ...), custom_call_target="tpu_custom_call" | custom-call | tf_op jit(solution)/shard_map/pallas_call | solution.py:278
  138.8 1.4 collective-permute-done.22.far
  140.3 0.3 shard_map.102.refs_0_
  140.6 0.7 collective-permute-start.25
  141.3 1.0 collective-permute-start.24
  142.3 2.3 %collective-permute-start.23 = (bf16[32,2176]{1,0:T(8,128)(2,1)S(1)}, bf16[32,2176]{1,0:T(8,128)(2,1)S(1)}, u32[]{:S(2)}, u32[]{:S(2)}) collective-permute-start(bf16[32,2176]{1,0:T(8,128)(2,1)S(1)} %shard_map.102.refs_0_), channel_id=1, source_target_pairs={{0,2},{1,3},{2,0},{3,1},{4,6},{5,7},{6,4},{7,5},{8,10},{9,11},{10,... | collective-permute-start | bytes 417800 | tf_op jit(solution)/shard_map/ppermute | solution.py:290
  144.6 1.1 collective-permute-done.25.refs_4_
  145.7 4.9 %collective-permute-done.24.refs_3_ = bf16[32,2176]{1,0:T(8,128)(2,1)S(1)} collective-permute-done((bf16[32,2176]{1,0:T(8,128)(2,1)S(1)}, bf16[32,2176]{1,0:T(8,128)(2,1)S(1)}, u32[]{:S(2)}, u32[]{:S(2)}) %collective-permute-start.24) | collective-permute-done | bytes 139296 | tf_op jit(solution)/shard_map/ppermute | solution.py:290
  150.6 0.7 collective-permute-start.26
  151.3 0.2 collective-permute-start.29
  151.6 1.8 %collective-permute-start.27 = (bf16[32,2176]{1,0:T(8,128)(2,1)S(1)}, bf16[32,2176]{1,0:T(8,128)(2,1)S(1)}, u32[]{:S(2)}, u32[]{:S(2)}) collective-permute-start(bf16[32,2176]{1,0:T(8,128)(2,1)S(1)} %collective-permute-done.23.refs_1_), channel_id=1, source_target_pairs={{0,1},{1,0},{2,3},{3,2},{4,5},{5,4},{6,7},{7,6},{8,9},{9,8},{10,11... | collective-permute-start | bytes 417800 | tf_op jit(solution)/shard_map/ppermute | solution.py:290
  153.4 3.2 %collective-permute-done.26.refs_2_ = bf16[32,2176]{1,0:T(8,128)(2,1)S(1)} collective-permute-done((bf16[32,2176]{1,0:T(8,128)(2,1)S(1)}, bf16[32,2176]{1,0:T(8,128)(2,1)S(1)}, u32[]{:S(2)}, u32[]{:S(2)}) %collective-permute-start.26) | collective-permute-done | bytes 139296 | tf_op jit(solution)/shard_map/ppermute | solution.py:290
  156.6 1.0 collective-permute-start.28
  157.5 0.3 collective-permute-done.27.refs_5_
  157.9 3.8 %collective-permute-done.28.refs_6_ = bf16[32,2176]{1,0:T(8,128)(2,1)S(1)} collective-permute-done((bf16[32,2176]{1,0:T(8,128)(2,1)S(1)}, bf16[32,2176]{1,0:T(8,128)(2,1)S(1)}, u32[]{:S(2)}, u32[]{:S(2)}) %collective-permute-start.28) | collective-permute-done | bytes 139296 | tf_op jit(solution)/shard_map/ppermute | solution.py:290
  161.6 1.5 shard_map.103
  (23 shorter events, 0.2 us)
Async XLA Ops:
  0.6 5.9 %copy-start = (f32[256,2048]{1,0:T(8,128)S(1)}, f32[256,2048]{1,0:T(8,128)}, u32[]{:S(2)}) copy-start(f32[256,2048]{1,0:T(8,128)} %refs_4_.1) | copy-start | bytes 6291460
  0.6 5.9 %copy-start.2 = (s32[256,16]{0,1:T(8,128)S(1)}, s32[256,16]{0,1:T(8,128)}, u32[]{:S(2)}) copy-start(s32[256,16]{0,1:T(8,128)} %param.15) | copy-start | bytes 49156
  0.7 5.9 %copy-start.3 = (s32[256]{0:T(256)S(1)}, s32[256]{0:T(256)}, u32[]{:S(2)}) copy-start(s32[256]{0:T(256)} %param.13) | copy-start | bytes 3076
  0.7 5.9 %copy-start.4 = (s32[256]{0:T(256)S(1)}, s32[256]{0:T(256)}, u32[]{:S(2)}) copy-start(s32[256]{0:T(256)} %param.14) | copy-start | bytes 3076
  0.7 5.9 %copy-start.5 = (f32[256]{0:T(256)S(1)}, f32[256]{0:T(256)}, u32[]{:S(2)}) copy-start(f32[256]{0:T(256)} %param.11) | copy-start | bytes 3076
  0.7 5.9 %copy-start.6 = (f32[256]{0:T(256)S(1)}, f32[256]{0:T(256)}, u32[]{:S(2)}) copy-start(f32[256]{0:T(256)} %param.12) | copy-start | bytes 3076
  0.7 8.8 %copy-start.1 = (bf16[3072,256]{1,0:T(8,128)(2,1)S(1)}, bf16[3072,256]{1,0:T(8,128)(2,1)}, u32[]{:S(2)}) copy-start(bf16[3072,256]{1,0:T(8,128)(2,1)} %refs_5_.1) | copy-start | bytes 4718596
  3.7 5.7 %collective-permute-start.1 = (bf16[3072,512]{1,0:T(8,128)(2,1)S(1)}, bf16[3072,512]{1,0:T(8,128)(2,1)S(1)}, u32[]{:S(2)}, u32[]{:S(2)}) collective-permute-start(bf16[3072,512]{1,0:T(8,128)(2,1)S(1)} %get-tuple-element.25.third.refs_3_), channel_id=1, source_target_pairs={{0,16},{16,0},{32,48},{48,32},{64,80},{80,64},{96,112},{112,96},{1... | collective-permute-start | bytes 9437192 | tf_op jit(solution)/shard_map/ppermute | solution.py:340
  3.8 38.6 %collective-permute-start = (bf16[3072,512]{1,0:T(8,128)(2,1)S(1)}, bf16[3072,512]{1,0:T(8,128)(2,1)S(1)}, u32[]{:S(2)}, u32[]{:S(2)}) collective-permute-start(bf16[3072,512]{1,0:T(8,128)(2,1)S(1)} %get-tuple-element.24.second.refs_2_), channel_id=1, source_target_pairs={{16,32},{32,16},{48,64},{64,48},{80,96},{96,80},{112,128},{128,112... | collective-permute-start | bytes 9437192 | tf_op jit(solution)/shard_map/ppermute | solution.py:339
  47.0 6.5 %collective-permute-start.2 = (bf16[64,2048]{1,0:T(8,128)(2,1)S(1)}, bf16[64,2048]{1,0:T(8,128)(2,1)S(1)}, u32[]{:S(2)}, u32[]{:S(2)}) collective-permute-start(bf16[64,2048]{1,0:T(8,128)(2,1)S(1)} %get-tuple-element.29), channel_id=1, source_target_pairs={{0,1},{1,0},{2,3},{3,2},{4,5},{5,4},{6,7},{7,6},{8,9},{9,8},{10,11... | collective-permute-start | bytes 786440 | tf_op jit(solution)/shard_map/ppermute | solution.py:290
  48.6 7.3 %collective-permute-start.4 = (bf16[32,2048]{1,0:T(8,128)(2,1)S(1)}, bf16[32,2048]{1,0:T(8,128)(2,1)S(1)}, u32[]{:S(2)}, u32[]{:S(2)}) collective-permute-start(bf16[32,2048]{1,0:T(8,128)(2,1)S(1)} %get-tuple-element.31), channel_id=1, source_target_pairs={{0,1},{1,0},{2,3},{3,2},{4,5},{5,4},{6,7},{7,6},{8,9},{9,8},{10,11... | collective-permute-start | bytes 393224 | tf_op jit(solution)/shard_map/ppermute | solution.py:290
  53.5 6.5 %collective-permute-start.3 = (bf16[32,2048]{1,0:T(8,128)(2,1)S(1)}, bf16[32,2048]{1,0:T(8,128)(2,1)S(1)}, u32[]{:S(2)}, u32[]{:S(2)}) collective-permute-start(bf16[32,2048]{1,0:T(8,128)(2,1)S(1)} %get-tuple-element.30), channel_id=1, source_target_pairs={{0,1},{1,0},{2,3},{3,2},{4,5},{5,4},{6,7},{7,6},{8,9},{9,8},{10,11... | collective-permute-start | bytes 393224 | tf_op jit(solution)/shard_map/ppermute | solution.py:290
  56.0 6.8 %collective-permute-start.6 = (bf16[32,2048]{1,0:T(8,128)(2,1)S(1)}, bf16[32,2048]{1,0:T(8,128)(2,1)S(1)}, u32[]{:S(2)}, u32[]{:S(2)}) collective-permute-start(bf16[32,2048]{1,0:T(8,128)(2,1)S(1)} %get-tuple-element.46), channel_id=1, source_target_pairs={{0,4},{1,5},{2,6},{3,7},{4,0},{5,1},{6,2},{7,3},{8,12},{9,13},{10,... | collective-permute-start | bytes 393224 | tf_op jit(solution)/shard_map/ppermute | solution.py:290
  59.4 5.0 %collective-permute-start.7 = (bf16[32,2048]{1,0:T(8,128)(2,1)S(1)}, bf16[32,2048]{1,0:T(8,128)(2,1)S(1)}, u32[]{:S(2)}, u32[]{:S(2)}) collective-permute-start(bf16[32,2048]{1,0:T(8,128)(2,1)S(1)} %get-tuple-element.47), channel_id=1, source_target_pairs={{0,2},{1,3},{2,0},{3,1},{4,6},{5,7},{6,4},{7,5},{8,10},{9,11},{10,... | collective-permute-start | bytes 393224 | tf_op jit(solution)/shard_map/ppermute | solution.py:290
  59.5 8.9 %collective-permute-start.5 = (bf16[32,2048]{1,0:T(8,128)(2,1)S(1)}, bf16[32,2048]{1,0:T(8,128)(2,1)S(1)}, u32[]{:S(2)}, u32[]{:S(2)}) collective-permute-start(bf16[32,2048]{1,0:T(8,128)(2,1)S(1)} %get-tuple-element.49), channel_id=1, source_target_pairs={{0,6},{1,7},{2,4},{3,5},{4,2},{5,3},{6,0},{7,1},{8,14},{9,15},{10,... | collective-permute-start | bytes 393224 | tf_op jit(solution)/shard_map/ppermute | solution.py:290
  68.5 10.0 %collective-permute-start.8 = (bf16[32,2048]{1,0:T(8,128)(2,1)S(1)}, bf16[32,2048]{1,0:T(8,128)(2,1)S(1)}, u32[]{:S(2)}, u32[]{:S(2)}) collective-permute-start(bf16[32,2048]{1,0:T(8,128)(2,1)S(1)} %add_convert_fusion.4.near), channel_id=1, source_target_pairs={{0,14},{1,15},{2,12},{3,13},{4,10},{5,11},{6,8},{7,9},{8,6},{9,7},... | collective-permute-start | bytes 393224 | tf_op jit(solution)/shard_map/ppermute | solution.py:290
  78.8 6.6 %collective-permute-start.11 = (bf16[32,2048]{1,0:T(8,128)(2,1)S(1)}, bf16[32,2048]{1,0:T(8,128)(2,1)S(1)}, u32[]{:S(2)}, u32[]{:S(2)}) collective-permute-start(bf16[32,2048]{1,0:T(8,128)(2,1)S(1)} %get-tuple-element.34.refs_6_.base), channel_id=1, source_target_pairs={{0,1},{1,0},{2,3},{3,2},{4,5},{5,4},{6,7},{7,6},{8,9},{9,8},{10,11... | collective-permute-start | bytes 393224 | tf_op jit(solution)/shard_map/ppermute | solution.py:290
  79.1 8.6 %collective-permute-start.10 = (bf16[32,2048]{1,0:T(8,128)(2,1)S(1)}, bf16[32,2048]{1,0:T(8,128)(2,1)S(1)}, u32[]{:S(2)}, u32[]{:S(2)}) collective-permute-start(bf16[32,2048]{1,0:T(8,128)(2,1)S(1)} %get-tuple-element.34.refs_6_.base), channel_id=1, source_target_pairs={{0,6},{1,7},{2,4},{3,5},{4,2},{5,3},{6,0},{7,1},{8,14},{9,15},{10,... | collective-permute-start | bytes 393224 | tf_op jit(solution)/shard_map/ppermute | solution.py:290
  82.4 6.3 %collective-permute-start.9 = (bf16[32,2048]{1,0:T(8,128)(2,1)S(1)}, bf16[32,2048]{1,0:T(8,128)(2,1)S(1)}, u32[]{:S(2)}, u32[]{:S(2)}) collective-permute-start(bf16[32,2048]{1,0:T(8,128)(2,1)S(1)} %get-tuple-element.34.refs_6_.base), channel_id=1, source_target_pairs={{0,2},{1,3},{2,0},{3,1},{4,6},{5,7},{6,4},{7,5},{8,10},{9,11},{10,... | collective-permute-start | bytes 393224 | tf_op jit(solution)/shard_map/ppermute | solution.py:290
  87.6 6.1 %collective-permute-start.12 = (bf16[32,2048]{1,0:T(8,128)(2,1)S(1)}, bf16[32,2048]{1,0:T(8,128)(2,1)S(1)}, u32[]{:S(2)}, u32[]{:S(2)}) collective-permute-start(bf16[32,2048]{1,0:T(8,128)(2,1)S(1)} %get-tuple-element.34.refs_6_.base), channel_id=1, source_target_pairs={{0,4},{1,5},{2,6},{3,7},{4,0},{5,1},{6,2},{7,3},{8,12},{9,13},{10,... | collective-permute-start | bytes 393224 | tf_op jit(solution)/shard_map/ppermute | solution.py:290
  87.6 6.7 %collective-permute-start.15 = (bf16[32,2048]{1,0:T(8,128)(2,1)S(1)}, bf16[32,2048]{1,0:T(8,128)(2,1)S(1)}, u32[]{:S(2)}, u32[]{:S(2)}) collective-permute-start(bf16[32,2048]{1,0:T(8,128)(2,1)S(1)} %collective-permute-done.10.refs_9_), channel_id=1, source_target_pairs={{0,1},{1,0},{2,3},{3,2},{4,5},{5,4},{6,7},{7,6},{8,9},{9,8},{10,11... | collective-permute-start | bytes 393224 | tf_op jit(solution)/shard_map/ppermute | solution.py:290
  88.7 7.0 %collective-permute-start.13 = (bf16[32,2048]{1,0:T(8,128)(2,1)S(1)}, bf16[32,2048]{1,0:T(8,128)(2,1)S(1)}, u32[]{:S(2)}, u32[]{:S(2)}) collective-permute-start(bf16[32,2048]{1,0:T(8,128)(2,1)S(1)} %collective-permute-done.9.refs_7_), channel_id=1, source_target_pairs={{0,1},{1,0},{2,3},{3,2},{4,5},{5,4},{6,7},{7,6},{8,9},{9,8},{10,11... | collective-permute-start | bytes 393224 | tf_op jit(solution)/shard_map/ppermute | solution.py:290
  93.8 6.1 %collective-permute-start.14 = (bf16[32,2048]{1,0:T(8,128)(2,1)S(1)}, bf16[32,2048]{1,0:T(8,128)(2,1)S(1)}, u32[]{:S(2)}, u32[]{:S(2)}) collective-permute-start(bf16[32,2048]{1,0:T(8,128)(2,1)S(1)} %collective-permute-done.12.refs_8_), channel_id=1, source_target_pairs={{0,1},{1,0},{2,3},{3,2},{4,5},{5,4},{6,7},{7,6},{8,9},{9,8},{10,11... | collective-permute-start | bytes 393224 | tf_op jit(solution)/shard_map/ppermute | solution.py:290
  107.0 9.3 %collective-permute-start.16 = (bf16[64,2048]{1,0:T(8,128)(2,1)S(1)}, bf16[64,2048]{1,0:T(8,128)(2,1)S(1)}, u32[]{:S(2)}, u32[]{:S(2)}) collective-permute-start(bf16[64,2048]{1,0:T(8,128)(2,1)S(1)} %get-tuple-element.37), channel_id=1, source_target_pairs={{0,1},{1,0},{2,3},{3,2},{4,5},{5,4},{6,7},{7,6},{8,9},{9,8},{10,11... | collective-permute-start | bytes 786440 | tf_op jit(solution)/shard_map/ppermute | solution.py:290
  107.7 11.4 %collective-permute-start.18 = (bf16[32,2048]{1,0:T(8,128)(2,1)S(1)}, bf16[32,2048]{1,0:T(8,128)(2,1)S(1)}, u32[]{:S(2)}, u32[]{:S(2)}) collective-permute-start(bf16[32,2048]{1,0:T(8,128)(2,1)S(1)} %get-tuple-element.39), channel_id=1, source_target_pairs={{0,1},{1,0},{2,3},{3,2},{4,5},{5,4},{6,7},{7,6},{8,9},{9,8},{10,11... | collective-permute-start | bytes 393224 | tf_op jit(solution)/shard_map/ppermute | solution.py:290
  116.3 7.7 %collective-permute-start.17 = (bf16[32,2048]{1,0:T(8,128)(2,1)S(1)}, bf16[32,2048]{1,0:T(8,128)(2,1)S(1)}, u32[]{:S(2)}, u32[]{:S(2)}) collective-permute-start(bf16[32,2048]{1,0:T(8,128)(2,1)S(1)} %get-tuple-element.38), channel_id=1, source_target_pairs={{0,1},{1,0},{2,3},{3,2},{4,5},{5,4},{6,7},{7,6},{8,9},{9,8},{10,11... | collective-permute-start | bytes 393224 | tf_op jit(solution)/shard_map/ppermute | solution.py:290
  119.2 7.5 %collective-permute-start.20 = (bf16[32,2048]{1,0:T(8,128)(2,1)S(1)}, bf16[32,2048]{1,0:T(8,128)(2,1)S(1)}, u32[]{:S(2)}, u32[]{:S(2)}) collective-permute-start(bf16[32,2048]{1,0:T(8,128)(2,1)S(1)} %get-tuple-element.44), channel_id=1, source_target_pairs={{0,4},{1,5},{2,6},{3,7},{4,0},{5,1},{6,2},{7,3},{8,12},{9,13},{10,... | collective-permute-start | bytes 393224 | tf_op jit(solution)/shard_map/ppermute | solution.py:290
  119.3 8.9 %collective-permute-start.21 = (bf16[32,2048]{1,0:T(8,128)(2,1)S(1)}, bf16[32,2048]{1,0:T(8,128)(2,1)S(1)}, u32[]{:S(2)}, u32[]{:S(2)}) collective-permute-start(bf16[32,2048]{1,0:T(8,128)(2,1)S(1)} %get-tuple-element.45), channel_id=1, source_target_pairs={{0,2},{1,3},{2,0},{3,1},{4,6},{5,7},{6,4},{7,5},{8,10},{9,11},{10,... | collective-permute-start | bytes 393224 | tf_op jit(solution)/shard_map/ppermute | solution.py:290
  122.6 9.2 %collective-permute-start.19 = (bf16[32,2048]{1,0:T(8,128)(2,1)S(1)}, bf16[32,2048]{1,0:T(8,128)(2,1)S(1)}, u32[]{:S(2)}, u32[]{:S(2)}) collective-permute-start(bf16[32,2048]{1,0:T(8,128)(2,1)S(1)} %get-tuple-element.48), channel_id=1, source_target_pairs={{0,6},{1,7},{2,4},{3,5},{4,2},{5,3},{6,0},{7,1},{8,14},{9,15},{10,... | collective-permute-start | bytes 393224 | tf_op jit(solution)/shard_map/ppermute | solution.py:290
  131.9 8.4 %collective-permute-start.22 = (bf16[32,2048]{1,0:T(8,128)(2,1)S(1)}, bf16[32,2048]{1,0:T(8,128)(2,1)S(1)}, u32[]{:S(2)}, u32[]{:S(2)}) collective-permute-start(bf16[32,2048]{1,0:T(8,128)(2,1)S(1)} %add_convert_fusion.near), channel_id=1, source_target_pairs={{0,14},{1,15},{2,12},{3,13},{4,10},{5,11},{6,8},{7,9},{8,6},{9,7},... | collective-permute-start | bytes 393224 | tf_op jit(solution)/shard_map/ppermute | solution.py:290
  140.6 5.1 %collective-permute-start.25 = (bf16[32,2176]{1,0:T(8,128)(2,1)S(1)}, bf16[32,2176]{1,0:T(8,128)(2,1)S(1)}, u32[]{:S(2)}, u32[]{:S(2)}) collective-permute-start(bf16[32,2176]{1,0:T(8,128)(2,1)S(1)} %shard_map.102.refs_0_), channel_id=1, source_target_pairs={{0,1},{1,0},{2,3},{3,2},{4,5},{5,4},{6,7},{7,6},{8,9},{9,8},{10,11... | collective-permute-start | bytes 417800 | tf_op jit(solution)/shard_map/ppermute | solution.py:290
  141.3 9.3 %collective-permute-start.24 = (bf16[32,2176]{1,0:T(8,128)(2,1)S(1)}, bf16[32,2176]{1,0:T(8,128)(2,1)S(1)}, u32[]{:S(2)}, u32[]{:S(2)}) collective-permute-start(bf16[32,2176]{1,0:T(8,128)(2,1)S(1)} %shard_map.102.refs_0_), channel_id=1, source_target_pairs={{0,6},{1,7},{2,4},{3,5},{4,2},{5,3},{6,0},{7,1},{8,14},{9,15},{10,... | collective-permute-start | bytes 417800 | tf_op jit(solution)/shard_map/ppermute | solution.py:290
  142.3 9.3 %collective-permute-start.23 = (bf16[32,2176]{1,0:T(8,128)(2,1)S(1)}, bf16[32,2176]{1,0:T(8,128)(2,1)S(1)}, u32[]{:S(2)}, u32[]{:S(2)}) collective-permute-start(bf16[32,2176]{1,0:T(8,128)(2,1)S(1)} %shard_map.102.refs_0_), channel_id=1, source_target_pairs={{0,2},{1,3},{2,0},{3,1},{4,6},{5,7},{6,4},{7,5},{8,10},{9,11},{10,... | collective-permute-start | bytes 417800 | tf_op jit(solution)/shard_map/ppermute | solution.py:290
  150.6 6.0 %collective-permute-start.26 = (bf16[32,2176]{1,0:T(8,128)(2,1)S(1)}, bf16[32,2176]{1,0:T(8,128)(2,1)S(1)}, u32[]{:S(2)}, u32[]{:S(2)}) collective-permute-start(bf16[32,2176]{1,0:T(8,128)(2,1)S(1)} %shard_map.102.refs_0_), channel_id=1, source_target_pairs={{0,4},{1,5},{2,6},{3,7},{4,0},{5,1},{6,2},{7,3},{8,12},{9,13},{10,... | collective-permute-start | bytes 417800 | tf_op jit(solution)/shard_map/ppermute | solution.py:290
  151.3 6.2 %collective-permute-start.29 = (bf16[32,2176]{1,0:T(8,128)(2,1)S(1)}, bf16[32,2176]{1,0:T(8,128)(2,1)S(1)}, u32[]{:S(2)}, u32[]{:S(2)}) collective-permute-start(bf16[32,2176]{1,0:T(8,128)(2,1)S(1)} %collective-permute-done.24.refs_3_), channel_id=1, source_target_pairs={{0,1},{1,0},{2,3},{3,2},{4,5},{5,4},{6,7},{7,6},{8,9},{9,8},{10,11... | collective-permute-start | bytes 417800 | tf_op jit(solution)/shard_map/ppermute | solution.py:290
  151.6 6.3 %collective-permute-start.27 = (bf16[32,2176]{1,0:T(8,128)(2,1)S(1)}, bf16[32,2176]{1,0:T(8,128)(2,1)S(1)}, u32[]{:S(2)}, u32[]{:S(2)}) collective-permute-start(bf16[32,2176]{1,0:T(8,128)(2,1)S(1)} %collective-permute-done.23.refs_1_), channel_id=1, source_target_pairs={{0,1},{1,0},{2,3},{3,2},{4,5},{5,4},{6,7},{7,6},{8,9},{9,8},{10,11... | collective-permute-start | bytes 417800 | tf_op jit(solution)/shard_map/ppermute | solution.py:290
  156.6 5.1 %collective-permute-start.28 = (bf16[32,2176]{1,0:T(8,128)(2,1)S(1)}, bf16[32,2176]{1,0:T(8,128)(2,1)S(1)}, u32[]{:S(2)}, u32[]{:S(2)}) collective-permute-start(bf16[32,2176]{1,0:T(8,128)(2,1)S(1)} %collective-permute-done.26.refs_2_), channel_id=1, source_target_pairs={{0,1},{1,0},{2,3},{3,2},{4,5},{5,4},{6,7},{7,6},{8,9},{9,8},{10,11... | collective-permute-start | bytes 417800 | tf_op jit(solution)/shard_map/ppermute | solution.py:290
